TPU v7x, 512 devices: a whole 4x8x8 slice. The times are simulated.
512 devices in a mesh: outer: 32 (over z_lo, y, core), inner: 16 (over x, z_hi).
Axes of the slice: x: 4, y: 8, z: 8 (z_hi: 4, z_lo: 2; z = z_hi * 2 + z_lo), core: 2. Of those that a mesh axis runs over, the one named last changes fastest.
Arguments:
- inputs: bfloat16 [65536, 8192], P(('outer', 'inner')), may hold values from -6 to 6
- segment_ids: int32 [512, 128], P(('outer', 'inner')), may hold values from 0 to 7, never falling along the last dimension, each value on 1 to 32 neighbouring positions
- qkv_weight: bfloat16 [8192, 768], P('inner'), may hold values from -0.0625 to 0.0625
- attn_cotangent: bfloat16 [65536, 512], P(('outer', 'inner')), may hold values from -6 to 6
Outputs:
- input_grad: bfloat16 [65536, 8192], P(('outer', 'inner'))
- weight_grad: float32 [8192, 768], P('inner', 'outer')
Inputs may be any that keep to these rules, and one draw needn't show every extreme that they name: `segment_ids`: within each sequence the ids never fall, and each id covers one run of 1 to 32 tokens.
All inputs are finite; a program needn't handle non-finite values.
Results may differ from a plain program's by a relative error of at most 0.033.
Values may be sent and summed in bfloat16 or wider, within the bound.
No kernel may reach another device: no remote copies, remote signals or barrier semaphores. Data moves between devices by JAX's collectives and lax.ppermute only.
A program may use at most 64 MiB of HBM per device.

v0:
```python
import math

import jax
import jax.numpy as jnp
from jax import lax
from jax.sharding import PartitionSpec as P

HD = 128


def attention_grad(projected, cotangent, segments):
    count = projected.shape[0]
    heads = cotangent.shape[1] // HD
    values = projected.astype(jnp.float32)
    query = values[:, : heads * HD].reshape(count, heads, HD)
    keys = values[:, heads * HD : (heads + 1) * HD]
    vals = values[:, (heads + 1) * HD :]
    positions = jnp.arange(count)
    allowed = (positions[:, None] >= positions[None, :]) & (segments[:, None] == segments[None, :])

    def forward(query, keys, vals):
        scores = jnp.einsum("shd,td->hst", query, keys) / math.sqrt(HD)
        scores = jnp.where(allowed[None], scores, 0.0)
        weights = jnp.where(allowed[None], jnp.exp(scores), 0.0)
        weights = weights / jnp.sum(weights, axis=2, keepdims=True)
        return jnp.einsum("hst,td->shd", weights, vals).reshape(count, heads * HD)

    unused, pullback = jax.vjp(forward, query, keys, vals)
    grad_q, grad_k, grad_v = pullback(cotangent.astype(jnp.float32))
    return jnp.concatenate([grad_q.reshape(count, heads * HD), grad_k, grad_v], axis=1).astype(
        jnp.bfloat16
    )


def on_device(inputs, segment_ids, qkv_weight, attn_cotangent):
    tok_rows = inputs.shape[0]
    segments = segment_ids.reshape(tok_rows)
    width = qkv_weight.shape[1]
    block_width = qkv_weight.shape[0]
    groups = lax.axis_size("inner")
    columns = lax.all_to_all(inputs, "inner", split_axis=1, concat_axis=0, tiled=True)
    whole = lax.all_gather(qkv_weight, "inner", axis=0, tiled=True)
    x_blocks = inputs.reshape(tok_rows, groups, block_width)
    w_blocks = whole.reshape(groups, block_width, width)
    parts = jnp.einsum(
        "snd,ndc->nsc", x_blocks, w_blocks, preferred_element_type=jnp.float32
    ).astype(jnp.bfloat16)
    parts = lax.optimization_barrier(parts)
    projected = jnp.sum(parts.astype(jnp.float32), axis=0).astype(jnp.bfloat16)
    grads = attention_grad(projected, attn_cotangent, segments)
    input_grad = lax.dot_general(
        grads, whole, (((1,), (1,)), ((), ())), preferred_element_type=jnp.float32
    ).astype(jnp.bfloat16)
    weight_part = lax.dot_general(
        columns,
        lax.all_gather(grads, "inner", axis=0, tiled=True),
        (((0,), (0,)), ((), ())),
        preferred_element_type=jnp.float32,
    )
    weight_grad = lax.psum_scatter(
        weight_part.astype(jnp.bfloat16).astype(jnp.float32).astype(jnp.bfloat16),
        "outer",
        scatter_dimension=1,
        tiled=True,
    ).astype(jnp.float32)
    return (input_grad, weight_grad)


def solution(mesh):
    return jax.shard_map(
        on_device,
        mesh=mesh,
        in_specs=(
            P(("outer", "inner"), None),
            P(("outer", "inner"), None),
            P("inner", None),
            P(("outer", "inner"), None),
        ),
        out_specs=(P(("outer", "inner"), None), P("inner", "outer")),
        check_vma=False,
    )
```

profile of v0, /device:TPU:6, one launch (start us, length us, event | category | flops | bytes accessed | tf_op | source)
XLA Modules:
  0.0 428.8 jit_solution(1653126295104554458)
XLA Ops:
  7.2 0.0 all-gather.3.cloned.1.call-start
  7.2 0.7 all-gather.3.cloned.1.call-update
  7.9 0.0 all-gather.5.cloned.1.call-start
  7.9 1.0 copy.31
  9.0 0.8 fusion.17
  9.8 0.1 copy.22
  9.9 3.2 copy.19
  13.2 147.2 %all-gather.3.cloned.1.call-done = bf16[8192,768]{1,0:T(8,128)(2,1)} async-done(((bf16[512,768]{1,0:T(8,128)(2,1)}), bf16[8192,768]{1,0:T(8,128)(2,1)}) %all-gather.3.cloned.1.call-update) | async-done | bytes 12582928 | tf_op jit(solution)/shard_map/all_gather | solution.py:42
  160.4 8.2 %convolution_convert_fusion.1 = bf16[16,128,768]{2,1,0:T(8,128)(2,1)} fusion(bf16[128,16,512]{0,2,1:T(8,128)(2,1)S(1)} %bitcast.76, bf16[16,512,768]{2,1,0:T(8,128)(2,1)} %bitcast.75), kind=kOutput, calls=%fused_computation.1 | convolution fusion | flops 1612185600 | bytes 17825792 | tf_op jit(solution)/shard_map/snd,ndc->nsc/dot_general | solution.py:45
  168.6 2.3 reduce_sum.34
  171.0 0.1 copy.33
  171.1 0.2 fusion.13
  171.3 0.2 fusion.2
  171.6 0.2 fusion.3
  171.8 0.3 fusion.1
  172.0 0.3 convolution_convert_fusion.3
  172.3 0.7 pad_maximum_fusion
  173.0 0.0 all-gather.5.cloned.1.call-update
  173.0 0.0 reduce-scatter.2.cloned.1.call-start
  173.1 84.2 %all_to_all.16 = bf16[128,16,512]{0,2,1:T(8,128)(2,1)} all-to-all(bf16[128,16,512]{0,2,1:T(8,128)(2,1)S(1)} %bitcast.77), channel_id=1, replica_groups=mesh['outer'=32,'inner'=16] {'inner'}, dimensions={1} | all-to-all | bytes 4194304 | tf_op jit(solution)/shard_map/all_to_all | solution.py:41
  257.2 2.9 copy.27
  260.1 39.7 %all-gather.5.cloned.1.call-done = bf16[2048,768]{0,1:T(8,128)(2,1)} async-done(((bf16[128,768]{0,1:T(8,128)(2,1)}), bf16[2048,768]{0,1:T(8,128)(2,1)}) %all-gather.5.cloned.1.call-update) | async-done | bytes 3145744 | tf_op jit(solution)/shard_map/all_gather | solution.py:56
  299.8 4.6 %fusion = bf16[512,768]{0,1:T(8,128)(2,1)} fusion(bf16[2048,768]{0,1:T(8,128)(2,1)} %all-gather.5.cloned.1.call-done, bf16[2048,512]{1,0:T(8,128)(2,1)S(1)} %bitcast.79), kind=kOutput, calls=%fused_computation.3 | convolution fusion | flops 1611005952 | bytes 6029312 | tf_op jit(solution)/shard_map/dot_general | solution.py:54
  304.4 0.0 reduce-scatter.2.cloned.1.call-update
  304.4 10.1 %convolution_convert_fusion = bf16[128,8192]{1,0:T(8,128)(2,1)} fusion(bf16[8192,768]{1,0:T(8,128)(2,1)} %all-gather.3.cloned.1.call-done, bf16[128,128]{0,1:T(8,128)(2,1)S(1)} %fusion.2, bf16[128,128]{0,1:T(8,128)(2,1)S(1)} %fusion.1, bf16[128,512]{0,1:T(8,128)(2,1)S(1)} %bitcast.81), kind=kOutput, calls=%fused_computation | convolution fusion | flops 1612251136 | bytes 14876672 | tf_op jit(solution)/shard_map/dot_general | solution.py:51
  314.6 106.4 %reduce-scatter.2.cloned.1.call-done = bf16[512,24]{0,1:T(8,128)(2,1)} async-done(((bf16[512,768]{0,1:T(8,128)(2,1)}), bf16[512,24]{0,1:T(8,128)(2,1)}) %reduce-scatter.2.cloned.1.call-update) | async-done | bytes 24592 | tf_op jit(solution)/shard_map/reduce_scatter | solution.py:60
  420.9 1.4 convert_element_type.26
  (3 shorter events, 0.0 us)
Async XLA Ops:
  7.2 153.2 %all-gather.3.cloned.1.call-start = ((), (), s32[]{:S(2)}) async-start(), calls=%async_computation.2 | async-start | bytes 13369344 | tf_op jit(solution)/shard_map/all_gather | solution.py:42
  7.9 291.9 %all-gather.5.cloned.1.call-start = ((), (), s32[]{:S(2)}) async-start(), calls=%async_computation.3 | async-start | bytes 3342336 | tf_op jit(solution)/shard_map/all_gather | solution.py:56
  173.0 247.9 %reduce-scatter.2.cloned.1.call-start = ((), (), s32[]{:S(2)}) async-start(), calls=%async_computation.4 | async-start | bytes 811008 | tf_op jit(solution)/shard_map/reduce_scatter | solution.py:60
Sparse Core Ops, SparseCore 0:
  11.1 149.3 all-gather.2
  173.1 126.6 all-gather.4
  304.6 116.3 reduce-scatter.1
where the time goes:
time: 429 us
  waiting for transfers between devices  294 us (69%)
  blocking collectives  84.2 us (20%)
  matrix products  24.1 us (6%)
  between operations  13.8 us (3%)
  local copies, waits for them, and re-layouts  7.34 us (2%)
  other arithmetic  5.22 us (1%)
    all_gather x1, waiting for transfers between devices, on_device(): whole = lax.all_gather(qkv_weight, 'inner', axis=0, tiled=True)  147 us
    reduce_scatter x1, waiting for transfers between devices, on_device(): lax.psum_scatter(weight_part.astype(jnp.bfloat16).astype(jnp.float32).ast...  106 us
    all_to_all x1, blocking collectives, on_device(): lax.all_to_all(inputs, 'inner', split_axis=1, concat_axis=0, tiled=True)  84.2 us
    all_gather x1, waiting for transfers between devices, on_device(): lax.all_gather(grads, 'inner', axis=0, tiled=True)  39.7 us
    dot_general x1, matrix products, on_device(): lax.dot_general(grads, whole, (((1,), (1,)), ((), ())), preferred_element...  10.1 us
  transfers between devices with their start and end apart: 3, of which 3 were waited for; matrix products, arithmetic and copies ran while one was open for 4% of the time, Pallas kernels for 0%

commit v1 on v0

v1 whole, which is shorter than its diff:
```python
import math

import jax
import jax.numpy as jnp
from jax import lax
from jax.experimental import pallas as pl
from jax.experimental.pallas import tpu as pltpu
from jax.sharding import Mesh
from jax.sharding import PartitionSpec as P

HD = 128
BF16 = jnp.bfloat16
F32 = jnp.float32
ANY = pl.BlockSpec(memory_space=pl.ANY)
PARAMS = pltpu.CompilerParams(vmem_limit_bytes=40 * 1024 * 1024)

NT = (((1,), (1,)), ((), ()))
TN = (((0,), (0,)), ((), ()))


def arr(shape, dtype=BF16):
    return jax.ShapeDtypeStruct(shape, dtype)


def cost(flops, nbytes):
    return pl.CostEstimate(flops=flops, bytes_accessed=nbytes, transcendentals=0)


def dot(a, b, dims=(((1,), (0,)), ((), ()))):
    return lax.dot_general(a, b, dims, preferred_element_type=F32)


def split_kernel(x_ref, *rest):
    outs, sems = rest[:-1], rest[-1]
    n = len(outs)
    width = outs[0].shape[1]
    me = lax.axis_index("x")
    copies = []
    for k in range(n):
        start = pl.multiple_of(lax.rem(me + k, n) * width, width)
        copies.append(pltpu.make_async_copy(x_ref.at[:, pl.ds(start, width)], outs[k], sems.at[k]))
    for copy in copies:
        copy.start()
    for copy in copies:
        copy.wait()


def join_kernel(*refs):
    ins, out, sems = refs[:-2], refs[-2], refs[-1]
    n = len(ins)
    width = ins[0].shape[1]
    me = lax.axis_index("x")
    copies = []
    for k in range(n):
        start = pl.multiple_of(lax.rem(me + k, n) * width, width)
        copies.append(pltpu.make_async_copy(ins[k], out.at[:, pl.ds(start, width)], sems.at[k]))
    for copy in copies:
        copy.start()
    for copy in copies:
        copy.wait()


def piece_places(rows):
    zl, zh, c = lax.axis_index("zl"), lax.axis_index("zh"), lax.axis_index("c")
    near = lax.rem(zh + 3 + 2 * zl, 4)
    far = lax.rem(zh + 5 - 2 * zl, 4)
    opposite = lax.rem(zh + 2, 4)
    places = [zh * (2 * rows)]
    for block in (near, far, opposite):
        places.append(block * (2 * rows) + c * rows)
        places.append(block * (2 * rows) + (1 - c) * rows)
    return [pl.multiple_of(p, rows) for p in places]


def forward_kernel(x0, x1, x2, x3, w0, a, a2, b, b2, d, d2, p0, p1, p2, p3, acc):
    rows = a.shape[0]
    places = piece_places(rows)
    xs = (x0, x1, x2, x3)
    tokens = x0.shape[0]
    for i, (place, w) in enumerate(zip(places, (w0, a, a2, b, b2, d, d2))):
        depth = w.shape[0]
        x = jnp.concatenate([r[:, pl.ds(place, depth)] for r in xs], axis=0)
        term = dot(x, w[...])
        if i == 0:
            acc[...] = term
        else:
            acc[...] += term
    for k, p in enumerate((p0, p1, p2, p3)):
        p[...] = acc[k * tokens : (k + 1) * tokens, :].astype(BF16)


def attention_kernel(p0, p1, p2, p3, seg_ref, cot_ref, out):
    total = p0[...].astype(F32) + p1[...].astype(F32) + p2[...].astype(F32) + p3[...].astype(F32)
    projected = total.astype(BF16)
    count = projected.shape[0]
    heads = cot_ref.shape[1] // HD
    row = jnp.broadcast_to(seg_ref[...], (count, count))
    col = row.T
    here = lax.broadcasted_iota(jnp.int32, (count, count), 0)
    there = lax.broadcasted_iota(jnp.int32, (count, count), 1)
    allowed = (here >= there) & (row == col)
    keys = projected[:, heads * HD : (heads + 1) * HD]
    vals = projected[:, (heads + 1) * HD :]
    scale = 1.0 / math.sqrt(HD)
    grad_k = jnp.zeros((count, HD), F32)
    grad_v = jnp.zeros((count, HD), F32)
    for h in range(heads):
        query = projected[:, h * HD : (h + 1) * HD]
        cot = cot_ref[:, h * HD : (h + 1) * HD]
        scores = dot(query, keys, NT) * scale
        scores = jnp.where(allowed, scores, 0.0)
        weights = jnp.where(allowed, jnp.exp(scores), 0.0)
        weights = weights / jnp.sum(weights, axis=1, keepdims=True)
        grad_w = dot(cot, vals, NT)
        lean = jnp.sum(weights * grad_w, axis=1, keepdims=True)
        grad_s = (weights * (grad_w - lean) * scale).astype(BF16)
        out[:, h * HD : (h + 1) * HD] = dot(grad_s, keys).astype(BF16)
        grad_k += dot(grad_s, query, TN)
        grad_v += dot(weights.astype(BF16), cot, TN)
    out[:, heads * HD : (heads + 1) * HD] = grad_k.astype(BF16)
    out[:, (heads + 1) * HD :] = grad_v.astype(BF16)


def weight_kernel(g0, g1, g2, g3, x0, x1, x2, x3, mine, other):
    groups, span, wide = mine.shape
    zl, y, c = lax.axis_index("zl"), lax.axis_index("y"), lax.axis_index("c")
    zh = lax.axis_index("zh")
    grads = jnp.concatenate([g0[...], g1[...], g2[...], g3[...]], axis=0)
    cols = grads.shape[1]
    n_y = groups // 2
    shape = (groups * span, cols)
    place = lax.broadcasted_iota(jnp.int32, shape, 0)
    source = lax.broadcasted_iota(jnp.int32, shape, 1)
    group, within = place // span, place % span
    at_z = lax.rem(zl + group // n_y, 2)
    at_y = lax.rem(y + group % n_y, n_y)
    left = []
    for core in (c, 1 - c):
        wanted = ((at_z * n_y + at_y) * 2 + core) * span + within
        pick = jnp.where(source == wanted, 1.0, 0.0).astype(BF16)
        left.append(dot(pick, grads, NT).astype(BF16))
    tile = 256
    block = wide // 4
    for kz in range(4):
        for t in range(block // tile):
            start = pl.multiple_of(lax.rem(zh + kz, 4) * block + t * tile, tile)
            x = jnp.concatenate([r[:, pl.ds(start, tile)] for r in (x0, x1, x2, x3)], axis=0)
            at = kz * block + t * tile
            other[:, :, at : at + tile] = dot(left[1], x).astype(BF16).reshape(groups, span, tile)
            mine[:, :, at : at + tile] = dot(left[0], x).reshape(groups, span, tile)


def input_kernel(g0, g1, g2, g3, w0, a, a2, b, b2, d, d2, o0, o1, o2, o3):
    rows = a.shape[0]
    tokens = g0.shape[0]
    places = piece_places(rows)
    grads = jnp.concatenate([g0[...], g1[...], g2[...], g3[...]], axis=0)
    for place, w in zip(places, (w0, a, a2, b, b2, d, d2)):
        depth = w.shape[0]
        term = dot(grads, w[...], NT).astype(BF16)
        for k, o in enumerate((o0, o1, o2, o3)):
            o[:, pl.ds(place, depth)] = term[k * tokens : (k + 1) * tokens]


def first_kernel(mine, got, *outs):
    groups, span, wide = mine.shape
    n_y = groups // 2
    block = wide // 4
    half = block // 2
    for lz in range(2):
        for ky in range(n_y):
            g = lz * n_y + ky
            total = mine[g] + got[g].astype(F32)
            for kz in range(4):
                at = kz * block
                outs[ky][lz, :, kz * half : (kz + 1) * half] = total[:, at : at + half].astype(BF16)
                outs[n_y + lz * 4 + kz][ky] = total[:, at + half : at + block].astype(BF16)


def second_kernel(*refs):
    ins, outs = refs[:16], refs[16:]
    half = ins[8].shape[2]
    first = sum(r[...].astype(F32) for r in ins[:8])
    second = sum(r[...].astype(F32) for r in ins[8:])
    for lz in range(2):
        for kz in range(4):
            outs[lz * 4 + kz][...] = first[lz, :, kz * half : (kz + 1) * half].astype(BF16)
    for ky in range(8):
        outs[8 + ky][...] = second[ky].astype(BF16)


def third_kernel(*refs):
    ins, out = refs[:16], refs[16]
    half = ins[0].shape[1]
    out[:, :half] = sum(r[...].astype(F32) for r in ins[:8])
    out[:, half:] = sum(r[...].astype(F32) for r in ins[8:])


def shift(value, axis, k):
    n = lax.axis_size(axis)
    return lax.ppermute(value, axis, [(i, (i + k) % n) for i in range(n)])


def z_move(value, target):
    pairs = []
    for zl in range(2):
        for zh in range(4):
            to_l, to_h = target(zl, zh)
            pairs.append((zl * 4 + zh, to_l * 4 + to_h % 4))
    return lax.ppermute(value, ("zl", "zh"), pairs)


def across(value):
    return z_move(value, lambda zl, zh: (0, zh + 1) if zl else (1, zh - 1))


def beside(value):
    return z_move(value, lambda zl, zh: (1 - zl, zh))


def on_device(inputs, segment_ids, qkv_weight, attn_cotangent):
    tokens, features = inputs.shape
    block, cols = qkv_weight.shape
    n = 4
    width = features // n
    half = block // 2
    n_y = 8
    span = cols // 32
    c = lax.axis_index("c")

    sent = pl.pallas_call(
        split_kernel,
        out_shape=[arr((tokens, width))] * n,
        in_specs=[ANY],
        out_specs=[ANY] * n,
        scratch_shapes=[pltpu.SemaphoreType.DMA((n,))],
        name="split_features",
    )(inputs)
    own = lax.dynamic_slice_in_dim(qkv_weight, c * half, half, 0)
    a = across(own)
    x2 = shift(sent[2], "x", 2)
    x1 = shift(sent[1], "x", 1)
    x3 = shift(sent[3], "x", 3)
    a2 = shift(a, "c", 1)
    b = beside(a)
    b2 = shift(b, "c", 1)
    d = across(b)
    d2 = shift(d, "c", 1)
    xs = (sent[0], x1, x2, x3)
    weights = (qkv_weight, a, a2, b, b2, d, d2)

    flops = 2 * n * tokens * width * cols
    parts = pl.pallas_call(
        forward_kernel,
        out_shape=[arr((tokens, cols))] * n,
        scratch_shapes=[pltpu.VMEM((n * tokens, cols), F32)],
        compiler_params=PARAMS,
        cost_estimate=cost(flops, 6 << 20),
        name="forward",
    )(*xs, *weights)
    back = [parts[0]] + [shift(parts[k], "x", n - k) for k in range(1, n)]

    grads = pl.pallas_call(
        attention_kernel,
        out_shape=arr((tokens, cols)),
        compiler_params=PARAMS,
        cost_estimate=cost(1 << 28, 1 << 20),
        name="attention",
    )(*back, segment_ids, attn_cotangent)
    gs = [grads] + [shift(grads, "x", k) for k in range(1, n)]

    mine, other = pl.pallas_call(
        weight_kernel,
        out_shape=[arr((2 * n_y, span, width), F32), arr((2 * n_y, span, width))],
        compiler_params=PARAMS,
        cost_estimate=cost(flops, 8 << 20),
        name="weight_grad",
    )(*gs, *xs)
    got = shift(other, "c", 1)

    back = pl.pallas_call(
        input_kernel,
        out_shape=[arr((tokens, width))] * n,
        compiler_params=PARAMS,
        cost_estimate=cost(flops, 6 << 20),
        name="input_grad",
    )(*gs, *weights)
    home = [back[0]] + [shift(back[k], "x", n - k) for k in range(1, n)]

    pieces = pl.pallas_call(
        first_kernel,
        out_shape=[arr((2, span, n * half))] * n_y + [arr((n_y, span, half))] * 8,
        compiler_params=PARAMS,
        cost_estimate=cost(1 << 20, 8 << 20),
        name="add_cores",
    )(mine, got)

    def spread_y(values):
        return [values[0]] + [shift(values[k], "y", k) for k in range(1, n_y)]

    def spread_z(values):
        out = [values[0]]
        for i in range(1, 8):
            lz, kz = divmod(i, 4)
            out.append(z_move(values[i], lambda zl, zh: ((zl + lz) % 2, zh + kz)))
        return out

    pieces = spread_y(pieces[:8]) + spread_z(pieces[8:])
    pieces = pl.pallas_call(
        second_kernel,
        out_shape=[arr((span, half))] * 16,
        compiler_params=PARAMS,
        cost_estimate=cost(1 << 20, 2 << 20),
        name="add_first",
    )(*pieces)
    pieces = spread_z(pieces[:8]) + spread_y(pieces[8:])
    weight_grad = pl.pallas_call(
        third_kernel,
        out_shape=arr((span, block), F32),
        compiler_params=PARAMS,
        cost_estimate=cost(1 << 18, 1 << 18),
        name="add_second",
    )(*pieces).T

    input_grad = pl.pallas_call(
        join_kernel,
        out_shape=arr((tokens, features)),
        in_specs=[ANY] * n,
        out_specs=ANY,
        scratch_shapes=[pltpu.SemaphoreType.DMA((n,))],
        name="join_features",
    )(*home)
    return (input_grad, weight_grad)


def solution(mesh):
    outer, inner = ("zl", "y", "c"), ("x", "zh")
    fine = Mesh(mesh.devices.reshape(2, 8, 2, 4, 4), outer + inner)
    return jax.shard_map(
        on_device,
        mesh=fine,
        in_specs=(
            P(outer + inner, None),
            P(outer + inner, None),
            P(inner, None),
            P(outer + inner, None),
        ),
        out_specs=(P(outer + inner, None), P(inner, outer)),
        check_vma=False,
    )
```

time: 429 us -> 377 us (0.88)
  waiting for transfers between devices: 294 us -> 50.1 us
  starting transfers between devices: 0.12 us -> 183 us
  Pallas kernels: 0 us -> 138 us
  blocking collectives: 84.2 us -> 0 us
  matrix products: 24.1 us -> 0 us
  between operations: 13.8 us -> 1.37 us
  other arithmetic: 5.22 us -> 0 us
  local copies, waits for them, and re-layouts: 7.34 us -> 2.97 us
    all_gather x2 -> x0, waiting for transfers between devices: 187 us -> none  [the longest x1 147 us: on_device(): whole = lax.all_gather(qkv_weight, 'inner', axis=0, tiled=True)]
    ppermute x0 -> x47, starting transfers between devices: none -> 183 us  [the longest x30 113 us: shift(): return lax.ppermute(value, axis, [(i, (i + k) % n) for i in range(n)])]
    pallas_call x0 -> x9, Pallas kernels: none -> 138 us  [the longest x1 64.7 us: on_device(): pl.pallas_call(split_kernel, out_shape=[arr((tokens, width))] * n, in_spe...]
    reduce_scatter x1 -> x0, waiting for transfers between devices: 106 us -> none  [on_device(): lax.psum_scatter(weight_part.astype(jnp.bfloat16).astype(jnp.float32).ast...]
    all_to_all x1 -> x0, blocking collectives: 84.2 us -> none  [on_device(): lax.all_to_all(inputs, 'inner', split_axis=1, concat_axis=0, tiled=True)]
    ppermute x0 -> x47, waiting for transfers between devices: none -> 50.1 us  [the longest x30 29 us: shift(): return lax.ppermute(value, axis, [(i, (i + k) % n) for i in range(n)])]
    dot_general x8 -> x0, matrix products: 24.1 us -> none  [the longest x1 10.1 us: on_device(): lax.dot_general(grads, whole, (((1,), (1,)), ((), ())), preferred_element...]
  transfers between devices with their start and end apart: 3 -> 47, of which waited for: 3 -> 16; matrix products, arithmetic and copies ran while one was open for 4% -> 0% of each run, Pallas kernels for 0% -> 35%
where the time goes in v1:
time: 377 us; the launch traced here: 376 us
  starting transfers between devices  183 us (49%)
  Pallas kernels  138 us (37%)
  waiting for transfers between devices  50.1 us (13%)
    ppermute x30, starting transfers between devices, shift(): return lax.ppermute(value, axis, [(i, (i + k) % n) for i in range(n)])  113 us
    ppermute x17, starting transfers between devices, z_move(): return lax.ppermute(value, ('zl', 'zh'), pairs)  70.4 us
    pallas_call x1, Pallas kernels, on_device(): pl.pallas_call(split_kernel, out_shape=[arr((tokens, width))] * n, in_spe...  64.7 us
    pallas_call x1, Pallas kernels, on_device(): pl.pallas_call(join_kernel, out_shape=arr((tokens, features)), in_specs=[...  64.7 us
    ppermute x30, waiting for transfers between devices, shift(): return lax.ppermute(value, axis, [(i, (i + k) % n) for i in range(n)])  29 us
    ppermute x17, waiting for transfers between devices, z_move(): return lax.ppermute(value, ('zl', 'zh'), pairs)  21.1 us
  transfers between devices with their start and end apart: 47, of which 16 were waited for; matrix products, arithmetic and copies ran while one was open for 0% of the time, Pallas kernels for 35%

profile of v1, /device:TPU:6, one launch (start us, length us, event | category | flops | bytes accessed | tf_op | source)
XLA Modules:
  0.0 375.8 jit_solution(18135078229127860396)
XLA Ops:
  1.7 10.9 %collective-permute-start.3 = (bf16[256,768]{1,0:T(8,128)(2,1)S(1)}, bf16[256,768]{1,0:T(8,128)(2,1)S(1)}, u32[]{:S(2)}, u32[]{:S(2)}) collective-permute-start(bf16[256,768]{1,0:T(8,128)(2,1)S(1)} %constant_dynamic-slice_fusion), channel_id=1, source_target_pairs={{0,259},{1,256},{2,257},{3,258},{256,1},{257,2},{258,3},{259,0},{4... | collective-permute-start | bytes 1179656 | tf_op jit(solution)/shard_map/ppermute | solution.py:210
  12.7 9.1 %collective-permute-done.3.a = bf16[256,768]{1,0:T(8,128)(2,1)S(1)} collective-permute-done((bf16[256,768]{1,0:T(8,128)(2,1)S(1)}, bf16[256,768]{1,0:T(8,128)(2,1)S(1)}, u32[]{:S(2)}, u32[]{:S(2)}) %collective-permute-start.3) | collective-permute-done | bytes 393248 | tf_op jit(solution)/shard_map/ppermute | solution.py:210
  21.8 1.9 collective-permute-start.5
  23.7 64.7 %split_features.1 = (bf16[128,2048]{1,0:T(8,128)(2,1)}, bf16[128,2048]{1,0:T(8,128)(2,1)}, bf16[128,2048]{1,0:T(8,128)(2,1)}, bf16[128,2048]{1,0:T(8,128)(2,1)}) custom-call(bf16[128,8192]{1,0:T(8,128)(2,1)} %x_ref.1), custom_call_target="tpu_custom_call" | custom-call | tf_op jit(solution)/shard_map/split_features/pallas_call | solution.py:231
  88.4 2.4 collective-permute-start
  90.8 4.9 %collective-permute-start.7 = (bf16[256,768]{1,0:T(8,128)(2,1)S(1)}, bf16[256,768]{1,0:T(8,128)(2,1)S(1)}, u32[]{:S(2)}, u32[]{:S(2)}) collective-permute-start(bf16[256,768]{1,0:T(8,128)(2,1)S(1)} %collective-permute-done.5.b), channel_id=1, source_target_pairs={{0,259},{1,256},{2,257},{3,258},{256,1},{257,2},{258,3},{259,0},{4... | collective-permute-start | bytes 1179656 | tf_op jit(solution)/shard_map/ppermute | solution.py:210
  95.7 4.3 %collective-permute-start.1 = (bf16[128,2048]{1,0:T(8,128)(2,1)}, bf16[128,2048]{1,0:T(8,128)(2,1)S(1)}, u32[]{:S(2)}, u32[]{:S(2)}) collective-permute-start(bf16[128,2048]{1,0:T(8,128)(2,1)} %get-tuple-element.50), channel_id=1, source_target_pairs={{0,8},{4,12},{8,0},{12,4},{1,9},{5,13},{9,1},{13,5},{2,10},{6,14},... | collective-permute-start | bytes 1572872 | tf_op jit(solution)/shard_map/ppermute | solution.py:201
  100.0 1.9 collective-permute-start.2
  101.9 1.9 collective-permute-start.4
  103.9 1.5 collective-permute-done.x1
  105.4 1.9 collective-permute-start.6
  107.3 2.4 collective-permute-start.8
  109.7 4.5 %collective-permute-done.1.x2 = bf16[128,2048]{1,0:T(8,128)(2,1)S(1)} collective-permute-done((bf16[128,2048]{1,0:T(8,128)(2,1)}, bf16[128,2048]{1,0:T(8,128)(2,1)S(1)}, u32[]{:S(2)}, u32[]{:S(2)}) %collective-permute-start.1) | collective-permute-done | bytes 524320 | tf_op jit(solution)/shard_map/ppermute | solution.py:201
  114.2 8.6 %collective-permute-done.2.x3 = bf16[128,2048]{1,0:T(8,128)(2,1)S(1)} collective-permute-done((bf16[128,2048]{1,0:T(8,128)(2,1)}, bf16[128,2048]{1,0:T(8,128)(2,1)S(1)}, u32[]{:S(2)}, u32[]{:S(2)}) %collective-permute-start.2) | collective-permute-done | bytes 524320 | tf_op jit(solution)/shard_map/ppermute | solution.py:201
  123.8 1.8 forward.1
  125.6 2.9 collective-permute-start.9
  128.5 3.4 collective-permute-start.10
  131.9 4.5 %collective-permute-start.11 = (bf16[128,768]{1,0:T(8,128)(2,1)S(1)}, bf16[128,768]{1,0:T(8,128)(2,1)S(1)}, u32[]{:S(2)}, u32[]{:S(2)}) collective-permute-start(bf16[128,768]{1,0:T(8,128)(2,1)S(1)} %get-tuple-element.55), channel_id=1, source_target_pairs={{0,4},{4,8},{8,12},{12,0},{1,5},{5,9},{9,13},{13,1},{2,6},{6,10},{... | collective-permute-start | bytes 589832 | tf_op jit(solution)/shard_map/ppermute | solution.py:201
  136.4 3.3 collective-permute-done.9.p1
  139.8 2.5 collective-permute-done.11.p3
  142.3 1.5 attention.1.g0
  143.8 3.7 collective-permute-start.14
  147.5 4.3 %collective-permute-start.13 = (bf16[128,768]{1,0:T(8,128)(2,1)S(1)}, bf16[128,768]{1,0:T(8,128)(2,1)S(1)}, u32[]{:S(2)}, u32[]{:S(2)}) collective-permute-start(bf16[128,768]{1,0:T(8,128)(2,1)S(1)} %attention.1.g0), channel_id=1, source_target_pairs={{0,8},{4,12},{8,0},{12,4},{1,9},{5,13},{9,1},{13,5},{2,10},{6,14},... | collective-permute-start | bytes 589832 | tf_op jit(solution)/shard_map/ppermute | solution.py:201
  151.8 2.7 collective-permute-start.12
  154.6 3.6 collective-permute-done.13.g2
  159.5 2.7 weight_grad.1
  162.2 1.9 collective-permute-start.18
  164.1 3.4 collective-permute-done.18.got
  167.8 3.5 collective-permute-start.19
  171.3 4.5 %collective-permute-start.20 = (bf16[2,24,1024]{2,1,0:T(8,128)(2,1)S(1)}, bf16[2,24,1024]{2,1,0:T(8,128)(2,1)S(1)}, u32[]{:S(2)}, u32[]{:S(2)}) collective-permute-start(bf16[2,24,1024]{2,1,0:T(8,128)(2,1)S(1)} %get-tuple-element.64), channel_id=1, source_target_pairs={{0,64},{32,96},{64,128},{96,160},{128,192},{160,224},{192,0},{224,... | collective-permute-start | bytes 294920 | tf_op jit(solution)/shard_map/ppermute | solution.py:201
  175.8 4.9 %collective-permute-start.21 = (bf16[2,24,1024]{2,1,0:T(8,128)(2,1)S(1)}, bf16[2,24,1024]{2,1,0:T(8,128)(2,1)S(1)}, u32[]{:S(2)}, u32[]{:S(2)}) collective-permute-start(bf16[2,24,1024]{2,1,0:T(8,128)(2,1)S(1)} %get-tuple-element.65), channel_id=1, source_target_pairs={{0,96},{32,128},{64,160},{96,192},{128,224},{160,0},{192,32},{224,... | collective-permute-start | bytes 294920 | tf_op jit(solution)/shard_map/ppermute | solution.py:201
  180.7 3.8 %collective-permute-start.22 = (bf16[2,24,1024]{2,1,0:T(8,128)(2,1)S(1)}, bf16[2,24,1024]{2,1,0:T(8,128)(2,1)S(1)}, u32[]{:S(2)}, u32[]{:S(2)}) collective-permute-start(bf16[2,24,1024]{2,1,0:T(8,128)(2,1)S(1)} %get-tuple-element.66), channel_id=1, source_target_pairs={{0,128},{32,160},{64,192},{96,224},{128,0},{160,32},{192,64},{224,... | collective-permute-start | bytes 294920 | tf_op jit(solution)/shard_map/ppermute | solution.py:201
  184.5 1.8 input_grad.1
  187.2 4.2 %collective-permute-start.15 = (bf16[128,2048]{1,0:T(8,128)(2,1)S(1)}, bf16[128,2048]{1,0:T(8,128)(2,1)S(1)}, u32[]{:S(2)}, u32[]{:S(2)}) collective-permute-start(bf16[128,2048]{1,0:T(8,128)(2,1)S(1)} %get-tuple-element.57), channel_id=1, source_target_pairs={{0,12},{4,0},{8,4},{12,8},{1,13},{5,1},{9,5},{13,9},{2,14},{6,2},{... | collective-permute-start | bytes 1572872 | tf_op jit(solution)/shard_map/ppermute | solution.py:201
  191.4 3.7 collective-permute-start.16
  195.2 3.3 collective-permute-start.17
  198.5 5.2 %collective-permute-start.23 = (bf16[2,24,1024]{2,1,0:T(8,128)(2,1)S(1)}, bf16[2,24,1024]{2,1,0:T(8,128)(2,1)S(1)}, u32[]{:S(2)}, u32[]{:S(2)}) collective-permute-start(bf16[2,24,1024]{2,1,0:T(8,128)(2,1)S(1)} %get-tuple-element.67), channel_id=1, source_target_pairs={{0,160},{32,192},{64,224},{96,0},{128,32},{160,64},{192,96},{224,1... | collective-permute-start | bytes 294920 | tf_op jit(solution)/shard_map/ppermute | solution.py:201
  203.7 5.3 %collective-permute-start.24 = (bf16[2,24,1024]{2,1,0:T(8,128)(2,1)S(1)}, bf16[2,24,1024]{2,1,0:T(8,128)(2,1)S(1)}, u32[]{:S(2)}, u32[]{:S(2)}) collective-permute-start(bf16[2,24,1024]{2,1,0:T(8,128)(2,1)S(1)} %get-tuple-element.68), channel_id=1, source_target_pairs={{0,192},{32,224},{64,0},{96,32},{128,64},{160,96},{192,128},{224,1... | collective-permute-start | bytes 294920 | tf_op jit(solution)/shard_map/ppermute | solution.py:201
  208.9 8.0 %collective-permute-start.25 = (bf16[2,24,1024]{2,1,0:T(8,128)(2,1)S(1)}, bf16[2,24,1024]{2,1,0:T(8,128)(2,1)S(1)}, u32[]{:S(2)}, u32[]{:S(2)}) collective-permute-start(bf16[2,24,1024]{2,1,0:T(8,128)(2,1)S(1)} %get-tuple-element.69), channel_id=1, source_target_pairs={{0,224},{32,0},{64,32},{96,64},{128,96},{160,128},{192,160},{224,1... | collective-permute-start | bytes 294920 | tf_op jit(solution)/shard_map/ppermute | solution.py:201
  216.9 2.5 collective-permute-start.26
  219.7 5.0 %collective-permute-start.27 = (bf16[8,24,256]{2,1,0:T(8,128)(2,1)S(1)}, bf16[8,24,256]{2,1,0:T(8,128)(2,1)S(1)}, u32[]{:S(2)}, u32[]{:S(2)}) collective-permute-start(bf16[8,24,256]{2,1,0:T(8,128)(2,1)S(1)} %get-tuple-element.72), channel_id=1, source_target_pairs={{0,2},{1,3},{2,0},{3,1},{256,258},{257,259},{258,256},{259,257},{4... | collective-permute-start | bytes 294920 | tf_op jit(solution)/shard_map/ppermute | solution.py:210
  224.6 2.1 collective-permute-done.26.refs_9_
  226.7 1.9 collective-permute-start.28
  228.6 1.5 collective-permute-done.27.refs_10_
  230.1 4.0 %collective-permute-start.29 = (bf16[8,24,256]{2,1,0:T(8,128)(2,1)S(1)}, bf16[8,24,256]{2,1,0:T(8,128)(2,1)S(1)}, u32[]{:S(2)}, u32[]{:S(2)}) collective-permute-start(bf16[8,24,256]{2,1,0:T(8,128)(2,1)S(1)} %get-tuple-element.74), channel_id=1, source_target_pairs={{0,256},{1,257},{2,258},{3,259},{256,0},{257,1},{258,2},{259,3},{4... | collective-permute-start | bytes 294920 | tf_op jit(solution)/shard_map/ppermute | solution.py:210
  235.1 3.6 collective-permute-start.30
  238.7 5.5 %collective-permute-start.31 = (bf16[8,24,256]{2,1,0:T(8,128)(2,1)S(1)}, bf16[8,24,256]{2,1,0:T(8,128)(2,1)S(1)}, u32[]{:S(2)}, u32[]{:S(2)}) collective-permute-start(bf16[8,24,256]{2,1,0:T(8,128)(2,1)S(1)} %get-tuple-element.76), channel_id=1, source_target_pairs={{0,258},{1,259},{2,256},{3,257},{256,2},{257,3},{258,0},{259,1},{4... | collective-permute-start | bytes 294920 | tf_op jit(solution)/shard_map/ppermute | solution.py:210
  245.5 2.1 collective-permute-start.32
  248.3 5.4 %collective-permute-done.32.refs_15_ = bf16[8,24,256]{2,1,0:T(8,128)(2,1)S(1)} collective-permute-done((bf16[8,24,256]{2,1,0:T(8,128)(2,1)S(1)}, bf16[8,24,256]{2,1,0:T(8,128)(2,1)S(1)}, u32[]{:S(2)}, u32[]{:S(2)}) %collective-permute-start.32) | collective-permute-done | bytes 98336 | tf_op jit(solution)/shard_map/ppermute | solution.py:210
  254.0 4.4 %collective-permute-start.33 = (bf16[24,256]{1,0:T(8,128)(2,1)S(1)}, bf16[24,256]{1,0:T(8,128)(2,1)S(1)}, u32[]{:S(2)}, u32[]{:S(2)}) collective-permute-start(bf16[24,256]{1,0:T(8,128)(2,1)S(1)} %get-tuple-element.79), channel_id=1, source_target_pairs={{0,1},{1,2},{2,3},{3,0},{256,257},{257,258},{258,259},{259,256},{4... | collective-permute-start | bytes 36872 | tf_op jit(solution)/shard_map/ppermute | solution.py:210
  258.4 3.5 collective-permute-start.34
  261.9 3.9 %collective-permute-start.35 = (bf16[24,256]{1,0:T(8,128)(2,1)S(1)}, bf16[24,256]{1,0:T(8,128)(2,1)S(1)}, u32[]{:S(2)}, u32[]{:S(2)}) collective-permute-start(bf16[24,256]{1,0:T(8,128)(2,1)S(1)} %get-tuple-element.81), channel_id=1, source_target_pairs={{0,3},{1,0},{2,1},{3,2},{256,259},{257,256},{258,257},{259,258},{4... | collective-permute-start | bytes 36872 | tf_op jit(solution)/shard_map/ppermute | solution.py:210
  265.8 3.1 collective-permute-start.36
  269.0 3.1 collective-permute-start.37
  272.1 4.0 %collective-permute-start.38 = (bf16[24,256]{1,0:T(8,128)(2,1)S(1)}, bf16[24,256]{1,0:T(8,128)(2,1)S(1)}, u32[]{:S(2)}, u32[]{:S(2)}) collective-permute-start(bf16[24,256]{1,0:T(8,128)(2,1)S(1)} %get-tuple-element.84), channel_id=1, source_target_pairs={{0,258},{1,259},{2,256},{3,257},{256,2},{257,3},{258,0},{259,1},{4... | collective-permute-start | bytes 36872 | tf_op jit(solution)/shard_map/ppermute | solution.py:210
  276.2 6.0 %collective-permute-start.39 = (bf16[24,256]{1,0:T(8,128)(2,1)S(1)}, bf16[24,256]{1,0:T(8,128)(2,1)S(1)}, u32[]{:S(2)}, u32[]{:S(2)}) collective-permute-start(bf16[24,256]{1,0:T(8,128)(2,1)S(1)} %get-tuple-element.85), channel_id=1, source_target_pairs={{0,259},{1,256},{2,257},{3,258},{256,3},{257,0},{258,1},{259,2},{4... | collective-permute-start | bytes 36872 | tf_op jit(solution)/shard_map/ppermute | solution.py:210
  282.2 1.9 collective-permute-start.40
  284.2 4.9 %collective-permute-start.41 = (bf16[24,256]{1,0:T(8,128)(2,1)S(1)}, bf16[24,256]{1,0:T(8,128)(2,1)S(1)}, u32[]{:S(2)}, u32[]{:S(2)}) collective-permute-start(bf16[24,256]{1,0:T(8,128)(2,1)S(1)} %get-tuple-element.88), channel_id=1, source_target_pairs={{0,64},{32,96},{64,128},{96,160},{128,192},{160,224},{192,0},{224,... | collective-permute-start | bytes 36872 | tf_op jit(solution)/shard_map/ppermute | solution.py:201
  289.1 3.0 collective-permute-start.42
  292.1 6.1 %collective-permute-start.43 = (bf16[24,256]{1,0:T(8,128)(2,1)S(1)}, bf16[24,256]{1,0:T(8,128)(2,1)S(1)}, u32[]{:S(2)}, u32[]{:S(2)}) collective-permute-start(bf16[24,256]{1,0:T(8,128)(2,1)S(1)} %get-tuple-element.90), channel_id=1, source_target_pairs={{0,128},{32,160},{64,192},{96,224},{128,0},{160,32},{192,64},{224,... | collective-permute-start | bytes 36872 | tf_op jit(solution)/shard_map/ppermute | solution.py:201
  298.2 2.7 collective-permute-start.44
  301.0 5.5 %collective-permute-start.45 = (bf16[24,256]{1,0:T(8,128)(2,1)S(1)}, bf16[24,256]{1,0:T(8,128)(2,1)S(1)}, u32[]{:S(2)}, u32[]{:S(2)}) collective-permute-start(bf16[24,256]{1,0:T(8,128)(2,1)S(1)} %get-tuple-element.92), channel_id=1, source_target_pairs={{0,192},{32,224},{64,0},{96,32},{128,64},{160,96},{192,128},{224,1... | collective-permute-start | bytes 36872 | tf_op jit(solution)/shard_map/ppermute | solution.py:201
  306.5 3.9 %collective-permute-start.46 = (bf16[24,256]{1,0:T(8,128)(2,1)S(1)}, bf16[24,256]{1,0:T(8,128)(2,1)S(1)}, u32[]{:S(2)}, u32[]{:S(2)}) collective-permute-start(bf16[24,256]{1,0:T(8,128)(2,1)S(1)} %get-tuple-element.93), channel_id=1, source_target_pairs={{0,224},{32,0},{64,32},{96,64},{128,96},{160,128},{192,160},{224,1... | collective-permute-start | bytes 36872 | tf_op jit(solution)/shard_map/ppermute | solution.py:201
  310.4 64.7 %join_features.1 = bf16[128,8192]{1,0:T(8,128)(2,1)} custom-call(bf16[128,2048]{1,0:T(8,128)(2,1)} %copy-done, bf16[128,2048]{1,0:T(8,128)(2,1)} %copy-done.6, bf16[128,2048]{1,0:T(8,128)(2,1)} %copy-done.7, bf16[128,2048]{1,0:T(8,128)(2,1)} %copy-done.8), custom_call_target="tpu_custom_call" | custom-call | tf_op jit(solution)/shard_map/join_features/pallas_call | solution.py:325
  (58 shorter events, 8.8 us)
Async XLA Ops:
  0.6 122.1 %copy-start.1 = (bf16[512,768]{1,0:T(8,128)(2,1)S(1)}, bf16[512,768]{1,0:T(8,128)(2,1)}, u32[]{:S(2)}) copy-start(bf16[512,768]{1,0:T(8,128)(2,1)} %w0.3) | copy-start | bytes 2359300
  1.7 20.1 %collective-permute-start.3 = (bf16[256,768]{1,0:T(8,128)(2,1)S(1)}, bf16[256,768]{1,0:T(8,128)(2,1)S(1)}, u32[]{:S(2)}, u32[]{:S(2)}) collective-permute-start(bf16[256,768]{1,0:T(8,128)(2,1)S(1)} %constant_dynamic-slice_fusion), channel_id=1, source_target_pairs={{0,259},{1,256},{2,257},{3,258},{256,1},{257,2},{258,3},{259,0},{4... | collective-permute-start | bytes 1179656 | tf_op jit(solution)/shard_map/ppermute | solution.py:210
  21.8 69.0 %collective-permute-start.5 = (bf16[256,768]{1,0:T(8,128)(2,1)S(1)}, bf16[256,768]{1,0:T(8,128)(2,1)S(1)}, u32[]{:S(2)}, u32[]{:S(2)}) collective-permute-start(bf16[256,768]{1,0:T(8,128)(2,1)S(1)} %collective-permute-done.3.a), channel_id=1, source_target_pairs={{0,256},{1,257},{2,258},{3,259},{256,0},{257,1},{258,2},{259,3},{4... | collective-permute-start | bytes 1179656 | tf_op jit(solution)/shard_map/ppermute | solution.py:210
  88.4 17.0 %collective-permute-start = (bf16[128,2048]{1,0:T(8,128)(2,1)}, bf16[128,2048]{1,0:T(8,128)(2,1)S(1)}, u32[]{:S(2)}, u32[]{:S(2)}) collective-permute-start(bf16[128,2048]{1,0:T(8,128)(2,1)} %get-tuple-element.49), channel_id=1, source_target_pairs={{0,4},{4,8},{8,12},{12,0},{1,5},{5,9},{9,13},{13,1},{2,6},{6,10},{... | collective-permute-start | bytes 1572872 | tf_op jit(solution)/shard_map/ppermute | solution.py:201
  90.8 16.5 %collective-permute-start.7 = (bf16[256,768]{1,0:T(8,128)(2,1)S(1)}, bf16[256,768]{1,0:T(8,128)(2,1)S(1)}, u32[]{:S(2)}, u32[]{:S(2)}) collective-permute-start(bf16[256,768]{1,0:T(8,128)(2,1)S(1)} %collective-permute-done.5.b), channel_id=1, source_target_pairs={{0,259},{1,256},{2,257},{3,258},{256,1},{257,2},{258,3},{259,0},{4... | collective-permute-start | bytes 1179656 | tf_op jit(solution)/shard_map/ppermute | solution.py:210
  95.7 18.5 %collective-permute-start.1 = (bf16[128,2048]{1,0:T(8,128)(2,1)}, bf16[128,2048]{1,0:T(8,128)(2,1)S(1)}, u32[]{:S(2)}, u32[]{:S(2)}) collective-permute-start(bf16[128,2048]{1,0:T(8,128)(2,1)} %get-tuple-element.50), channel_id=1, source_target_pairs={{0,8},{4,12},{8,0},{12,4},{1,9},{5,13},{9,1},{13,5},{2,10},{6,14},... | collective-permute-start | bytes 1572872 | tf_op jit(solution)/shard_map/ppermute | solution.py:201
  100.0 22.7 %collective-permute-start.2 = (bf16[128,2048]{1,0:T(8,128)(2,1)}, bf16[128,2048]{1,0:T(8,128)(2,1)S(1)}, u32[]{:S(2)}, u32[]{:S(2)}) collective-permute-start(bf16[128,2048]{1,0:T(8,128)(2,1)} %get-tuple-element.51), channel_id=1, source_target_pairs={{0,12},{4,0},{8,4},{12,8},{1,13},{5,1},{9,5},{13,9},{2,14},{6,2},{... | collective-permute-start | bytes 1572872 | tf_op jit(solution)/shard_map/ppermute | solution.py:201
  101.9 20.8 %collective-permute-start.4 = (bf16[256,768]{1,0:T(8,128)(2,1)S(1)}, bf16[256,768]{1,0:T(8,128)(2,1)S(1)}, u32[]{:S(2)}, u32[]{:S(2)}) collective-permute-start(bf16[256,768]{1,0:T(8,128)(2,1)S(1)} %collective-permute-done.3.a), channel_id=1, source_target_pairs={{0,16},{16,0},{1,17},{17,1},{2,18},{18,2},{3,19},{19,3},{4,20},{20... | collective-permute-start | bytes 1179656 | tf_op jit(solution)/shard_map/ppermute | solution.py:201
  105.4 17.4 %collective-permute-start.6 = (bf16[256,768]{1,0:T(8,128)(2,1)S(1)}, bf16[256,768]{1,0:T(8,128)(2,1)S(1)}, u32[]{:S(2)}, u32[]{:S(2)}) collective-permute-start(bf16[256,768]{1,0:T(8,128)(2,1)S(1)} %collective-permute-done.5.b), channel_id=1, source_target_pairs={{0,16},{16,0},{1,17},{17,1},{2,18},{18,2},{3,19},{19,3},{4,20},{20... | collective-permute-start | bytes 1179656 | tf_op jit(solution)/shard_map/ppermute | solution.py:201
  107.3 15.5 %collective-permute-start.8 = (bf16[256,768]{1,0:T(8,128)(2,1)S(1)}, bf16[256,768]{1,0:T(8,128)(2,1)S(1)}, u32[]{:S(2)}, u32[]{:S(2)}) collective-permute-start(bf16[256,768]{1,0:T(8,128)(2,1)S(1)} %collective-permute-done.7.d), channel_id=1, source_target_pairs={{0,16},{16,0},{1,17},{17,1},{2,18},{18,2},{3,19},{19,3},{4,20},{20... | collective-permute-start | bytes 1179656 | tf_op jit(solution)/shard_map/ppermute | solution.py:201
  122.8 1.0 copy-start.4
  123.8 18.5 %copy-start.2 = (bf16[128,512]{1,0:T(8,128)(2,1)S(1)}, bf16[128,512]{1,0:T(8,128)(2,1)}, u32[]{:S(2)}) copy-start(bf16[128,512]{1,0:T(8,128)(2,1)} %cot_ref.1) | copy-start | bytes 393220
  123.8 18.5 %copy-start.3 = (s32[1,128]{1,0:T(1,128)S(1)}, s32[1,128]{1,0:T(1,128)}, u32[]{:S(2)}) copy-start(s32[1,128]{1,0:T(1,128)} %seg_ref.1) | copy-start | bytes 1540
  123.8 35.7 %copy-start.5 = (bf16[128,2048]{1,0:T(8,128)(2,1)S(1)}, bf16[128,2048]{1,0:T(8,128)(2,1)}, u32[]{:S(2)}) copy-start(bf16[128,2048]{1,0:T(8,128)(2,1)} %get-tuple-element.48.x0) | copy-start | bytes 1572868
  125.6 14.1 %collective-permute-start.9 = (bf16[128,768]{1,0:T(8,128)(2,1)S(1)}, bf16[128,768]{1,0:T(8,128)(2,1)S(1)}, u32[]{:S(2)}, u32[]{:S(2)}) collective-permute-start(bf16[128,768]{1,0:T(8,128)(2,1)S(1)} %get-tuple-element.53), channel_id=1, source_target_pairs={{0,12},{4,0},{8,4},{12,8},{1,13},{5,1},{9,5},{13,9},{2,14},{6,2},{... | collective-permute-start | bytes 589832 | tf_op jit(solution)/shard_map/ppermute | solution.py:201
  128.5 11.3 %collective-permute-start.10 = (bf16[128,768]{1,0:T(8,128)(2,1)S(1)}, bf16[128,768]{1,0:T(8,128)(2,1)S(1)}, u32[]{:S(2)}, u32[]{:S(2)}) collective-permute-start(bf16[128,768]{1,0:T(8,128)(2,1)S(1)} %get-tuple-element.54), channel_id=1, source_target_pairs={{0,8},{4,12},{8,0},{12,4},{1,9},{5,13},{9,1},{13,5},{2,10},{6,14},... | collective-permute-start | bytes 589832 | tf_op jit(solution)/shard_map/ppermute | solution.py:201
  131.9 10.4 %collective-permute-start.11 = (bf16[128,768]{1,0:T(8,128)(2,1)S(1)}, bf16[128,768]{1,0:T(8,128)(2,1)S(1)}, u32[]{:S(2)}, u32[]{:S(2)}) collective-permute-start(bf16[128,768]{1,0:T(8,128)(2,1)S(1)} %get-tuple-element.55), channel_id=1, source_target_pairs={{0,4},{4,8},{8,12},{12,0},{1,5},{5,9},{9,13},{13,1},{2,6},{6,10},{... | collective-permute-start | bytes 589832 | tf_op jit(solution)/shard_map/ppermute | solution.py:201
  143.8 10.8 %collective-permute-start.14 = (bf16[128,768]{1,0:T(8,128)(2,1)S(1)}, bf16[128,768]{1,0:T(8,128)(2,1)S(1)}, u32[]{:S(2)}, u32[]{:S(2)}) collective-permute-start(bf16[128,768]{1,0:T(8,128)(2,1)S(1)} %attention.1.g0), channel_id=1, source_target_pairs={{0,12},{4,0},{8,4},{12,8},{1,13},{5,1},{9,5},{13,9},{2,14},{6,2},{... | collective-permute-start | bytes 589832 | tf_op jit(solution)/shard_map/ppermute | solution.py:201
  147.5 10.7 %collective-permute-start.13 = (bf16[128,768]{1,0:T(8,128)(2,1)S(1)}, bf16[128,768]{1,0:T(8,128)(2,1)S(1)}, u32[]{:S(2)}, u32[]{:S(2)}) collective-permute-start(bf16[128,768]{1,0:T(8,128)(2,1)S(1)} %attention.1.g0), channel_id=1, source_target_pairs={{0,8},{4,12},{8,0},{12,4},{1,9},{5,13},{9,1},{13,5},{2,10},{6,14},... | collective-permute-start | bytes 589832 | tf_op jit(solution)/shard_map/ppermute | solution.py:201
  151.8 7.7 %collective-permute-start.12 = (bf16[128,768]{1,0:T(8,128)(2,1)S(1)}, bf16[128,768]{1,0:T(8,128)(2,1)S(1)}, u32[]{:S(2)}, u32[]{:S(2)}) collective-permute-start(bf16[128,768]{1,0:T(8,128)(2,1)S(1)} %attention.1.g0), channel_id=1, source_target_pairs={{0,4},{4,8},{8,12},{12,0},{1,5},{5,9},{9,13},{13,1},{2,6},{6,10},{... | collective-permute-start | bytes 589832 | tf_op jit(solution)/shard_map/ppermute | solution.py:201
  162.2 5.3 %collective-permute-start.18 = (bf16[16,24,2048]{2,1,0:T(8,128)(2,1)S(1)}, bf16[16,24,2048]{2,1,0:T(8,128)(2,1)S(1)}, u32[]{:S(2)}, u32[]{:S(2)}) collective-permute-start(bf16[16,24,2048]{2,1,0:T(8,128)(2,1)S(1)} %get-tuple-element.61), channel_id=1, source_target_pairs={{0,16},{16,0},{1,17},{17,1},{2,18},{18,2},{3,19},{19,3},{4,20},{20... | collective-permute-start | bytes 4718600 | tf_op jit(solution)/shard_map/ppermute | solution.py:201
  167.8 23.6 %collective-permute-start.19 = (bf16[2,24,1024]{2,1,0:T(8,128)(2,1)S(1)}, bf16[2,24,1024]{2,1,0:T(8,128)(2,1)S(1)}, u32[]{:S(2)}, u32[]{:S(2)}) collective-permute-start(bf16[2,24,1024]{2,1,0:T(8,128)(2,1)S(1)} %get-tuple-element.63), channel_id=1, source_target_pairs={{0,32},{32,64},{64,96},{96,128},{128,160},{160,192},{192,224},{224... | collective-permute-start | bytes 294920 | tf_op jit(solution)/shard_map/ppermute | solution.py:201
  171.3 23.9 %collective-permute-start.20 = (bf16[2,24,1024]{2,1,0:T(8,128)(2,1)S(1)}, bf16[2,24,1024]{2,1,0:T(8,128)(2,1)S(1)}, u32[]{:S(2)}, u32[]{:S(2)}) collective-permute-start(bf16[2,24,1024]{2,1,0:T(8,128)(2,1)S(1)} %get-tuple-element.64), channel_id=1, source_target_pairs={{0,64},{32,96},{64,128},{96,160},{128,192},{160,224},{192,0},{224,... | collective-permute-start | bytes 294920 | tf_op jit(solution)/shard_map/ppermute | solution.py:201
  175.8 22.7 %collective-permute-start.21 = (bf16[2,24,1024]{2,1,0:T(8,128)(2,1)S(1)}, bf16[2,24,1024]{2,1,0:T(8,128)(2,1)S(1)}, u32[]{:S(2)}, u32[]{:S(2)}) collective-permute-start(bf16[2,24,1024]{2,1,0:T(8,128)(2,1)S(1)} %get-tuple-element.65), channel_id=1, source_target_pairs={{0,96},{32,128},{64,160},{96,192},{128,224},{160,0},{192,32},{224,... | collective-permute-start | bytes 294920 | tf_op jit(solution)/shard_map/ppermute | solution.py:201
  180.7 23.0 %collective-permute-start.22 = (bf16[2,24,1024]{2,1,0:T(8,128)(2,1)S(1)}, bf16[2,24,1024]{2,1,0:T(8,128)(2,1)S(1)}, u32[]{:S(2)}, u32[]{:S(2)}) collective-permute-start(bf16[2,24,1024]{2,1,0:T(8,128)(2,1)S(1)} %get-tuple-element.66), channel_id=1, source_target_pairs={{0,128},{32,160},{64,192},{96,224},{128,0},{160,32},{192,64},{224,... | collective-permute-start | bytes 294920 | tf_op jit(solution)/shard_map/ppermute | solution.py:201
  186.4 0.8 copy-start
  187.2 74.7 %collective-permute-start.15 = (bf16[128,2048]{1,0:T(8,128)(2,1)S(1)}, bf16[128,2048]{1,0:T(8,128)(2,1)S(1)}, u32[]{:S(2)}, u32[]{:S(2)}) collective-permute-start(bf16[128,2048]{1,0:T(8,128)(2,1)S(1)} %get-tuple-element.57), channel_id=1, source_target_pairs={{0,12},{4,0},{8,4},{12,8},{1,13},{5,1},{9,5},{13,9},{2,14},{6,2},{... | collective-permute-start | bytes 1572872 | tf_op jit(solution)/shard_map/ppermute | solution.py:201
  191.4 74.4 %collective-permute-start.16 = (bf16[128,2048]{1,0:T(8,128)(2,1)S(1)}, bf16[128,2048]{1,0:T(8,128)(2,1)S(1)}, u32[]{:S(2)}, u32[]{:S(2)}) collective-permute-start(bf16[128,2048]{1,0:T(8,128)(2,1)S(1)} %get-tuple-element.58), channel_id=1, source_target_pairs={{0,8},{4,12},{8,0},{12,4},{1,9},{5,13},{9,1},{13,5},{2,10},{6,14},... | collective-permute-start | bytes 1572872 | tf_op jit(solution)/shard_map/ppermute | solution.py:201
  195.2 73.8 %collective-permute-start.17 = (bf16[128,2048]{1,0:T(8,128)(2,1)S(1)}, bf16[128,2048]{1,0:T(8,128)(2,1)S(1)}, u32[]{:S(2)}, u32[]{:S(2)}) collective-permute-start(bf16[128,2048]{1,0:T(8,128)(2,1)S(1)} %get-tuple-element.59), channel_id=1, source_target_pairs={{0,4},{4,8},{8,12},{12,0},{1,5},{5,9},{9,13},{13,1},{2,6},{6,10},{... | collective-permute-start | bytes 1572872 | tf_op jit(solution)/shard_map/ppermute | solution.py:201
  198.5 10.4 %collective-permute-start.23 = (bf16[2,24,1024]{2,1,0:T(8,128)(2,1)S(1)}, bf16[2,24,1024]{2,1,0:T(8,128)(2,1)S(1)}, u32[]{:S(2)}, u32[]{:S(2)}) collective-permute-start(bf16[2,24,1024]{2,1,0:T(8,128)(2,1)S(1)} %get-tuple-element.67), channel_id=1, source_target_pairs={{0,160},{32,192},{64,224},{96,0},{128,32},{160,64},{192,96},{224,1... | collective-permute-start | bytes 294920 | tf_op jit(solution)/shard_map/ppermute | solution.py:201
  203.7 13.3 %collective-permute-start.24 = (bf16[2,24,1024]{2,1,0:T(8,128)(2,1)S(1)}, bf16[2,24,1024]{2,1,0:T(8,128)(2,1)S(1)}, u32[]{:S(2)}, u32[]{:S(2)}) collective-permute-start(bf16[2,24,1024]{2,1,0:T(8,128)(2,1)S(1)} %get-tuple-element.68), channel_id=1, source_target_pairs={{0,192},{32,224},{64,0},{96,32},{128,64},{160,96},{192,128},{224,1... | collective-permute-start | bytes 294920 | tf_op jit(solution)/shard_map/ppermute | solution.py:201
  208.9 10.7 %collective-permute-start.25 = (bf16[2,24,1024]{2,1,0:T(8,128)(2,1)S(1)}, bf16[2,24,1024]{2,1,0:T(8,128)(2,1)S(1)}, u32[]{:S(2)}, u32[]{:S(2)}) collective-permute-start(bf16[2,24,1024]{2,1,0:T(8,128)(2,1)S(1)} %get-tuple-element.69), channel_id=1, source_target_pairs={{0,224},{32,0},{64,32},{96,64},{128,96},{160,128},{192,160},{224,1... | collective-permute-start | bytes 294920 | tf_op jit(solution)/shard_map/ppermute | solution.py:201
  216.9 9.7 %collective-permute-start.26 = (bf16[8,24,256]{2,1,0:T(8,128)(2,1)S(1)}, bf16[8,24,256]{2,1,0:T(8,128)(2,1)S(1)}, u32[]{:S(2)}, u32[]{:S(2)}) collective-permute-start(bf16[8,24,256]{2,1,0:T(8,128)(2,1)S(1)} %get-tuple-element.71), channel_id=1, source_target_pairs={{0,1},{1,2},{2,3},{3,0},{256,257},{257,258},{258,259},{259,256},{4... | collective-permute-start | bytes 294920 | tf_op jit(solution)/shard_map/ppermute | solution.py:210
  219.7 10.4 %collective-permute-start.27 = (bf16[8,24,256]{2,1,0:T(8,128)(2,1)S(1)}, bf16[8,24,256]{2,1,0:T(8,128)(2,1)S(1)}, u32[]{:S(2)}, u32[]{:S(2)}) collective-permute-start(bf16[8,24,256]{2,1,0:T(8,128)(2,1)S(1)} %get-tuple-element.72), channel_id=1, source_target_pairs={{0,2},{1,3},{2,0},{3,1},{256,258},{257,259},{258,256},{259,257},{4... | collective-permute-start | bytes 294920 | tf_op jit(solution)/shard_map/ppermute | solution.py:210
  226.7 8.5 %collective-permute-start.28 = (bf16[8,24,256]{2,1,0:T(8,128)(2,1)S(1)}, bf16[8,24,256]{2,1,0:T(8,128)(2,1)S(1)}, u32[]{:S(2)}, u32[]{:S(2)}) collective-permute-start(bf16[8,24,256]{2,1,0:T(8,128)(2,1)S(1)} %get-tuple-element.73), channel_id=1, source_target_pairs={{0,3},{1,0},{2,1},{3,2},{256,259},{257,256},{258,257},{259,258},{4... | collective-permute-start | bytes 294920 | tf_op jit(solution)/shard_map/ppermute | solution.py:210
  230.1 8.6 %collective-permute-start.29 = (bf16[8,24,256]{2,1,0:T(8,128)(2,1)S(1)}, bf16[8,24,256]{2,1,0:T(8,128)(2,1)S(1)}, u32[]{:S(2)}, u32[]{:S(2)}) collective-permute-start(bf16[8,24,256]{2,1,0:T(8,128)(2,1)S(1)} %get-tuple-element.74), channel_id=1, source_target_pairs={{0,256},{1,257},{2,258},{3,259},{256,0},{257,1},{258,2},{259,3},{4... | collective-permute-start | bytes 294920 | tf_op jit(solution)/shard_map/ppermute | solution.py:210
  235.1 10.3 %collective-permute-start.30 = (bf16[8,24,256]{2,1,0:T(8,128)(2,1)S(1)}, bf16[8,24,256]{2,1,0:T(8,128)(2,1)S(1)}, u32[]{:S(2)}, u32[]{:S(2)}) collective-permute-start(bf16[8,24,256]{2,1,0:T(8,128)(2,1)S(1)} %get-tuple-element.75), channel_id=1, source_target_pairs={{0,257},{1,258},{2,259},{3,256},{256,1},{257,2},{258,3},{259,0},{4... | collective-permute-start | bytes 294920 | tf_op jit(solution)/shard_map/ppermute | solution.py:210
  238.7 9.6 %collective-permute-start.31 = (bf16[8,24,256]{2,1,0:T(8,128)(2,1)S(1)}, bf16[8,24,256]{2,1,0:T(8,128)(2,1)S(1)}, u32[]{:S(2)}, u32[]{:S(2)}) collective-permute-start(bf16[8,24,256]{2,1,0:T(8,128)(2,1)S(1)} %get-tuple-element.76), channel_id=1, source_target_pairs={{0,258},{1,259},{2,256},{3,257},{256,2},{257,3},{258,0},{259,1},{4... | collective-permute-start | bytes 294920 | tf_op jit(solution)/shard_map/ppermute | solution.py:210
  245.5 8.3 %collective-permute-start.32 = (bf16[8,24,256]{2,1,0:T(8,128)(2,1)S(1)}, bf16[8,24,256]{2,1,0:T(8,128)(2,1)S(1)}, u32[]{:S(2)}, u32[]{:S(2)}) collective-permute-start(bf16[8,24,256]{2,1,0:T(8,128)(2,1)S(1)} %get-tuple-element.77), channel_id=1, source_target_pairs={{0,259},{1,256},{2,257},{3,258},{256,3},{257,0},{258,1},{259,2},{4... | collective-permute-start | bytes 294920 | tf_op jit(solution)/shard_map/ppermute | solution.py:210
  254.0 18.2 %collective-permute-start.33 = (bf16[24,256]{1,0:T(8,128)(2,1)S(1)}, bf16[24,256]{1,0:T(8,128)(2,1)S(1)}, u32[]{:S(2)}, u32[]{:S(2)}) collective-permute-start(bf16[24,256]{1,0:T(8,128)(2,1)S(1)} %get-tuple-element.79), channel_id=1, source_target_pairs={{0,1},{1,2},{2,3},{3,0},{256,257},{257,258},{258,259},{259,256},{4... | collective-permute-start | bytes 36872 | tf_op jit(solution)/shard_map/ppermute | solution.py:210
  258.4 17.8 %collective-permute-start.34 = (bf16[24,256]{1,0:T(8,128)(2,1)S(1)}, bf16[24,256]{1,0:T(8,128)(2,1)S(1)}, u32[]{:S(2)}, u32[]{:S(2)}) collective-permute-start(bf16[24,256]{1,0:T(8,128)(2,1)S(1)} %get-tuple-element.80), channel_id=1, source_target_pairs={{0,2},{1,3},{2,0},{3,1},{256,258},{257,259},{258,256},{259,257},{4... | collective-permute-start | bytes 36872 | tf_op jit(solution)/shard_map/ppermute | solution.py:210
  261.9 48.5 %copy-start.6 = (bf16[128,2048]{1,0:T(8,128)(2,1)}, bf16[128,2048]{1,0:T(8,128)(2,1)S(1)}, u32[]{:S(2)}) copy-start(bf16[128,2048]{1,0:T(8,128)(2,1)S(1)} %collective-permute-done.15.refs_1_) | copy-start | bytes 1572868
  261.9 20.3 %collective-permute-start.35 = (bf16[24,256]{1,0:T(8,128)(2,1)S(1)}, bf16[24,256]{1,0:T(8,128)(2,1)S(1)}, u32[]{:S(2)}, u32[]{:S(2)}) collective-permute-start(bf16[24,256]{1,0:T(8,128)(2,1)S(1)} %get-tuple-element.81), channel_id=1, source_target_pairs={{0,3},{1,0},{2,1},{3,2},{256,259},{257,256},{258,257},{259,258},{4... | collective-permute-start | bytes 36872 | tf_op jit(solution)/shard_map/ppermute | solution.py:210
  265.8 44.6 %copy-start.7 = (bf16[128,2048]{1,0:T(8,128)(2,1)}, bf16[128,2048]{1,0:T(8,128)(2,1)S(1)}, u32[]{:S(2)}) copy-start(bf16[128,2048]{1,0:T(8,128)(2,1)S(1)} %collective-permute-done.16.refs_2_) | copy-start | bytes 1572868
  265.8 18.3 %collective-permute-start.36 = (bf16[24,256]{1,0:T(8,128)(2,1)S(1)}, bf16[24,256]{1,0:T(8,128)(2,1)S(1)}, u32[]{:S(2)}, u32[]{:S(2)}) collective-permute-start(bf16[24,256]{1,0:T(8,128)(2,1)S(1)} %get-tuple-element.82), channel_id=1, source_target_pairs={{0,256},{1,257},{2,258},{3,259},{256,0},{257,1},{258,2},{259,3},{4... | collective-permute-start | bytes 36872 | tf_op jit(solution)/shard_map/ppermute | solution.py:210
  269.0 41.5 %copy-start.8 = (bf16[128,2048]{1,0:T(8,128)(2,1)}, bf16[128,2048]{1,0:T(8,128)(2,1)S(1)}, u32[]{:S(2)}) copy-start(bf16[128,2048]{1,0:T(8,128)(2,1)S(1)} %collective-permute-done.17.refs_3_) | copy-start | bytes 1572868
  269.0 20.1 %collective-permute-start.37 = (bf16[24,256]{1,0:T(8,128)(2,1)S(1)}, bf16[24,256]{1,0:T(8,128)(2,1)S(1)}, u32[]{:S(2)}, u32[]{:S(2)}) collective-permute-start(bf16[24,256]{1,0:T(8,128)(2,1)S(1)} %get-tuple-element.83), channel_id=1, source_target_pairs={{0,257},{1,258},{2,259},{3,256},{256,1},{257,2},{258,3},{259,0},{4... | collective-permute-start | bytes 36872 | tf_op jit(solution)/shard_map/ppermute | solution.py:210
  272.1 20.0 %collective-permute-start.38 = (bf16[24,256]{1,0:T(8,128)(2,1)S(1)}, bf16[24,256]{1,0:T(8,128)(2,1)S(1)}, u32[]{:S(2)}, u32[]{:S(2)}) collective-permute-start(bf16[24,256]{1,0:T(8,128)(2,1)S(1)} %get-tuple-element.84), channel_id=1, source_target_pairs={{0,258},{1,259},{2,256},{3,257},{256,2},{257,3},{258,0},{259,1},{4... | collective-permute-start | bytes 36872 | tf_op jit(solution)/shard_map/ppermute | solution.py:210
  276.2 22.0 %collective-permute-start.39 = (bf16[24,256]{1,0:T(8,128)(2,1)S(1)}, bf16[24,256]{1,0:T(8,128)(2,1)S(1)}, u32[]{:S(2)}, u32[]{:S(2)}) collective-permute-start(bf16[24,256]{1,0:T(8,128)(2,1)S(1)} %get-tuple-element.85), channel_id=1, source_target_pairs={{0,259},{1,256},{2,257},{3,258},{256,3},{257,0},{258,1},{259,2},{4... | collective-permute-start | bytes 36872 | tf_op jit(solution)/shard_map/ppermute | solution.py:210
  282.2 18.7 %collective-permute-start.40 = (bf16[24,256]{1,0:T(8,128)(2,1)S(1)}, bf16[24,256]{1,0:T(8,128)(2,1)S(1)}, u32[]{:S(2)}, u32[]{:S(2)}) collective-permute-start(bf16[24,256]{1,0:T(8,128)(2,1)S(1)} %get-tuple-element.87), channel_id=1, source_target_pairs={{0,32},{32,64},{64,96},{96,128},{128,160},{160,192},{192,224},{224... | collective-permute-start | bytes 36872 | tf_op jit(solution)/shard_map/ppermute | solution.py:201
  284.2 22.3 %collective-permute-start.41 = (bf16[24,256]{1,0:T(8,128)(2,1)S(1)}, bf16[24,256]{1,0:T(8,128)(2,1)S(1)}, u32[]{:S(2)}, u32[]{:S(2)}) collective-permute-start(bf16[24,256]{1,0:T(8,128)(2,1)S(1)} %get-tuple-element.88), channel_id=1, source_target_pairs={{0,64},{32,96},{64,128},{96,160},{128,192},{160,224},{192,0},{224,... | collective-permute-start | bytes 36872 | tf_op jit(solution)/shard_map/ppermute | solution.py:201
  289.1 86.0 %collective-permute-start.42 = (bf16[24,256]{1,0:T(8,128)(2,1)S(1)}, bf16[24,256]{1,0:T(8,128)(2,1)S(1)}, u32[]{:S(2)}, u32[]{:S(2)}) collective-permute-start(bf16[24,256]{1,0:T(8,128)(2,1)S(1)} %get-tuple-element.89), channel_id=1, source_target_pairs={{0,96},{32,128},{64,160},{96,192},{128,224},{160,0},{192,32},{224,... | collective-permute-start | bytes 36872 | tf_op jit(solution)/shard_map/ppermute | solution.py:201
  292.1 83.0 %collective-permute-start.43 = (bf16[24,256]{1,0:T(8,128)(2,1)S(1)}, bf16[24,256]{1,0:T(8,128)(2,1)S(1)}, u32[]{:S(2)}, u32[]{:S(2)}) collective-permute-start(bf16[24,256]{1,0:T(8,128)(2,1)S(1)} %get-tuple-element.90), channel_id=1, source_target_pairs={{0,128},{32,160},{64,192},{96,224},{128,0},{160,32},{192,64},{224,... | collective-permute-start | bytes 36872 | tf_op jit(solution)/shard_map/ppermute | solution.py:201
  298.2 76.9 %collective-permute-start.44 = (bf16[24,256]{1,0:T(8,128)(2,1)S(1)}, bf16[24,256]{1,0:T(8,128)(2,1)S(1)}, u32[]{:S(2)}, u32[]{:S(2)}) collective-permute-start(bf16[24,256]{1,0:T(8,128)(2,1)S(1)} %get-tuple-element.91), channel_id=1, source_target_pairs={{0,160},{32,192},{64,224},{96,0},{128,32},{160,64},{192,96},{224,1... | collective-permute-start | bytes 36872 | tf_op jit(solution)/shard_map/ppermute | solution.py:201
  301.0 74.2 %collective-permute-start.45 = (bf16[24,256]{1,0:T(8,128)(2,1)S(1)}, bf16[24,256]{1,0:T(8,128)(2,1)S(1)}, u32[]{:S(2)}, u32[]{:S(2)}) collective-permute-start(bf16[24,256]{1,0:T(8,128)(2,1)S(1)} %get-tuple-element.92), channel_id=1, source_target_pairs={{0,192},{32,224},{64,0},{96,32},{128,64},{160,96},{192,128},{224,1... | collective-permute-start | bytes 36872 | tf_op jit(solution)/shard_map/ppermute | solution.py:201
  306.5 68.7 %collective-permute-start.46 = (bf16[24,256]{1,0:T(8,128)(2,1)S(1)}, bf16[24,256]{1,0:T(8,128)(2,1)S(1)}, u32[]{:S(2)}, u32[]{:S(2)}) collective-permute-start(bf16[24,256]{1,0:T(8,128)(2,1)S(1)} %get-tuple-element.93), channel_id=1, source_target_pairs={{0,224},{32,0},{64,32},{96,64},{128,96},{160,128},{192,160},{224,1... | collective-permute-start | bytes 36872 | tf_op jit(solution)/shard_map/ppermute | solution.py:201

commit v2 on v1

v2 whole, which is shorter than its diff:
```python
import math

import jax
import jax.numpy as jnp
from jax import lax
from jax.experimental import pallas as pl
from jax.experimental.pallas import tpu as pltpu
from jax.sharding import Mesh
from jax.sharding import PartitionSpec as P

HD = 128
BF16 = jnp.bfloat16
F32 = jnp.float32
PARAMS = pltpu.CompilerParams(vmem_limit_bytes=40 * 1024 * 1024)

NT = (((1,), (1,)), ((), ()))
TN = (((0,), (0,)), ((), ()))


def arr(shape, dtype=BF16):
    return jax.ShapeDtypeStruct(shape, dtype)


def cost(flops, nbytes):
    return pl.CostEstimate(flops=flops, bytes_accessed=nbytes, transcendentals=0)


def dot(a, b, dims=(((1,), (0,)), ((), ()))):
    return lax.dot_general(a, b, dims, preferred_element_type=F32)


def join_kernel(*refs):
    ins, out = refs[:-1], refs[-1]
    n = len(ins)
    width = ins[0].shape[1]
    me = lax.axis_index("x")
    for k in range(n):
        start = pl.multiple_of(lax.rem(me + k, n) * width, width)
        out[:, pl.ds(start, width)] = ins[k][...]


def piece_places(rows):
    zl, zh, c = lax.axis_index("zl"), lax.axis_index("zh"), lax.axis_index("c")
    near = lax.rem(zh + 3 + 2 * zl, 4)
    far = lax.rem(zh + 5 - 2 * zl, 4)
    opposite = lax.rem(zh + 2, 4)
    places = [zh * (2 * rows)]
    for block in (near, far, opposite):
        places.append(block * (2 * rows) + c * rows)
        places.append(block * (2 * rows) + (1 - c) * rows)
    return [pl.multiple_of(p, rows) for p in places]


def forward_kernel(x0, x1, x2, x3, w0, a, a2, b, b2, d, d2, parts, acc):
    rows = a.shape[0]
    places = piece_places(rows)
    xs = (x0, x1, x2, x3)
    tokens = x0.shape[0]
    for i, (place, w) in enumerate(zip(places, (w0, a, a2, b, b2, d, d2))):
        depth = w.shape[0]
        x = jnp.concatenate([r[:, pl.ds(place, depth)] for r in xs], axis=0)
        term = dot(x, w[...])
        if i == 0:
            acc[...] = term
        else:
            acc[...] += term
    me = lax.axis_index("x")
    for k in range(4):
        parts[lax.rem(me + 4 - k, 4)] = acc[k * tokens : (k + 1) * tokens, :].astype(BF16)


def attention_kernel(parts, seg_ref, cot_ref, out):
    total = sum(parts[k].astype(F32) for k in range(4))
    projected = total.astype(BF16)
    count = projected.shape[0]
    heads = cot_ref.shape[1] // HD
    row = jnp.broadcast_to(seg_ref[...], (count, count))
    col = row.T
    here = lax.broadcasted_iota(jnp.int32, (count, count), 0)
    there = lax.broadcasted_iota(jnp.int32, (count, count), 1)
    allowed = (here >= there) & (row == col)
    keys = projected[:, heads * HD : (heads + 1) * HD]
    vals = projected[:, (heads + 1) * HD :]
    scale = 1.0 / math.sqrt(HD)
    grad_k = jnp.zeros((count, HD), F32)
    grad_v = jnp.zeros((count, HD), F32)
    for h in range(heads):
        query = projected[:, h * HD : (h + 1) * HD]
        cot = cot_ref[:, h * HD : (h + 1) * HD]
        scores = dot(query, keys, NT) * scale
        scores = jnp.where(allowed, scores, 0.0)
        weights = jnp.where(allowed, jnp.exp(scores), 0.0)
        weights = weights / jnp.sum(weights, axis=1, keepdims=True)
        grad_w = dot(cot, vals, NT)
        lean = jnp.sum(weights * grad_w, axis=1, keepdims=True)
        grad_s = (weights * (grad_w - lean) * scale).astype(BF16)
        out[:, h * HD : (h + 1) * HD] = dot(grad_s, keys).astype(BF16)
        grad_k += dot(grad_s, query, TN)
        grad_v += dot(weights.astype(BF16), cot, TN)
    out[:, heads * HD : (heads + 1) * HD] = grad_k.astype(BF16)
    out[:, (heads + 1) * HD :] = grad_v.astype(BF16)


def relative(gathered):
    me = lax.axis_index("x")
    return jnp.concatenate([gathered[lax.rem(me + 4 - k, 4)] for k in range(4)], axis=0)


def weight_kernel(g, x0, x1, x2, x3, mine, other):
    pieces, span, block = mine.shape
    groups = pieces // 4
    c = lax.axis_index("c")
    grads = relative(g)
    shape = (groups * span, grads.shape[1])
    place = lax.broadcasted_iota(jnp.int32, shape, 0)
    source = lax.broadcasted_iota(jnp.int32, shape, 1)
    left = []
    for core in (c, 1 - c):
        wanted = (place // span * 2 + core) * span + place % span
        pick = jnp.where(source == wanted, 1.0, 0.0).astype(BF16)
        left.append(dot(pick, grads, NT).astype(BF16))
    tile = 256
    for zh in range(4):
        for at in range(0, block, tile):
            start = zh * block + at
            x = jnp.concatenate([r[:, start : start + tile] for r in (x0, x1, x2, x3)], axis=0)
            for out, rows in ((other, left[1]), (mine, left[0])):
                term = dot(rows, x)
                for k in range(groups):
                    out[k * 4 + zh, :, at : at + tile] = term[k * span : (k + 1) * span].astype(out.dtype)


def input_kernel(g, w0, a, a2, b, b2, d, d2, o0, o1, o2, o3):
    rows = a.shape[0]
    tokens = g.shape[1]
    places = piece_places(rows)
    grads = relative(g)
    for place, w in zip(places, (w0, a, a2, b, b2, d, d2)):
        depth = w.shape[0]
        term = dot(grads, w[...], NT).astype(BF16)
        for k, o in enumerate((o0, o1, o2, o3)):
            o[:, pl.ds(place, depth)] = term[k * tokens : (k + 1) * tokens]


def add_kernel(mine, got, out):
    out[...] = (mine[...] + got[...].astype(F32)).astype(BF16)


def total_kernel(ref, out):
    out[...] = jnp.sum(ref[...].astype(F32), axis=0)


def shift(value, axis, k):
    n = lax.axis_size(axis)
    return lax.ppermute(value, axis, [(i, (i + k) % n) for i in range(n)])


def z_move(value, target):
    pairs = []
    for zl in range(2):
        for zh in range(4):
            to_l, to_h = target(zl, zh)
            pairs.append((zl * 4 + zh, to_l * 4 + to_h % 4))
    return lax.ppermute(value, ("zl", "zh"), pairs)


def across(value):
    return z_move(value, lambda zl, zh: (0, zh + 1) if zl else (1, zh - 1))


def beside(value):
    return z_move(value, lambda zl, zh: (1 - zl, zh))


def on_device(inputs, segment_ids, qkv_weight, attn_cotangent):
    tokens, features = inputs.shape
    block, cols = qkv_weight.shape
    n = 4
    width = features // n
    half = block // 2
    span = cols // 32
    c = lax.axis_index("c")

    me = lax.axis_index("x")
    sent = [lax.dynamic_slice_in_dim(inputs, lax.rem(me + k, n) * width, width, 1) for k in range(n)]
    own = lax.dynamic_slice_in_dim(qkv_weight, c * half, half, 0)
    a = across(own)
    x2 = shift(sent[2], "x", 2)
    x1 = shift(sent[1], "x", 1)
    x3 = shift(sent[3], "x", 3)
    a2 = shift(a, "c", 1)
    b = beside(a)
    b2 = shift(b, "c", 1)
    d = across(b)
    d2 = shift(d, "c", 1)
    xs = (sent[0], x1, x2, x3)
    weights = (qkv_weight, a, a2, b, b2, d, d2)

    flops = 2 * n * tokens * width * cols
    parts = pl.pallas_call(
        forward_kernel,
        out_shape=arr((n, tokens, cols)),
        scratch_shapes=[pltpu.VMEM((n * tokens, cols), F32)],
        compiler_params=PARAMS,
        cost_estimate=cost(flops, 6 << 20),
        name="forward",
    )(*xs, *weights)
    parts = lax.all_to_all(parts, "x", 0, 0, tiled=True)

    grads = pl.pallas_call(
        attention_kernel,
        out_shape=arr((tokens, cols)),
        compiler_params=PARAMS,
        cost_estimate=cost(1 << 28, 1 << 20),
        name="attention",
    )(parts, segment_ids, attn_cotangent)
    grads = lax.all_gather(grads, "x", axis=0, tiled=False)

    mine, other = pl.pallas_call(
        weight_kernel,
        out_shape=[arr((64, span, block), F32), arr((64, span, block))],
        compiler_params=PARAMS,
        cost_estimate=cost(flops, 8 << 20),
        name="weight_grad",
    )(grads, *xs)
    got = shift(other, "c", 1)

    back = pl.pallas_call(
        input_kernel,
        out_shape=[arr((tokens, width))] * n,
        compiler_params=PARAMS,
        cost_estimate=cost(flops, 6 << 20),
        name="input_grad",
    )(grads, *weights)
    home = [back[0]] + [shift(back[k], "x", n - k) for k in (2, 1, 3)]

    summed = pl.pallas_call(
        add_kernel,
        out_shape=arr((64, span, block)),
        compiler_params=PARAMS,
        cost_estimate=cost(1 << 20, 8 << 20),
        name="add_cores",
    )(mine, got)
    pieces = lax.all_to_all(summed, ("zl", "y", "zh"), 0, 0, tiled=True)
    weight_grad = pl.pallas_call(
        total_kernel,
        out_shape=arr((span, block), F32),
        compiler_params=PARAMS,
        cost_estimate=cost(1 << 20, 2 << 20),
        name="add_replicas",
    )(pieces).T

    input_grad = pl.pallas_call(
        join_kernel,
        out_shape=arr((tokens, features)),
        compiler_params=PARAMS,
        cost_estimate=cost(1 << 20, 4 << 20),
        name="join_features",
    )(home[0], home[2], home[1], home[3])
    return (input_grad, weight_grad)


def solution(mesh):
    outer, inner = ("zl", "y", "c"), ("x", "zh")
    fine = Mesh(mesh.devices.reshape(2, 8, 2, 4, 4), outer + inner)
    return jax.shard_map(
        on_device,
        mesh=fine,
        in_specs=(
            P(outer + inner, None),
            P(outer + inner, None),
            P(inner, None),
            P(outer + inner, None),
        ),
        out_specs=(P(outer + inner, None), P(inner, outer)),
        check_vma=False,
    )
```

time: 377 us -> 157 us (0.42)
  starting transfers between devices: 183 us -> 54.3 us
  Pallas kernels: 138 us -> 11.4 us
  blocking collectives: 0 us -> 34.3 us
  waiting for transfers between devices: 50.1 us -> 44.8 us
  local copies, waits for them, and re-layouts: 2.97 us -> 7.8 us
    pallas_call x7 -> x5, Pallas kernels: 135 us -> 8.08 us  [the longest x1 2.47 us: on_device(): pl.pallas_call(weight_kernel, out_shape=[arr((64, span, block), F32), arr...]
    ppermute x30 -> x10, starting transfers between devices: 113 us -> 27.4 us  [shift(): return lax.ppermute(value, axis, [(i, (i + k) % n) for i in range(n)])]
    ppermute x17 -> x3, starting transfers between devices: 70.4 us -> 17.4 us  [z_move(): return lax.ppermute(value, ('zl', 'zh'), pairs)]
    all_to_all x0 -> x1, blocking collectives: none -> 20.2 us  [on_device(): parts = lax.all_to_all(parts, 'x', 0, 0, tiled=True)]
    all_gather x0 -> x1, blocking collectives: none -> 14.1 us  [on_device(): grads = lax.all_gather(grads, 'x', axis=0, tiled=False)]
    all_to_all x0 -> x1, starting transfers between devices: none -> 9.48 us  [on_device(): pieces = lax.all_to_all(summed, ('zl', 'y', 'zh'), 0, 0, tiled=True)]
    ppermute x17 -> x3, waiting for transfers between devices: 21.1 us -> 14.8 us  [z_move(): return lax.ppermute(value, ('zl', 'zh'), pairs)]
    ppermute x30 -> x10, waiting for transfers between devices: 29 us -> 28.2 us  [shift(): return lax.ppermute(value, axis, [(i, (i + k) % n) for i in range(n)])]
  transfers between devices with their start and end apart: 47 -> 14, of which waited for: 16 -> 9; matrix products, arithmetic and copies ran while one was open for 0% -> 1% of each run, Pallas kernels for 35% -> 2%
where the time goes in v2:
time: 157 us; the launch traced here: 154 us
  starting transfers between devices  54.3 us (35%)
  waiting for transfers between devices  44.8 us (29%)
  blocking collectives  34.3 us (22%)
  Pallas kernels  11.4 us (7%)
  local copies, waits for them, and re-layouts  7.8 us (5%)
    ppermute x10, waiting for transfers between devices, shift(): return lax.ppermute(value, axis, [(i, (i + k) % n) for i in range(n)])  28.2 us
    ppermute x10, starting transfers between devices, shift(): return lax.ppermute(value, axis, [(i, (i + k) % n) for i in range(n)])  27.4 us
    all_to_all x1, blocking collectives, on_device(): parts = lax.all_to_all(parts, 'x', 0, 0, tiled=True)  20.2 us
    ppermute x3, starting transfers between devices, z_move(): return lax.ppermute(value, ('zl', 'zh'), pairs)  17.4 us
    ppermute x3, waiting for transfers between devices, z_move(): return lax.ppermute(value, ('zl', 'zh'), pairs)  14.8 us
    all_gather x1, blocking collectives, on_device(): grads = lax.all_gather(grads, 'x', axis=0, tiled=False)  14.1 us
    all_to_all x1, starting transfers between devices, on_device(): pieces = lax.all_to_all(summed, ('zl', 'y', 'zh'), 0, 0, tiled=True)  9.48 us
    unnamed x26, local copies, waits for them, and re-layouts  5.01 us
  transfers between devices with their start and end apart: 14, of which 9 were waited for; matrix products, arithmetic and copies ran while one was open for 1% of the time, Pallas kernels for 2%

profile of v2, /device:TPU:6, one launch (start us, length us, event | category | flops | bytes accessed | tf_op | source)
XLA Modules:
  0.0 153.6 jit_solution(5800535745905128605)
XLA Ops:
  0.6 1.0 constant_dynamic-slice_fusion
  1.7 10.9 %collective-permute-start.3 = (bf16[256,768]{1,0:T(8,128)(2,1)S(1)}, bf16[256,768]{1,0:T(8,128)(2,1)S(1)}, u32[]{:S(2)}, u32[]{:S(2)}) collective-permute-start(bf16[256,768]{1,0:T(8,128)(2,1)S(1)} %constant_dynamic-slice_fusion), channel_id=1, source_target_pairs={{0,259},{1,256},{2,257},{3,258},{256,1},{257,2},{258,3},{259,0},{4... | collective-permute-start | bytes 1179656 | tf_op jit(solution)/shard_map/ppermute | solution.py:164
  12.6 0.0 copy-start
  12.7 9.1 %collective-permute-done.3.a = bf16[256,768]{1,0:T(8,128)(2,1)S(1)} collective-permute-done((bf16[256,768]{1,0:T(8,128)(2,1)S(1)}, bf16[256,768]{1,0:T(8,128)(2,1)S(1)}, u32[]{:S(2)}, u32[]{:S(2)}) %collective-permute-start.3) | collective-permute-done | bytes 393248 | tf_op jit(solution)/shard_map/ppermute | solution.py:164
  21.7 1.9 %collective-permute-start.5 = (bf16[256,768]{1,0:T(8,128)(2,1)S(1)}, bf16[256,768]{1,0:T(8,128)(2,1)S(1)}, u32[]{:S(2)}, u32[]{:S(2)}) collective-permute-start(bf16[256,768]{1,0:T(8,128)(2,1)S(1)} %collective-permute-done.3.a), channel_id=1, source_target_pairs={{0,256},{1,257},{2,258},{3,259},{256,0},{257,1},{258,2},{259,3},{4... | collective-permute-start | bytes 1179656 | tf_op jit(solution)/shard_map/ppermute | solution.py:164
  23.6 1.8 %constant_dynamic-slice_fusion.1 = (bf16[128,2048]{1,0:T(8,128)(2,1)S(1)}, bf16[128,2048]{1,0:T(8,128)(2,1)S(1)}, bf16[128,2048]{1,0:T(8,128)(2,1)S(1)}, bf16[128,2048]{1,0:T(8,128)(2,1)S(1)}) fusion(bf16[128,8192]{1,0:T(8,128)(2,1)} %param.4, s32[]{:T(128)S(6)} %select_n.18, s32[]{:T(128)S(6)} %select_n.16, s32[]{:T(128)S(6)} %select_n.15, s32[]{:T(128)S(6)} %select_n.17), kind=kLoop, calls=%fused_computation.1 | loop fusion | bytes 4194320 | tf_op jit(solution)/shard_map/dynamic_slice | solution.py:185
  25.4 2.7 %collective-permute-start.2 = (bf16[128,2048]{1,0:T(8,128)(2,1)S(1)}, bf16[128,2048]{1,0:T(8,128)(2,1)S(1)}, u32[]{:S(2)}, u32[]{:S(2)}) collective-permute-start(bf16[128,2048]{1,0:T(8,128)(2,1)S(1)} %get-tuple-element.14), channel_id=1, source_target_pairs={{0,12},{4,0},{8,4},{12,8},{1,13},{5,1},{9,5},{13,9},{2,14},{6,2},{... | collective-permute-start | bytes 1572872 | tf_op jit(solution)/shard_map/ppermute | solution.py:155
  28.2 5.7 %collective-permute-done.5.b = bf16[256,768]{1,0:T(8,128)(2,1)S(1)} collective-permute-done((bf16[256,768]{1,0:T(8,128)(2,1)S(1)}, bf16[256,768]{1,0:T(8,128)(2,1)S(1)}, u32[]{:S(2)}, u32[]{:S(2)}) %collective-permute-start.5) | collective-permute-done | bytes 393248 | tf_op jit(solution)/shard_map/ppermute | solution.py:164
  33.9 0.0 copy-start.1
  33.9 4.5 %collective-permute-start.7 = (bf16[256,768]{1,0:T(8,128)(2,1)S(1)}, bf16[256,768]{1,0:T(8,128)(2,1)S(1)}, u32[]{:S(2)}, u32[]{:S(2)}) collective-permute-start(bf16[256,768]{1,0:T(8,128)(2,1)S(1)} %collective-permute-done.5.b), channel_id=1, source_target_pairs={{0,259},{1,256},{2,257},{3,258},{256,1},{257,2},{258,3},{259,0},{4... | collective-permute-start | bytes 1179656 | tf_op jit(solution)/shard_map/ppermute | solution.py:164
  38.4 2.4 %collective-permute-start = (bf16[128,2048]{1,0:T(8,128)(2,1)S(1)}, bf16[128,2048]{1,0:T(8,128)(2,1)S(1)}, u32[]{:S(2)}, u32[]{:S(2)}) collective-permute-start(bf16[128,2048]{1,0:T(8,128)(2,1)S(1)} %get-tuple-element.15), channel_id=1, source_target_pairs={{0,4},{4,8},{8,12},{12,0},{1,5},{5,9},{9,13},{13,1},{2,6},{6,10},{... | collective-permute-start | bytes 1572872 | tf_op jit(solution)/shard_map/ppermute | solution.py:155
  40.8 4.3 %collective-permute-start.1 = (bf16[128,2048]{1,0:T(8,128)(2,1)S(1)}, bf16[128,2048]{1,0:T(8,128)(2,1)S(1)}, u32[]{:S(2)}, u32[]{:S(2)}) collective-permute-start(bf16[128,2048]{1,0:T(8,128)(2,1)S(1)} %get-tuple-element.17), channel_id=1, source_target_pairs={{0,8},{4,12},{8,0},{12,4},{1,9},{5,13},{9,1},{13,5},{2,10},{6,14},... | collective-permute-start | bytes 1572872 | tf_op jit(solution)/shard_map/ppermute | solution.py:155
  45.2 1.9 %collective-permute-start.4 = (bf16[256,768]{1,0:T(8,128)(2,1)S(1)}, bf16[256,768]{1,0:T(8,128)(2,1)S(1)}, u32[]{:S(2)}, u32[]{:S(2)}) collective-permute-start(bf16[256,768]{1,0:T(8,128)(2,1)S(1)} %collective-permute-done.3.a), channel_id=1, source_target_pairs={{0,16},{16,0},{1,17},{17,1},{2,18},{18,2},{3,19},{19,3},{4,20},{20... | collective-permute-start | bytes 1179656 | tf_op jit(solution)/shard_map/ppermute | solution.py:155
  47.1 0.0 collective-permute-done.2.x3
  47.1 2.4 %collective-permute-start.6 = (bf16[256,768]{1,0:T(8,128)(2,1)S(1)}, bf16[256,768]{1,0:T(8,128)(2,1)S(1)}, u32[]{:S(2)}, u32[]{:S(2)}) collective-permute-start(bf16[256,768]{1,0:T(8,128)(2,1)S(1)} %collective-permute-done.5.b), channel_id=1, source_target_pairs={{0,16},{16,0},{1,17},{17,1},{2,18},{18,2},{3,19},{19,3},{4,20},{20... | collective-permute-start | bytes 1179656 | tf_op jit(solution)/shard_map/ppermute | solution.py:155
  49.5 0.0 collective-permute-done.7.d
  49.5 0.0 copy-start.3
  49.5 1.9 %collective-permute-start.8 = (bf16[256,768]{1,0:T(8,128)(2,1)S(1)}, bf16[256,768]{1,0:T(8,128)(2,1)S(1)}, u32[]{:S(2)}, u32[]{:S(2)}) collective-permute-start(bf16[256,768]{1,0:T(8,128)(2,1)S(1)} %collective-permute-done.7.d), channel_id=1, source_target_pairs={{0,16},{16,0},{1,17},{17,1},{2,18},{18,2},{3,19},{19,3},{4,20},{20... | collective-permute-start | bytes 1179656 | tf_op jit(solution)/shard_map/ppermute | solution.py:155
  51.5 3.7 %collective-permute-done.x1 = bf16[128,2048]{1,0:T(8,128)(2,1)S(1)} collective-permute-done((bf16[128,2048]{1,0:T(8,128)(2,1)S(1)}, bf16[128,2048]{1,0:T(8,128)(2,1)S(1)}, u32[]{:S(2)}, u32[]{:S(2)}) %collective-permute-start) | collective-permute-done | bytes 524320 | tf_op jit(solution)/shard_map/ppermute | solution.py:155
  55.2 0.3 collective-permute-done.1.x2
  55.5 0.0 collective-permute-done.4.a2
  55.5 0.0 copy-start.5
  55.5 0.0 collective-permute-done.6.b2
  55.5 0.0 copy-start.7
  55.6 0.0 collective-permute-done.8.d2
  55.6 0.0 copy-start.9
  55.6 0.0 copy-done
  55.6 0.0 copy-start.11
  55.6 0.0 copy-start.12
  55.6 1.8 %forward.1 = bf16[4,128,768]{2,1,0:T(8,128)(2,1)S(1)} custom-call(bf16[128,2048]{1,0:T(8,128)(2,1)S(1)} %get-tuple-element.16.x0, bf16[128,2048]{1,0:T(8,128)(2,1)S(1)} %collective-permute-done.x1, bf16[128,2048]{1,0:T(8,128)(2,1)S(1)} %collective-permute-done.1.x2, bf16[128,2048]{1,0:T(8,128)(2,1)S(1)} %collective-permute-done.2.x3, ...), custom_call_target="tpu_custom_call" | custom-call | flops 1610612736 | bytes 6291456 | tf_op jit(solution)/shard_map/forward/pallas_call | solution.py:200
  57.4 0.0 copy-done.1
  57.4 0.0 copy-done.3
  57.5 0.0 copy-done.5
  57.5 0.0 copy-done.7
  57.5 0.0 copy-done.9
  57.5 20.2 %all_to_all.10.parts = bf16[4,128,768]{2,1,0:T(8,128)(2,1)S(1)} all-to-all(bf16[4,128,768]{2,1,0:T(8,128)(2,1)S(1)} %forward.1), channel_id=1, replica_groups=mesh['zl'=2,'y'=8,'c'=2,'x'=4,'zh'=4] {'x'}, dimensions={0} | all-to-all | bytes 1572864 | tf_op jit(solution)/shard_map/all_to_all | solution.py:208
  77.7 0.0 copy-done.11
  77.7 0.0 copy-done.12
  77.7 1.5 attention.1
  79.2 14.1 %all-gather = bf16[512,768]{1,0:T(8,128)(2,1)S(1)} all-gather(bf16[128,768]{1,0:T(8,128)(2,1)S(1)} %attention.1), channel_id=2, replica_groups=mesh['zl'=2,'y'=8,'c'=2,'x'=4,'zh'=4] {'x'}, dimensions={0}, use_global_device_ids=true | all-gather | bytes 983040 | tf_op jit(solution)/shard_map/all_gather | solution.py:217
  93.3 2.5 %weight_grad.1 = (f32[64,24,512]{2,1,0:T(8,128)S(1)}, bf16[64,24,512]{2,1,0:T(8,128)(2,1)S(1)}) custom-call(bf16[4,128,768]{2,1,0:T(8,128)(2,1)S(1)} %bitcast.2, bf16[128,2048]{1,0:T(8,128)(2,1)S(1)} %get-tuple-element.16.x0, bf16[128,2048]{1,0:T(8,128)(2,1)S(1)} %collective-permute-done.x1, bf16[128,2048]{1,0:T(8,128)(2,1)S(1)} %collective-permute-done.1.x2, ...), custom_call_target="tpu_custom_call" | custom-call | flops 1610612736 | bytes 8388608 | tf_op jit(solution)/shard_map/weight_grad/pallas_call | solution.py:219
  95.8 1.9 %collective-permute-start.12 = (bf16[64,24,512]{2,1,0:T(8,128)(2,1)S(1)}, bf16[64,24,512]{2,1,0:T(8,128)(2,1)S(1)}, u32[]{:S(2)}, u32[]{:S(2)}) collective-permute-start(bf16[64,24,512]{2,1,0:T(8,128)(2,1)S(1)} %get-tuple-element.13), channel_id=1, source_target_pairs={{0,16},{16,0},{1,17},{17,1},{2,18},{18,2},{3,19},{19,3},{4,20},{20... | collective-permute-start | bytes 4718600 | tf_op jit(solution)/shard_map/ppermute | solution.py:155
  97.7 3.4 %collective-permute-done.12.got = bf16[64,24,512]{2,1,0:T(8,128)(2,1)S(1)} collective-permute-done((bf16[64,24,512]{2,1,0:T(8,128)(2,1)S(1)}, bf16[64,24,512]{2,1,0:T(8,128)(2,1)S(1)}, u32[]{:S(2)}, u32[]{:S(2)}) %collective-permute-start.12) | collective-permute-done | bytes 1572896 | tf_op jit(solution)/shard_map/ppermute | solution.py:155
  101.1 1.5 add_cores.1
  102.6 9.5 %all-to-all-start.1 = ((bf16[64,24,512]{2,1,0:T(8,128)(2,1)}), bf16[64,24,512]{2,1,0:T(8,128)(2,1)S(1)}, u32[]{:S(2)}, u32[]{:S(2)}) async-start(bf16[64,24,512]{2,1,0:T(8,128)(2,1)} %add_cores.1), calls=%async_computation.1 | async-start | bytes 3145728 | tf_op jit(solution)/shard_map/all_to_all | solution.py:244
  112.0 0.0 copy-start.2
  112.1 1.0 copy-done.2
  113.0 0.0 copy-start.4
  113.0 1.0 copy-done.4
  114.0 0.0 copy-start.6
  114.0 1.0 copy-done.6
  115.0 0.0 copy-start.8
  115.0 1.0 copy-done.8
  116.0 1.0 copy-done.10
  117.0 1.8 %input_grad.1 = (bf16[128,2048]{1,0:T(8,128)(2,1)S(1)}, bf16[128,2048]{1,0:T(8,128)(2,1)S(1)}, bf16[128,2048]{1,0:T(8,128)(2,1)S(1)}, bf16[128,2048]{1,0:T(8,128)(2,1)S(1)}) custom-call(bf16[4,128,768]{2,1,0:T(8,128)(2,1)S(1)} %bitcast.3, bf16[512,768]{1,0:T(8,128)(2,1)S(1)} %copy-done, bf16[256,768]{1,0:T(8,128)(2,1)S(1)} %collective-permute-done.3.a, ...), custom_call_target="tpu_custom_call" | custom-call | flops 1610612736 | bytes 6291456 | tf_op jit(solution)/shard_map/input_grad/pallas_call | solution.py:228
  118.9 2.8 %collective-permute-start.9 = (bf16[128,2048]{1,0:T(8,128)(2,1)S(1)}, bf16[128,2048]{1,0:T(8,128)(2,1)S(1)}, u32[]{:S(2)}, u32[]{:S(2)}) collective-permute-start(bf16[128,2048]{1,0:T(8,128)(2,1)S(1)} %get-tuple-element.9), channel_id=1, source_target_pairs={{0,12},{4,0},{8,4},{12,8},{1,13},{5,1},{9,5},{13,9},{2,14},{6,2},{... | collective-permute-start | bytes 1572872 | tf_op jit(solution)/shard_map/ppermute | solution.py:155
  121.7 4.6 %collective-permute-start.10 = (bf16[128,2048]{1,0:T(8,128)(2,1)S(1)}, bf16[128,2048]{1,0:T(8,128)(2,1)S(1)}, u32[]{:S(2)}, u32[]{:S(2)}) collective-permute-start(bf16[128,2048]{1,0:T(8,128)(2,1)S(1)} %get-tuple-element.10), channel_id=1, source_target_pairs={{0,8},{4,12},{8,0},{12,4},{1,9},{5,13},{9,1},{13,5},{2,10},{6,14},... | collective-permute-start | bytes 1572872 | tf_op jit(solution)/shard_map/ppermute | solution.py:155
  126.3 2.4 %collective-permute-start.11 = (bf16[128,2048]{1,0:T(8,128)(2,1)S(1)}, bf16[128,2048]{1,0:T(8,128)(2,1)S(1)}, u32[]{:S(2)}, u32[]{:S(2)}) collective-permute-start(bf16[128,2048]{1,0:T(8,128)(2,1)S(1)} %get-tuple-element.11), channel_id=1, source_target_pairs={{0,4},{4,8},{8,12},{12,0},{1,5},{5,9},{9,13},{13,1},{2,6},{6,10},{... | collective-permute-start | bytes 1572872 | tf_op jit(solution)/shard_map/ppermute | solution.py:155
  128.7 7.8 %collective-permute-done.9.refs_1_ = bf16[128,2048]{1,0:T(8,128)(2,1)S(1)} collective-permute-done((bf16[128,2048]{1,0:T(8,128)(2,1)S(1)}, bf16[128,2048]{1,0:T(8,128)(2,1)S(1)}, u32[]{:S(2)}, u32[]{:S(2)}) %collective-permute-start.9) | collective-permute-done | bytes 524320 | tf_op jit(solution)/shard_map/ppermute | solution.py:155
  136.5 10.7 %collective-permute-done.10.refs_2_ = bf16[128,2048]{1,0:T(8,128)(2,1)S(1)} collective-permute-done((bf16[128,2048]{1,0:T(8,128)(2,1)S(1)}, bf16[128,2048]{1,0:T(8,128)(2,1)S(1)}, u32[]{:S(2)}, u32[]{:S(2)}) %collective-permute-start.10) | collective-permute-done | bytes 524320 | tf_op jit(solution)/shard_map/ppermute | solution.py:155
  147.2 2.2 %collective-permute-done.11.refs_3_ = bf16[128,2048]{1,0:T(8,128)(2,1)S(1)} collective-permute-done((bf16[128,2048]{1,0:T(8,128)(2,1)S(1)}, bf16[128,2048]{1,0:T(8,128)(2,1)S(1)}, u32[]{:S(2)}, u32[]{:S(2)}) %collective-permute-start.11) | collective-permute-done | bytes 524320 | tf_op jit(solution)/shard_map/ppermute | solution.py:155
  149.4 1.5 join_features.1
  150.9 1.8 %all-to-all-done.1.ref = bf16[64,24,512]{2,1,0:T(8,128)(2,1)S(1)} async-done(((bf16[64,24,512]{2,1,0:T(8,128)(2,1)}), bf16[64,24,512]{2,1,0:T(8,128)(2,1)S(1)}, u32[]{:S(2)}, u32[]{:S(2)}) %all-to-all-start.1) | async-done | bytes 1572896 | tf_op jit(solution)/shard_map/all_to_all | solution.py:244
  152.8 0.9 add_replicas.1
  (1 shorter events, 0.0 us)
Async XLA Ops:
  1.7 20.1 %collective-permute-start.3 = (bf16[256,768]{1,0:T(8,128)(2,1)S(1)}, bf16[256,768]{1,0:T(8,128)(2,1)S(1)}, u32[]{:S(2)}, u32[]{:S(2)}) collective-permute-start(bf16[256,768]{1,0:T(8,128)(2,1)S(1)} %constant_dynamic-slice_fusion), channel_id=1, source_target_pairs={{0,259},{1,256},{2,257},{3,258},{256,1},{257,2},{258,3},{259,0},{4... | collective-permute-start | bytes 1179656 | tf_op jit(solution)/shard_map/ppermute | solution.py:164
  12.6 42.9 %copy-start = (bf16[512,768]{1,0:T(8,128)(2,1)S(1)}, bf16[512,768]{1,0:T(8,128)(2,1)}, u32[]{:S(2)}) copy-start(bf16[512,768]{1,0:T(8,128)(2,1)} %w0.3) | copy-start | bytes 2359300
  21.7 12.2 %collective-permute-start.5 = (bf16[256,768]{1,0:T(8,128)(2,1)S(1)}, bf16[256,768]{1,0:T(8,128)(2,1)S(1)}, u32[]{:S(2)}, u32[]{:S(2)}) collective-permute-start(bf16[256,768]{1,0:T(8,128)(2,1)S(1)} %collective-permute-done.3.a), channel_id=1, source_target_pairs={{0,256},{1,257},{2,258},{3,259},{256,0},{257,1},{258,2},{259,3},{4... | collective-permute-start | bytes 1179656 | tf_op jit(solution)/shard_map/ppermute | solution.py:164
  25.4 21.7 %collective-permute-start.2 = (bf16[128,2048]{1,0:T(8,128)(2,1)S(1)}, bf16[128,2048]{1,0:T(8,128)(2,1)S(1)}, u32[]{:S(2)}, u32[]{:S(2)}) collective-permute-start(bf16[128,2048]{1,0:T(8,128)(2,1)S(1)} %get-tuple-element.14), channel_id=1, source_target_pairs={{0,12},{4,0},{8,4},{12,8},{1,13},{5,1},{9,5},{13,9},{2,14},{6,2},{... | collective-permute-start | bytes 1572872 | tf_op jit(solution)/shard_map/ppermute | solution.py:155
  33.9 23.5 %copy-start.1 = (bf16[256,768]{1,0:T(8,128)(2,1)}, bf16[256,768]{1,0:T(8,128)(2,1)S(1)}, u32[]{:S(2)}) copy-start(bf16[256,768]{1,0:T(8,128)(2,1)S(1)} %collective-permute-done.5.b) | copy-start | bytes 1179652
  33.9 15.6 %collective-permute-start.7 = (bf16[256,768]{1,0:T(8,128)(2,1)S(1)}, bf16[256,768]{1,0:T(8,128)(2,1)S(1)}, u32[]{:S(2)}, u32[]{:S(2)}) collective-permute-start(bf16[256,768]{1,0:T(8,128)(2,1)S(1)} %collective-permute-done.5.b), channel_id=1, source_target_pairs={{0,259},{1,256},{2,257},{3,258},{256,1},{257,2},{258,3},{259,0},{4... | collective-permute-start | bytes 1179656 | tf_op jit(solution)/shard_map/ppermute | solution.py:164
  38.4 16.8 %collective-permute-start = (bf16[128,2048]{1,0:T(8,128)(2,1)S(1)}, bf16[128,2048]{1,0:T(8,128)(2,1)S(1)}, u32[]{:S(2)}, u32[]{:S(2)}) collective-permute-start(bf16[128,2048]{1,0:T(8,128)(2,1)S(1)} %get-tuple-element.15), channel_id=1, source_target_pairs={{0,4},{4,8},{8,12},{12,0},{1,5},{5,9},{9,13},{13,1},{2,6},{6,10},{... | collective-permute-start | bytes 1572872 | tf_op jit(solution)/shard_map/ppermute | solution.py:155
  40.8 14.7 %collective-permute-start.1 = (bf16[128,2048]{1,0:T(8,128)(2,1)S(1)}, bf16[128,2048]{1,0:T(8,128)(2,1)S(1)}, u32[]{:S(2)}, u32[]{:S(2)}) collective-permute-start(bf16[128,2048]{1,0:T(8,128)(2,1)S(1)} %get-tuple-element.17), channel_id=1, source_target_pairs={{0,8},{4,12},{8,0},{12,4},{1,9},{5,13},{9,1},{13,5},{2,10},{6,14},... | collective-permute-start | bytes 1572872 | tf_op jit(solution)/shard_map/ppermute | solution.py:155
  45.2 10.4 %collective-permute-start.4 = (bf16[256,768]{1,0:T(8,128)(2,1)S(1)}, bf16[256,768]{1,0:T(8,128)(2,1)S(1)}, u32[]{:S(2)}, u32[]{:S(2)}) collective-permute-start(bf16[256,768]{1,0:T(8,128)(2,1)S(1)} %collective-permute-done.3.a), channel_id=1, source_target_pairs={{0,16},{16,0},{1,17},{17,1},{2,18},{18,2},{3,19},{19,3},{4,20},{20... | collective-permute-start | bytes 1179656 | tf_op jit(solution)/shard_map/ppermute | solution.py:155
  47.1 8.4 %collective-permute-start.6 = (bf16[256,768]{1,0:T(8,128)(2,1)S(1)}, bf16[256,768]{1,0:T(8,128)(2,1)S(1)}, u32[]{:S(2)}, u32[]{:S(2)}) collective-permute-start(bf16[256,768]{1,0:T(8,128)(2,1)S(1)} %collective-permute-done.5.b), channel_id=1, source_target_pairs={{0,16},{16,0},{1,17},{17,1},{2,18},{18,2},{3,19},{19,3},{4,20},{20... | collective-permute-start | bytes 1179656 | tf_op jit(solution)/shard_map/ppermute | solution.py:155
  49.5 7.9 %copy-start.3 = (bf16[256,768]{1,0:T(8,128)(2,1)}, bf16[256,768]{1,0:T(8,128)(2,1)S(1)}, u32[]{:S(2)}) copy-start(bf16[256,768]{1,0:T(8,128)(2,1)S(1)} %collective-permute-done.7.d) | copy-start | bytes 1179652
  49.5 6.0 %collective-permute-start.8 = (bf16[256,768]{1,0:T(8,128)(2,1)S(1)}, bf16[256,768]{1,0:T(8,128)(2,1)S(1)}, u32[]{:S(2)}, u32[]{:S(2)}) collective-permute-start(bf16[256,768]{1,0:T(8,128)(2,1)S(1)} %collective-permute-done.7.d), channel_id=1, source_target_pairs={{0,16},{16,0},{1,17},{17,1},{2,18},{18,2},{3,19},{19,3},{4,20},{20... | collective-permute-start | bytes 1179656 | tf_op jit(solution)/shard_map/ppermute | solution.py:155
  55.5 1.9 %copy-start.5 = (bf16[256,768]{1,0:T(8,128)(2,1)}, bf16[256,768]{1,0:T(8,128)(2,1)S(1)}, u32[]{:S(2)}) copy-start(bf16[256,768]{1,0:T(8,128)(2,1)S(1)} %collective-permute-done.4.a2) | copy-start | bytes 1179652
  55.5 1.9 %copy-start.7 = (bf16[256,768]{1,0:T(8,128)(2,1)}, bf16[256,768]{1,0:T(8,128)(2,1)S(1)}, u32[]{:S(2)}) copy-start(bf16[256,768]{1,0:T(8,128)(2,1)S(1)} %collective-permute-done.6.b2) | copy-start | bytes 1179652
  55.6 1.9 %copy-start.9 = (bf16[256,768]{1,0:T(8,128)(2,1)}, bf16[256,768]{1,0:T(8,128)(2,1)S(1)}, u32[]{:S(2)}) copy-start(bf16[256,768]{1,0:T(8,128)(2,1)S(1)} %collective-permute-done.8.d2) | copy-start | bytes 1179652
  55.6 22.1 %copy-start.11 = (bf16[128,512]{1,0:T(8,128)(2,1)S(1)}, bf16[128,512]{1,0:T(8,128)(2,1)}, u32[]{:S(2)}) copy-start(bf16[128,512]{1,0:T(8,128)(2,1)} %cot_ref.1) | copy-start | bytes 393220
  55.6 22.1 %copy-start.12 = (s32[1,128]{1,0:T(1,128)S(1)}, s32[1,128]{1,0:T(1,128)}, u32[]{:S(2)}) copy-start(s32[1,128]{1,0:T(1,128)} %seg_ref.1) | copy-start | bytes 1540
  95.8 5.3 %collective-permute-start.12 = (bf16[64,24,512]{2,1,0:T(8,128)(2,1)S(1)}, bf16[64,24,512]{2,1,0:T(8,128)(2,1)S(1)}, u32[]{:S(2)}, u32[]{:S(2)}) collective-permute-start(bf16[64,24,512]{2,1,0:T(8,128)(2,1)S(1)} %get-tuple-element.13), channel_id=1, source_target_pairs={{0,16},{16,0},{1,17},{17,1},{2,18},{18,2},{3,19},{19,3},{4,20},{20... | collective-permute-start | bytes 4718600 | tf_op jit(solution)/shard_map/ppermute | solution.py:155
  102.6 50.2 %all-to-all-start.1 = ((bf16[64,24,512]{2,1,0:T(8,128)(2,1)}), bf16[64,24,512]{2,1,0:T(8,128)(2,1)S(1)}, u32[]{:S(2)}, u32[]{:S(2)}) async-start(bf16[64,24,512]{2,1,0:T(8,128)(2,1)} %add_cores.1), calls=%async_computation.1 | async-start | bytes 3145728 | tf_op jit(solution)/shard_map/all_to_all | solution.py:244
  112.0 1.0 copy-start.2
  113.0 1.0 copy-start.4
  114.0 1.0 copy-start.6
  115.0 1.0 copy-start.8
  116.0 1.0 copy-start.10
  118.9 17.6 %collective-permute-start.9 = (bf16[128,2048]{1,0:T(8,128)(2,1)S(1)}, bf16[128,2048]{1,0:T(8,128)(2,1)S(1)}, u32[]{:S(2)}, u32[]{:S(2)}) collective-permute-start(bf16[128,2048]{1,0:T(8,128)(2,1)S(1)} %get-tuple-element.9), channel_id=1, source_target_pairs={{0,12},{4,0},{8,4},{12,8},{1,13},{5,1},{9,5},{13,9},{2,14},{6,2},{... | collective-permute-start | bytes 1572872 | tf_op jit(solution)/shard_map/ppermute | solution.py:155
  121.7 25.5 %collective-permute-start.10 = (bf16[128,2048]{1,0:T(8,128)(2,1)S(1)}, bf16[128,2048]{1,0:T(8,128)(2,1)S(1)}, u32[]{:S(2)}, u32[]{:S(2)}) collective-permute-start(bf16[128,2048]{1,0:T(8,128)(2,1)S(1)} %get-tuple-element.10), channel_id=1, source_target_pairs={{0,8},{4,12},{8,0},{12,4},{1,9},{5,13},{9,1},{13,5},{2,10},{6,14},... | collective-permute-start | bytes 1572872 | tf_op jit(solution)/shard_map/ppermute | solution.py:155
  126.3 23.2 %collective-permute-start.11 = (bf16[128,2048]{1,0:T(8,128)(2,1)S(1)}, bf16[128,2048]{1,0:T(8,128)(2,1)S(1)}, u32[]{:S(2)}, u32[]{:S(2)}) collective-permute-start(bf16[128,2048]{1,0:T(8,128)(2,1)S(1)} %get-tuple-element.11), channel_id=1, source_target_pairs={{0,4},{4,8},{8,12},{12,0},{1,5},{5,9},{9,13},{13,1},{2,6},{6,10},{... | collective-permute-start | bytes 1572872 | tf_op jit(solution)/shard_map/ppermute | solution.py:155

commit v3 on v2

--- a/solution.py
+++ b/solution.py
@@ -11,7 +11,7 @@
 HD = 128
 BF16 = jnp.bfloat16
 F32 = jnp.float32
-PARAMS = pltpu.CompilerParams(vmem_limit_bytes=40 * 1024 * 1024)
+PARAMS = pltpu.CompilerParams(vmem_limit_bytes=20 * 1024 * 1024)
 
 NT = (((1,), (1,)), ((), ()))
 TN = (((0,), (0,)), ((), ()))
@@ -51,20 +51,19 @@
     return [pl.multiple_of(p, rows) for p in places]
 
 
-def forward_kernel(x0, x1, x2, x3, w0, a, a2, b, b2, d, d2, parts, acc):
+def forward_kernel(x0, x1, x2, x3, w0, a, a2, b, b2, d, d2, parts, whole, acc):
     rows = a.shape[0]
-    places = piece_places(rows)
-    xs = (x0, x1, x2, x3)
     tokens = x0.shape[0]
-    for i, (place, w) in enumerate(zip(places, (w0, a, a2, b, b2, d, d2))):
+    me = lax.axis_index("x")
+    for i, (place, w) in enumerate(zip(piece_places(rows), (w0, a, a2, b, b2, d, d2))):
         depth = w.shape[0]
-        x = jnp.concatenate([r[:, pl.ds(place, depth)] for r in xs], axis=0)
+        x = jnp.concatenate([r[:, pl.ds(place, depth)] for r in (x0, x1, x2, x3)], axis=0)
+        whole[pl.ds(place, depth), :] = w[...]
         term = dot(x, w[...])
         if i == 0:
             acc[...] = term
         else:
             acc[...] += term
-    me = lax.axis_index("x")
     for k in range(4):
         parts[lax.rem(me + 4 - k, 4)] = acc[k * tokens : (k + 1) * tokens, :].astype(BF16)
 
@@ -101,49 +100,47 @@
     out[:, (heads + 1) * HD :] = grad_v.astype(BF16)
 
 
-def relative(gathered):
-    me = lax.axis_index("x")
-    return jnp.concatenate([gathered[lax.rem(me + 4 - k, 4)] for k in range(4)], axis=0)
-
-
-def weight_kernel(g, x0, x1, x2, x3, mine, other):
-    pieces, span, block = mine.shape
-    groups = pieces // 4
-    c = lax.axis_index("c")
-    grads = relative(g)
-    shape = (groups * span, grads.shape[1])
-    place = lax.broadcasted_iota(jnp.int32, shape, 0)
-    source = lax.broadcasted_iota(jnp.int32, shape, 1)
-    left = []
-    for core in (c, 1 - c):
-        wanted = (place // span * 2 + core) * span + place % span
-        pick = jnp.where(source == wanted, 1.0, 0.0).astype(BF16)
-        left.append(dot(pick, grads, NT).astype(BF16))
+def relative(g):
+    n = g.shape[0]
+    me = lax.axis_index("x")
+    return jnp.concatenate([g[lax.rem(me + n - k, n)] for k in range(n)], axis=0)
+
+
+def weight_terms(g, xs, core, shape):
+    pieces, span, block = shape
+    cols = g.shape[2]
+    place = lax.broadcasted_iota(jnp.int32, (cols // 2, cols), 0)
+    source = lax.broadcasted_iota(jnp.int32, (cols // 2, cols), 1)
+    wanted = (place // span * 2 + core) * span + place % span
+    pick = jnp.where(source == wanted, 1.0, 0.0).astype(BF16)
+    left = dot(pick, relative(g), NT).astype(BF16)
     tile = 256
     for zh in range(4):
         for at in range(0, block, tile):
             start = zh * block + at
-            x = jnp.concatenate([r[:, start : start + tile] for r in (x0, x1, x2, x3)], axis=0)
-            for out, rows in ((other, left[1]), (mine, left[0])):
-                term = dot(rows, x)
-                for k in range(groups):
-                    out[k * 4 + zh, :, at : at + tile] = term[k * span : (k + 1) * span].astype(out.dtype)
-
-
-def input_kernel(g, w0, a, a2, b, b2, d, d2, o0, o1, o2, o3):
-    rows = a.shape[0]
-    tokens = g.shape[1]
-    places = piece_places(rows)
+            term = dot(left, jnp.concatenate([r[:, start : start + tile] for r in xs], axis=0))
+            for k in range(pieces // 4):
+                yield (k * 4 + zh, slice(None), slice(at, at + tile)), term[k * span : (k + 1) * span]
+
+
+def other_kernel(g, x0, x1, x2, x3, out):
+    for at, piece in weight_terms(g, (x0, x1, x2, x3), 1 - lax.axis_index("c"), out.shape):
+        out[at] = piece.astype(BF16)
+
+
+def mine_kernel(g, x0, x1, x2, x3, got, out):
+    for at, piece in weight_terms(g, (x0, x1, x2, x3), lax.axis_index("c"), out.shape):
+        out[at] = (piece + got[at].astype(F32)).astype(BF16)
+
+
+def input_kernel(g, whole, *outs):
+    n, tokens, _ = g.shape
     grads = relative(g)
-    for place, w in zip(places, (w0, a, a2, b, b2, d, d2)):
-        depth = w.shape[0]
-        term = dot(grads, w[...], NT).astype(BF16)
-        for k, o in enumerate((o0, o1, o2, o3)):
-            o[:, pl.ds(place, depth)] = term[k * tokens : (k + 1) * tokens]
-
-
-def add_kernel(mine, got, out):
-    out[...] = (mine[...] + got[...].astype(F32)).astype(BF16)
+    tile = 256
+    for at in range(0, whole.shape[0], tile):
+        term = dot(grads, whole[at : at + tile, :], NT).astype(BF16)
+        for k, out in enumerate(outs):
+            out[:, at : at + tile] = term[k * tokens : (k + 1) * tokens]
 
 
 def total_kernel(ref, out):
@@ -153,6 +150,10 @@
 def shift(value, axis, k):
     n = lax.axis_size(axis)
     return lax.ppermute(value, axis, [(i, (i + k) % n) for i in range(n)])
+
+
+def swap(value, axes):
+    return lax.all_to_all(value, axes, 0, 0, tiled=True)
 
 
 def z_move(value, target):
@@ -185,11 +186,12 @@
     sent = [lax.dynamic_slice_in_dim(inputs, lax.rem(me + k, n) * width, width, 1) for k in range(n)]
     own = lax.dynamic_slice_in_dim(qkv_weight, c * half, half, 0)
     a = across(own)
-    x2 = shift(sent[2], "x", 2)
     x1 = shift(sent[1], "x", 1)
     x3 = shift(sent[3], "x", 3)
+    x2 = shift(sent[2], "x", 2)
     a2 = shift(a, "c", 1)
     b = beside(a)
+    b, x1, x3 = lax.optimization_barrier((b, x1, x3))
     b2 = shift(b, "c", 1)
     d = across(b)
     d2 = shift(d, "c", 1)
@@ -197,15 +199,15 @@
     weights = (qkv_weight, a, a2, b, b2, d, d2)
 
     flops = 2 * n * tokens * width * cols
-    parts = pl.pallas_call(
+    parts, whole = pl.pallas_call(
         forward_kernel,
-        out_shape=arr((n, tokens, cols)),
+        out_shape=[arr((n, tokens, cols)), arr((width, cols))],
         scratch_shapes=[pltpu.VMEM((n * tokens, cols), F32)],
         compiler_params=PARAMS,
         cost_estimate=cost(flops, 6 << 20),
         name="forward",
     )(*xs, *weights)
-    parts = lax.all_to_all(parts, "x", 0, 0, tiled=True)
+    parts = swap(parts, "x")
 
     grads = pl.pallas_call(
         attention_kernel,
@@ -216,12 +218,13 @@
     )(parts, segment_ids, attn_cotangent)
     grads = lax.all_gather(grads, "x", axis=0, tiled=False)
 
-    mine, other = pl.pallas_call(
-        weight_kernel,
-        out_shape=[arr((64, span, block), F32), arr((64, span, block))],
-        compiler_params=PARAMS,
-        cost_estimate=cost(flops, 8 << 20),
-        name="weight_grad",
+    share = arr((64, span, block))
+    other = pl.pallas_call(
+        other_kernel,
+        out_shape=share,
+        compiler_params=PARAMS,
+        cost_estimate=cost(flops // 2, 4 << 20),
+        name="weight_grad_other_core",
     )(grads, *xs)
     got = shift(other, "c", 1)
 
@@ -231,17 +234,18 @@
         compiler_params=PARAMS,
         cost_estimate=cost(flops, 6 << 20),
         name="input_grad",
-    )(grads, *weights)
-    home = [back[0]] + [shift(back[k], "x", n - k) for k in (2, 1, 3)]
+    )(grads, whole)
+    got, back = lax.optimization_barrier((got, back))
+    home = [back[0]] + [shift(back[k], "x", n - k) for k in range(1, n)]
 
     summed = pl.pallas_call(
-        add_kernel,
-        out_shape=arr((64, span, block)),
-        compiler_params=PARAMS,
-        cost_estimate=cost(1 << 20, 8 << 20),
-        name="add_cores",
-    )(mine, got)
-    pieces = lax.all_to_all(summed, ("zl", "y", "zh"), 0, 0, tiled=True)
+        mine_kernel,
+        out_shape=share,
+        compiler_params=PARAMS,
+        cost_estimate=cost(flops // 2, 6 << 20),
+        name="weight_grad_this_core",
+    )(grads, *xs, got)
+    pieces = swap(summed, ("zl", "y", "zh"))
     weight_grad = pl.pallas_call(
         total_kernel,
         out_shape=arr((span, block), F32),
@@ -256,7 +260,7 @@
         compiler_params=PARAMS,
         cost_estimate=cost(1 << 20, 4 << 20),
         name="join_features",
-    )(home[0], home[2], home[1], home[3])
+    )(*home)
     return (input_grad, weight_grad)
 
 

time: 157 us -> 146 us (0.930)
  blocking collectives: 34.3 us -> 25.9 us
  local copies, waits for them, and re-layouts: 7.8 us -> 3.62 us
  waiting for transfers between devices: 44.8 us -> 47.2 us
    ppermute x3, waiting for transfers between devices: 14.8 us -> 2.53 us  [z_move(): return lax.ppermute(value, ('zl', 'zh'), pairs)]
    all_to_all x1, blocking collectives: 20.2 us -> 12 us  [swap(): return lax.all_to_all(value, axes, 0, 0, tiled=True)]
    ppermute x10, waiting for transfers between devices: 28.2 us -> 36 us  [shift(): return lax.ppermute(value, axis, [(i, (i + k) % n) for i in range(n)])]
    all_to_all x1, waiting for transfers between devices: 1.84 us -> 8.68 us  [swap(): return lax.all_to_all(value, axes, 0, 0, tiled=True)]
    unnamed x26 -> x8, local copies, waits for them, and re-layouts: 5.01 us -> 0.81 us
  transfers between devices with their start and end apart: 14 -> 14, of which waited for: 9 -> 11; matrix products, arithmetic and copies ran while one was open for 1% -> 1% of each run, Pallas kernels for 2% -> 2%
where the time goes in v3:
time: 146 us; the launch traced here: 143 us
  starting transfers between devices  53.8 us (37%)
  waiting for transfers between devices  47.2 us (32%)
  blocking collectives  25.9 us (18%)
  Pallas kernels  11.5 us (8%)
  local copies, waits for them, and re-layouts  3.62 us (2%)
    ppermute x10, waiting for transfers between devices, shift(): return lax.ppermute(value, axis, [(i, (i + k) % n) for i in range(n)])  36 us
    ppermute x10, starting transfers between devices, shift(): return lax.ppermute(value, axis, [(i, (i + k) % n) for i in range(n)])  27.1 us
    ppermute x3, starting transfers between devices, z_move(): return lax.ppermute(value, ('zl', 'zh'), pairs)  17.4 us
    all_gather x1, blocking collectives, on_device(): grads = lax.all_gather(grads, 'x', axis=0, tiled=False)  13.9 us
    all_to_all x1, blocking collectives, swap(): return lax.all_to_all(value, axes, 0, 0, tiled=True)  12 us
    all_to_all x1, starting transfers between devices, swap(): return lax.all_to_all(value, axes, 0, 0, tiled=True)  9.29 us
    all_to_all x1, waiting for transfers between devices, swap(): return lax.all_to_all(value, axes, 0, 0, tiled=True)  8.68 us
  transfers between devices with their start and end apart: 14, of which 11 were waited for; matrix products, arithmetic and copies ran while one was open for 1% of the time, Pallas kernels for 2%

profile of v3, /device:TPU:6, one launch (start us, length us, event | category | flops | bytes accessed | tf_op | source)
XLA Modules:
  0.0 143.0 jit_solution(3695322989090850100)
XLA Ops:
  0.6 1.0 constant_dynamic-slice_fusion.3
  1.7 10.9 %collective-permute-start = (bf16[256,768]{1,0:T(8,128)(2,1)S(1)}, bf16[256,768]{1,0:T(8,128)(2,1)S(1)}, u32[]{:S(2)}, u32[]{:S(2)}) collective-permute-start(bf16[256,768]{1,0:T(8,128)(2,1)S(1)} %constant_dynamic-slice_fusion.3), channel_id=1, source_target_pairs={{0,259},{1,256},{2,257},{3,258},{256,1},{257,2},{258,3},{259,0},{4... | collective-permute-start | bytes 1179656 | tf_op jit(solution)/shard_map/ppermute | solution.py:165
  12.6 0.0 copy-start
  12.7 1.8 %constant_dynamic-slice_fusion = (bf16[128,2048]{1,0:T(8,128)(2,1)S(1)}, bf16[128,2048]{1,0:T(8,128)(2,1)S(1)}, bf16[128,2048]{1,0:T(8,128)(2,1)S(1)}, bf16[128,2048]{1,0:T(8,128)(2,1)S(1)}) fusion(bf16[128,8192]{1,0:T(8,128)(2,1)} %param.4, s32[]{:T(128)S(6)} %select_n.19, s32[]{:T(128)S(6)} %select_n.17, s32[]{:T(128)S(6)} %select_n.15, s32[]{:T(128)S(6)} %select_n.18), kind=kLoop, calls=%fused_computation | loop fusion | bytes 4194320 | tf_op jit(solution)/shard_map/dynamic_slice | solution.py:186
  14.5 2.4 %collective-permute-start.2 = (bf16[128,2048]{1,0:T(8,128)(2,1)S(1)}, bf16[128,2048]{1,0:T(8,128)(2,1)S(1)}, u32[]{:S(2)}, u32[]{:S(2)}) collective-permute-start(bf16[128,2048]{1,0:T(8,128)(2,1)S(1)} %get-tuple-element.31), channel_id=1, source_target_pairs={{0,4},{4,8},{8,12},{12,0},{1,5},{5,9},{9,13},{13,1},{2,6},{6,10},{... | collective-permute-start | bytes 1572872 | tf_op jit(solution)/shard_map/ppermute | solution.py:152
  16.8 3.5 %collective-permute-start.3 = (bf16[128,2048]{1,0:T(8,128)(2,1)S(1)}, bf16[128,2048]{1,0:T(8,128)(2,1)S(1)}, u32[]{:S(2)}, u32[]{:S(2)}) collective-permute-start(bf16[128,2048]{1,0:T(8,128)(2,1)S(1)} %get-tuple-element.33), channel_id=1, source_target_pairs={{0,12},{4,0},{8,4},{12,8},{1,13},{5,1},{9,5},{13,9},{2,14},{6,2},{... | collective-permute-start | bytes 1572872 | tf_op jit(solution)/shard_map/ppermute | solution.py:152
  20.3 1.4 collective-permute-done.a
  21.7 1.9 %collective-permute-start.1 = (bf16[256,768]{1,0:T(8,128)(2,1)S(1)}, bf16[256,768]{1,0:T(8,128)(2,1)S(1)}, u32[]{:S(2)}, u32[]{:S(2)}) collective-permute-start(bf16[256,768]{1,0:T(8,128)(2,1)S(1)} %collective-permute-done.a), channel_id=1, source_target_pairs={{0,256},{1,257},{2,258},{3,259},{256,0},{257,1},{258,2},{259,3},{4... | collective-permute-start | bytes 1179656 | tf_op jit(solution)/shard_map/ppermute | solution.py:165
  23.6 6.1 %collective-permute-done.2.x1 = bf16[128,2048]{1,0:T(8,128)(2,1)S(1)} collective-permute-done((bf16[128,2048]{1,0:T(8,128)(2,1)S(1)}, bf16[128,2048]{1,0:T(8,128)(2,1)S(1)}, u32[]{:S(2)}, u32[]{:S(2)}) %collective-permute-start.2) | collective-permute-done | bytes 524320 | tf_op jit(solution)/shard_map/ppermute | solution.py:152
  29.7 3.3 %collective-permute-done.3.x3 = bf16[128,2048]{1,0:T(8,128)(2,1)S(1)} collective-permute-done((bf16[128,2048]{1,0:T(8,128)(2,1)S(1)}, bf16[128,2048]{1,0:T(8,128)(2,1)S(1)}, u32[]{:S(2)}, u32[]{:S(2)}) %collective-permute-start.3) | collective-permute-done | bytes 524320 | tf_op jit(solution)/shard_map/ppermute | solution.py:152
  33.1 0.8 collective-permute-done.1.b
  33.9 4.5 %collective-permute-start.7 = (bf16[256,768]{1,0:T(8,128)(2,1)S(1)}, bf16[256,768]{1,0:T(8,128)(2,1)S(1)}, u32[]{:S(2)}, u32[]{:S(2)}) collective-permute-start(bf16[256,768]{1,0:T(8,128)(2,1)S(1)} %collective-permute-done.1.b), channel_id=1, source_target_pairs={{0,259},{1,256},{2,257},{3,258},{256,1},{257,2},{258,3},{259,0},{4... | collective-permute-start | bytes 1179656 | tf_op jit(solution)/shard_map/ppermute | solution.py:165
  38.4 3.3 %collective-permute-start.4 = (bf16[128,2048]{1,0:T(8,128)(2,1)S(1)}, bf16[128,2048]{1,0:T(8,128)(2,1)S(1)}, u32[]{:S(2)}, u32[]{:S(2)}) collective-permute-start(bf16[128,2048]{1,0:T(8,128)(2,1)S(1)} %get-tuple-element.30), channel_id=1, source_target_pairs={{0,8},{4,12},{8,0},{12,4},{1,9},{5,13},{9,1},{13,5},{2,10},{6,14},... | collective-permute-start | bytes 1572872 | tf_op jit(solution)/shard_map/ppermute | solution.py:152
  41.8 1.9 %collective-permute-start.5 = (bf16[256,768]{1,0:T(8,128)(2,1)S(1)}, bf16[256,768]{1,0:T(8,128)(2,1)S(1)}, u32[]{:S(2)}, u32[]{:S(2)}) collective-permute-start(bf16[256,768]{1,0:T(8,128)(2,1)S(1)} %collective-permute-done.a), channel_id=1, source_target_pairs={{0,16},{16,0},{1,17},{17,1},{2,18},{18,2},{3,19},{19,3},{4,20},{20... | collective-permute-start | bytes 1179656 | tf_op jit(solution)/shard_map/ppermute | solution.py:152
  43.7 2.4 %collective-permute-start.6 = (bf16[256,768]{1,0:T(8,128)(2,1)S(1)}, bf16[256,768]{1,0:T(8,128)(2,1)S(1)}, u32[]{:S(2)}, u32[]{:S(2)}) collective-permute-start(bf16[256,768]{1,0:T(8,128)(2,1)S(1)} %collective-permute-done.1.b), channel_id=1, source_target_pairs={{0,16},{16,0},{1,17},{17,1},{2,18},{18,2},{3,19},{19,3},{4,20},{20... | collective-permute-start | bytes 1179656 | tf_op jit(solution)/shard_map/ppermute | solution.py:152
  46.1 0.3 collective-permute-done.7.d
  46.4 1.9 %collective-permute-start.8 = (bf16[256,768]{1,0:T(8,128)(2,1)S(1)}, bf16[256,768]{1,0:T(8,128)(2,1)S(1)}, u32[]{:S(2)}, u32[]{:S(2)}) collective-permute-start(bf16[256,768]{1,0:T(8,128)(2,1)S(1)} %collective-permute-done.7.d), channel_id=1, source_target_pairs={{0,16},{16,0},{1,17},{17,1},{2,18},{18,2},{3,19},{19,3},{4,20},{20... | collective-permute-start | bytes 1179656 | tf_op jit(solution)/shard_map/ppermute | solution.py:152
  48.3 5.1 %collective-permute-done.4.x2 = bf16[128,2048]{1,0:T(8,128)(2,1)S(1)} collective-permute-done((bf16[128,2048]{1,0:T(8,128)(2,1)S(1)}, bf16[128,2048]{1,0:T(8,128)(2,1)S(1)}, u32[]{:S(2)}, u32[]{:S(2)}) %collective-permute-start.4) | collective-permute-done | bytes 524320 | tf_op jit(solution)/shard_map/ppermute | solution.py:152
  53.4 0.0 collective-permute-done.5.a2
  53.4 0.0 collective-permute-done.6.b2
  53.4 0.0 collective-permute-done.8.d2
  53.4 0.0 copy-done
  53.4 0.0 copy-start.1
  53.5 0.0 copy-start.2
  53.5 1.9 %forward.1 = (bf16[4,128,768]{2,1,0:T(8,128)(2,1)S(1)}, bf16[2048,768]{1,0:T(8,128)(2,1)S(1)}) custom-call(bf16[128,2048]{1,0:T(8,128)(2,1)S(1)} %get-tuple-element.32.x0, bf16[128,2048]{1,0:T(8,128)(2,1)S(1)} %collective-permute-done.2.x1, bf16[128,2048]{1,0:T(8,128)(2,1)S(1)} %collective-permute-done.4.x2, ...), custom_call_target="tpu_custom_call" | custom-call | flops 1610612736 | bytes 6291456 | tf_op jit(solution)/shard_map/forward/pallas_call | solution.py:202
  55.4 12.0 %all_to_all.10.parts = bf16[4,128,768]{2,1,0:T(8,128)(2,1)S(1)} all-to-all(bf16[4,128,768]{2,1,0:T(8,128)(2,1)S(1)} %get-tuple-element.19), channel_id=1, replica_groups=mesh['zl'=2,'y'=8,'c'=2,'x'=4,'zh'=4] {'x'}, dimensions={0} | all-to-all | bytes 1572864 | tf_op jit(solution)/shard_map/all_to_all | solution.py:156
  67.4 0.0 copy-done.1
  67.4 0.0 copy-done.2
  67.4 1.5 %attention.1 = bf16[128,768]{1,0:T(8,128)(2,1)S(1)} custom-call(bf16[4,128,768]{2,1,0:T(8,128)(2,1)S(1)} %all_to_all.10.parts, s32[1,128]{1,0:T(1,128)S(1)} %copy-done.2, bf16[128,512]{1,0:T(8,128)(2,1)S(1)} %copy-done.1), custom_call_target="tpu_custom_call" | custom-call | flops 268435456 | bytes 1048576 | tf_op jit(solution)/shard_map/attention/pallas_call | solution.py:212
  68.9 13.9 %all-gather = bf16[512,768]{1,0:T(8,128)(2,1)S(1)} all-gather(bf16[128,768]{1,0:T(8,128)(2,1)S(1)} %attention.1), channel_id=2, replica_groups=mesh['zl'=2,'y'=8,'c'=2,'x'=4,'zh'=4] {'x'}, dimensions={0}, use_global_device_ids=true | all-gather | bytes 983040 | tf_op jit(solution)/shard_map/all_gather | solution.py:219
  82.8 1.4 weight_grad_other_core.1
  84.2 1.9 %collective-permute-start.9 = (bf16[64,24,512]{2,1,0:T(8,128)(2,1)S(1)}, bf16[64,24,512]{2,1,0:T(8,128)(2,1)S(1)}, u32[]{:S(2)}, u32[]{:S(2)}) collective-permute-start(bf16[64,24,512]{2,1,0:T(8,128)(2,1)S(1)} %weight_grad_other_core.1), channel_id=1, source_target_pairs={{0,16},{16,0},{1,17},{17,1},{2,18},{18,2},{3,19},{19,3},{4,20},{20... | collective-permute-start | bytes 4718600 | tf_op jit(solution)/shard_map/ppermute | solution.py:152
  86.2 1.8 %input_grad.1 = (bf16[128,2048]{1,0:T(8,128)(2,1)S(1)}, bf16[128,2048]{1,0:T(8,128)(2,1)S(1)}, bf16[128,2048]{1,0:T(8,128)(2,1)S(1)}, bf16[128,2048]{1,0:T(8,128)(2,1)S(1)}) custom-call(bf16[4,128,768]{2,1,0:T(8,128)(2,1)S(1)} %bitcast.3, bf16[2048,768]{1,0:T(8,128)(2,1)S(1)} %get-tuple-element.20.whole), custom_call_target="tpu_custom_call" | custom-call | flops 1610612736 | bytes 6291456 | tf_op jit(solution)/shard_map/input_grad/pallas_call | solution.py:231
  88.0 0.0 copy-start.3
  88.0 0.8 copy-done.3
  88.8 0.7 collective-permute-done.9.got
  89.5 2.6 %weight_grad_this_core.1 = bf16[64,24,512]{2,1,0:T(8,128)(2,1)} custom-call(bf16[4,128,768]{2,1,0:T(8,128)(2,1)S(1)} %bitcast.4, bf16[128,2048]{1,0:T(8,128)(2,1)S(1)} %get-tuple-element.32.x0, bf16[128,2048]{1,0:T(8,128)(2,1)S(1)} %collective-permute-done.2.x1, bf16[128,2048]{1,0:T(8,128)(2,1)S(1)} %collective-permute-done.4.x2, ...), custom_call_target="tpu_custom_call" | custom-call | flops 805306368 | bytes 6291456 | tf_op jit(solution)/shard_map/weight_grad_this_core/pallas_call | solution.py:241
  92.1 9.3 %all-to-all-start.1 = ((bf16[64,24,512]{2,1,0:T(8,128)(2,1)}), bf16[64,24,512]{2,1,0:T(8,128)(2,1)S(1)}, u32[]{:S(2)}, u32[]{:S(2)}) async-start(bf16[64,24,512]{2,1,0:T(8,128)(2,1)} %weight_grad_this_core.1), calls=%async_computation.1 | async-start | bytes 3145728 | tf_op jit(solution)/shard_map/all_to_all | solution.py:156
  101.4 2.8 %collective-permute-start.10 = (bf16[128,2048]{1,0:T(8,128)(2,1)}, bf16[128,2048]{1,0:T(8,128)(2,1)S(1)}, u32[]{:S(2)}, u32[]{:S(2)}) collective-permute-start(bf16[128,2048]{1,0:T(8,128)(2,1)} %copy-done.3), channel_id=1, source_target_pairs={{0,12},{4,0},{8,4},{12,8},{1,13},{5,1},{9,5},{13,9},{2,14},{6,2},{... | collective-permute-start | bytes 1572872 | tf_op jit(solution)/shard_map/ppermute | solution.py:152
  104.2 4.6 %collective-permute-start.11 = (bf16[128,2048]{1,0:T(8,128)(2,1)S(1)}, bf16[128,2048]{1,0:T(8,128)(2,1)S(1)}, u32[]{:S(2)}, u32[]{:S(2)}) collective-permute-start(bf16[128,2048]{1,0:T(8,128)(2,1)S(1)} %get-tuple-element.27), channel_id=1, source_target_pairs={{0,8},{4,12},{8,0},{12,4},{1,9},{5,13},{9,1},{13,5},{2,10},{6,14},... | collective-permute-start | bytes 1572872 | tf_op jit(solution)/shard_map/ppermute | solution.py:152
  108.8 2.5 %collective-permute-start.12 = (bf16[128,2048]{1,0:T(8,128)(2,1)S(1)}, bf16[128,2048]{1,0:T(8,128)(2,1)S(1)}, u32[]{:S(2)}, u32[]{:S(2)}) collective-permute-start(bf16[128,2048]{1,0:T(8,128)(2,1)S(1)} %get-tuple-element.28), channel_id=1, source_target_pairs={{0,4},{4,8},{8,12},{12,0},{1,5},{5,9},{9,13},{13,1},{2,6},{6,10},{... | collective-permute-start | bytes 1572872 | tf_op jit(solution)/shard_map/ppermute | solution.py:152
  111.2 8.0 %collective-permute-done.10.refs_1_ = bf16[128,2048]{1,0:T(8,128)(2,1)S(1)} collective-permute-done((bf16[128,2048]{1,0:T(8,128)(2,1)}, bf16[128,2048]{1,0:T(8,128)(2,1)S(1)}, u32[]{:S(2)}, u32[]{:S(2)}) %collective-permute-start.10) | collective-permute-done | bytes 524320 | tf_op jit(solution)/shard_map/ppermute | solution.py:152
  119.2 10.7 %collective-permute-done.11.refs_2_ = bf16[128,2048]{1,0:T(8,128)(2,1)S(1)} collective-permute-done((bf16[128,2048]{1,0:T(8,128)(2,1)S(1)}, bf16[128,2048]{1,0:T(8,128)(2,1)S(1)}, u32[]{:S(2)}, u32[]{:S(2)}) %collective-permute-start.11) | collective-permute-done | bytes 524320 | tf_op jit(solution)/shard_map/ppermute | solution.py:152
  129.9 2.0 %collective-permute-done.12.refs_3_ = bf16[128,2048]{1,0:T(8,128)(2,1)S(1)} collective-permute-done((bf16[128,2048]{1,0:T(8,128)(2,1)S(1)}, bf16[128,2048]{1,0:T(8,128)(2,1)S(1)}, u32[]{:S(2)}, u32[]{:S(2)}) %collective-permute-start.12) | collective-permute-done | bytes 524320 | tf_op jit(solution)/shard_map/ppermute | solution.py:152
  132.0 1.5 %join_features.1 = bf16[128,8192]{1,0:T(8,128)(2,1)} custom-call(bf16[128,2048]{1,0:T(8,128)(2,1)S(1)} %get-tuple-element.25.refs_0_, bf16[128,2048]{1,0:T(8,128)(2,1)S(1)} %collective-permute-done.10.refs_1_, bf16[128,2048]{1,0:T(8,128)(2,1)S(1)} %collective-permute-done.11.refs_2_, bf16[128,2048]{1,0:T(8,128)(2,1)S(1)} %collective-permute-done.12.refs_3_), custom_call_target="tpu_custom_call" | custom-call | flops 1048576 | bytes 4194304 | tf_op jit(solution)/shard_map/join_features/pallas_call | solution.py:257
  133.4 8.7 %all-to-all-done.1.ref = bf16[64,24,512]{2,1,0:T(8,128)(2,1)S(1)} async-done(((bf16[64,24,512]{2,1,0:T(8,128)(2,1)}), bf16[64,24,512]{2,1,0:T(8,128)(2,1)S(1)}, u32[]{:S(2)}, u32[]{:S(2)}) %all-to-all-start.1) | async-done | bytes 1572896 | tf_op jit(solution)/shard_map/all_to_all | solution.py:156
  142.1 0.9 add_replicas.1
Async XLA Ops:
  1.7 20.1 %collective-permute-start = (bf16[256,768]{1,0:T(8,128)(2,1)S(1)}, bf16[256,768]{1,0:T(8,128)(2,1)S(1)}, u32[]{:S(2)}, u32[]{:S(2)}) collective-permute-start(bf16[256,768]{1,0:T(8,128)(2,1)S(1)} %constant_dynamic-slice_fusion.3), channel_id=1, source_target_pairs={{0,259},{1,256},{2,257},{3,258},{256,1},{257,2},{258,3},{259,0},{4... | collective-permute-start | bytes 1179656 | tf_op jit(solution)/shard_map/ppermute | solution.py:165
  12.6 40.8 %copy-start = (bf16[512,768]{1,0:T(8,128)(2,1)S(1)}, bf16[512,768]{1,0:T(8,128)(2,1)}, u32[]{:S(2)}) copy-start(bf16[512,768]{1,0:T(8,128)(2,1)} %w0.1) | copy-start | bytes 2359300
  14.5 15.3 %collective-permute-start.2 = (bf16[128,2048]{1,0:T(8,128)(2,1)S(1)}, bf16[128,2048]{1,0:T(8,128)(2,1)S(1)}, u32[]{:S(2)}, u32[]{:S(2)}) collective-permute-start(bf16[128,2048]{1,0:T(8,128)(2,1)S(1)} %get-tuple-element.31), channel_id=1, source_target_pairs={{0,4},{4,8},{8,12},{12,0},{1,5},{5,9},{9,13},{13,1},{2,6},{6,10},{... | collective-permute-start | bytes 1572872 | tf_op jit(solution)/shard_map/ppermute | solution.py:152
  16.8 16.2 %collective-permute-start.3 = (bf16[128,2048]{1,0:T(8,128)(2,1)S(1)}, bf16[128,2048]{1,0:T(8,128)(2,1)S(1)}, u32[]{:S(2)}, u32[]{:S(2)}) collective-permute-start(bf16[128,2048]{1,0:T(8,128)(2,1)S(1)} %get-tuple-element.33), channel_id=1, source_target_pairs={{0,12},{4,0},{8,4},{12,8},{1,13},{5,1},{9,5},{13,9},{2,14},{6,2},{... | collective-permute-start | bytes 1572872 | tf_op jit(solution)/shard_map/ppermute | solution.py:152
  21.7 12.2 %collective-permute-start.1 = (bf16[256,768]{1,0:T(8,128)(2,1)S(1)}, bf16[256,768]{1,0:T(8,128)(2,1)S(1)}, u32[]{:S(2)}, u32[]{:S(2)}) collective-permute-start(bf16[256,768]{1,0:T(8,128)(2,1)S(1)} %collective-permute-done.a), channel_id=1, source_target_pairs={{0,256},{1,257},{2,258},{3,259},{256,0},{257,1},{258,2},{259,3},{4... | collective-permute-start | bytes 1179656 | tf_op jit(solution)/shard_map/ppermute | solution.py:165
  33.9 12.5 %collective-permute-start.7 = (bf16[256,768]{1,0:T(8,128)(2,1)S(1)}, bf16[256,768]{1,0:T(8,128)(2,1)S(1)}, u32[]{:S(2)}, u32[]{:S(2)}) collective-permute-start(bf16[256,768]{1,0:T(8,128)(2,1)S(1)} %collective-permute-done.1.b), channel_id=1, source_target_pairs={{0,259},{1,256},{2,257},{3,258},{256,1},{257,2},{258,3},{259,0},{4... | collective-permute-start | bytes 1179656 | tf_op jit(solution)/shard_map/ppermute | solution.py:165
  38.4 15.0 %collective-permute-start.4 = (bf16[128,2048]{1,0:T(8,128)(2,1)S(1)}, bf16[128,2048]{1,0:T(8,128)(2,1)S(1)}, u32[]{:S(2)}, u32[]{:S(2)}) collective-permute-start(bf16[128,2048]{1,0:T(8,128)(2,1)S(1)} %get-tuple-element.30), channel_id=1, source_target_pairs={{0,8},{4,12},{8,0},{12,4},{1,9},{5,13},{9,1},{13,5},{2,10},{6,14},... | collective-permute-start | bytes 1572872 | tf_op jit(solution)/shard_map/ppermute | solution.py:152
  41.8 11.7 %collective-permute-start.5 = (bf16[256,768]{1,0:T(8,128)(2,1)S(1)}, bf16[256,768]{1,0:T(8,128)(2,1)S(1)}, u32[]{:S(2)}, u32[]{:S(2)}) collective-permute-start(bf16[256,768]{1,0:T(8,128)(2,1)S(1)} %collective-permute-done.a), channel_id=1, source_target_pairs={{0,16},{16,0},{1,17},{17,1},{2,18},{18,2},{3,19},{19,3},{4,20},{20... | collective-permute-start | bytes 1179656 | tf_op jit(solution)/shard_map/ppermute | solution.py:152
  43.7 9.7 %collective-permute-start.6 = (bf16[256,768]{1,0:T(8,128)(2,1)S(1)}, bf16[256,768]{1,0:T(8,128)(2,1)S(1)}, u32[]{:S(2)}, u32[]{:S(2)}) collective-permute-start(bf16[256,768]{1,0:T(8,128)(2,1)S(1)} %collective-permute-done.1.b), channel_id=1, source_target_pairs={{0,16},{16,0},{1,17},{17,1},{2,18},{18,2},{3,19},{19,3},{4,20},{20... | collective-permute-start | bytes 1179656 | tf_op jit(solution)/shard_map/ppermute | solution.py:152
  46.4 7.1 %collective-permute-start.8 = (bf16[256,768]{1,0:T(8,128)(2,1)S(1)}, bf16[256,768]{1,0:T(8,128)(2,1)S(1)}, u32[]{:S(2)}, u32[]{:S(2)}) collective-permute-start(bf16[256,768]{1,0:T(8,128)(2,1)S(1)} %collective-permute-done.7.d), channel_id=1, source_target_pairs={{0,16},{16,0},{1,17},{17,1},{2,18},{18,2},{3,19},{19,3},{4,20},{20... | collective-permute-start | bytes 1179656 | tf_op jit(solution)/shard_map/ppermute | solution.py:152
  53.4 14.0 %copy-start.1 = (bf16[128,512]{1,0:T(8,128)(2,1)S(1)}, bf16[128,512]{1,0:T(8,128)(2,1)}, u32[]{:S(2)}) copy-start(bf16[128,512]{1,0:T(8,128)(2,1)} %cot_ref.1) | copy-start | bytes 393220
  53.5 14.0 %copy-start.2 = (s32[1,128]{1,0:T(1,128)S(1)}, s32[1,128]{1,0:T(1,128)}, u32[]{:S(2)}) copy-start(s32[1,128]{1,0:T(1,128)} %seg_ref.1) | copy-start | bytes 1540
  84.2 5.3 %collective-permute-start.9 = (bf16[64,24,512]{2,1,0:T(8,128)(2,1)S(1)}, bf16[64,24,512]{2,1,0:T(8,128)(2,1)S(1)}, u32[]{:S(2)}, u32[]{:S(2)}) collective-permute-start(bf16[64,24,512]{2,1,0:T(8,128)(2,1)S(1)} %weight_grad_other_core.1), channel_id=1, source_target_pairs={{0,16},{16,0},{1,17},{17,1},{2,18},{18,2},{3,19},{19,3},{4,20},{20... | collective-permute-start | bytes 4718600 | tf_op jit(solution)/shard_map/ppermute | solution.py:152
  88.0 0.8 copy-start.3
  92.1 50.0 %all-to-all-start.1 = ((bf16[64,24,512]{2,1,0:T(8,128)(2,1)}), bf16[64,24,512]{2,1,0:T(8,128)(2,1)S(1)}, u32[]{:S(2)}, u32[]{:S(2)}) async-start(bf16[64,24,512]{2,1,0:T(8,128)(2,1)} %weight_grad_this_core.1), calls=%async_computation.1 | async-start | bytes 3145728 | tf_op jit(solution)/shard_map/all_to_all | solution.py:156
  101.4 17.8 %collective-permute-start.10 = (bf16[128,2048]{1,0:T(8,128)(2,1)}, bf16[128,2048]{1,0:T(8,128)(2,1)S(1)}, u32[]{:S(2)}, u32[]{:S(2)}) collective-permute-start(bf16[128,2048]{1,0:T(8,128)(2,1)} %copy-done.3), channel_id=1, source_target_pairs={{0,12},{4,0},{8,4},{12,8},{1,13},{5,1},{9,5},{13,9},{2,14},{6,2},{... | collective-permute-start | bytes 1572872 | tf_op jit(solution)/shard_map/ppermute | solution.py:152
  104.2 25.8 %collective-permute-start.11 = (bf16[128,2048]{1,0:T(8,128)(2,1)S(1)}, bf16[128,2048]{1,0:T(8,128)(2,1)S(1)}, u32[]{:S(2)}, u32[]{:S(2)}) collective-permute-start(bf16[128,2048]{1,0:T(8,128)(2,1)S(1)} %get-tuple-element.27), channel_id=1, source_target_pairs={{0,8},{4,12},{8,0},{12,4},{1,9},{5,13},{9,1},{13,5},{2,10},{6,14},... | collective-permute-start | bytes 1572872 | tf_op jit(solution)/shard_map/ppermute | solution.py:152
  108.8 23.2 %collective-permute-start.12 = (bf16[128,2048]{1,0:T(8,128)(2,1)S(1)}, bf16[128,2048]{1,0:T(8,128)(2,1)S(1)}, u32[]{:S(2)}, u32[]{:S(2)}) collective-permute-start(bf16[128,2048]{1,0:T(8,128)(2,1)S(1)} %get-tuple-element.28), channel_id=1, source_target_pairs={{0,4},{4,8},{8,12},{12,0},{1,5},{5,9},{9,13},{13,1},{2,6},{6,10},{... | collective-permute-start | bytes 1572872 | tf_op jit(solution)/shard_map/ppermute | solution.py:152

commit v4 on v3

--- a/solution.py
+++ b/solution.py
@@ -51,21 +51,32 @@
     return [pl.multiple_of(p, rows) for p in places]
 
 
-def forward_kernel(x0, x1, x2, x3, w0, a, a2, b, b2, d, d2, parts, whole, acc):
-    rows = a.shape[0]
+def weight_product(xs, pieces):
+    places = piece_places(pieces[1].shape[0])
+    for place, w in zip(places, pieces):
+        depth = w.shape[0]
+        yield pl.ds(place, depth), dot(jnp.concatenate([x[:, pl.ds(place, depth)] for x in xs], axis=0), w[...])
+
+
+def forward_kernel(x0, x1, x3, w0, a, a2, b, b2, d, d2, parts, whole, acc):
     tokens = x0.shape[0]
-    me = lax.axis_index("x")
-    for i, (place, w) in enumerate(zip(piece_places(rows), (w0, a, a2, b, b2, d, d2))):
-        depth = w.shape[0]
-        x = jnp.concatenate([r[:, pl.ds(place, depth)] for r in (x0, x1, x2, x3)], axis=0)
-        whole[pl.ds(place, depth), :] = w[...]
-        term = dot(x, w[...])
-        if i == 0:
+    pieces = (w0, a, a2, b, b2, d, d2)
+    for w, (rows, term) in zip(pieces, weight_product((x0, x1, x3), pieces)):
+        whole[rows, :] = w[...]
+        if w is w0:
             acc[...] = term
         else:
             acc[...] += term
-    for k in range(4):
-        parts[lax.rem(me + 4 - k, 4)] = acc[k * tokens : (k + 1) * tokens, :].astype(BF16)
+    me = lax.axis_index("x")
+    for i, k in enumerate((0, 1, 3)):
+        parts[lax.rem(me + 4 - k, 4)] = acc[i * tokens : (i + 1) * tokens, :].astype(BF16)
+
+
+def last_forward_kernel(x2, w0, a, a2, b, b2, d, d2, begun, parts):
+    opposite = lax.rem(lax.axis_index("x") + 2, 4)
+    total = sum(term for _, term in weight_product((x2,), (w0, a, a2, b, b2, d, d2)))
+    parts[...] = begun[...]
+    parts[opposite] = total.astype(BF16)
 
 
 def attention_kernel(parts, seg_ref, cot_ref, out):
@@ -169,6 +180,10 @@
     return z_move(value, lambda zl, zh: (0, zh + 1) if zl else (1, zh - 1))
 
 
+def over(value):
+    return z_move(value, lambda zl, zh: (zl, zh - 1 if zl else zh + 1))
+
+
 def beside(value):
     return z_move(value, lambda zl, zh: (1 - zl, zh))
 
@@ -188,25 +203,32 @@
     a = across(own)
     x1 = shift(sent[1], "x", 1)
     x3 = shift(sent[3], "x", 3)
-    x2 = shift(sent[2], "x", 2)
+    x1, x3, opposite = lax.optimization_barrier((x1, x3, sent[2]))
+    x2 = shift(opposite, "x", 2)
     a2 = shift(a, "c", 1)
     b = beside(a)
-    b, x1, x3 = lax.optimization_barrier((b, x1, x3))
     b2 = shift(b, "c", 1)
-    d = across(b)
+    d = over(a)
     d2 = shift(d, "c", 1)
     xs = (sent[0], x1, x2, x3)
     weights = (qkv_weight, a, a2, b, b2, d, d2)
 
     flops = 2 * n * tokens * width * cols
-    parts, whole = pl.pallas_call(
+    begun, whole = pl.pallas_call(
         forward_kernel,
         out_shape=[arr((n, tokens, cols)), arr((width, cols))],
-        scratch_shapes=[pltpu.VMEM((n * tokens, cols), F32)],
-        compiler_params=PARAMS,
-        cost_estimate=cost(flops, 6 << 20),
+        scratch_shapes=[pltpu.VMEM(((n - 1) * tokens, cols), F32)],
+        compiler_params=PARAMS,
+        cost_estimate=cost(flops * 3 // 4, 6 << 20),
         name="forward",
-    )(*xs, *weights)
+    )(sent[0], x1, x3, *weights)
+    parts = pl.pallas_call(
+        last_forward_kernel,
+        out_shape=arr((n, tokens, cols)),
+        compiler_params=PARAMS,
+        cost_estimate=cost(flops // 4, 5 << 20),
+        name="last_forward",
+    )(x2, *weights, begun)
     parts = swap(parts, "x")
 
     grads = pl.pallas_call(

time: 146 us -> 143 us (0.979)
  waiting for transfers between devices: 47.2 us -> 38 us
  blocking collectives: 25.9 us -> 29.2 us
  starting transfers between devices: 53.8 us -> 56.4 us
    ppermute x10, waiting for transfers between devices: 36 us -> 25.4 us  [shift(): return lax.ppermute(value, axis, [(i, (i + k) % n) for i in range(n)])]
    all_to_all x1, blocking collectives: 12 us -> 15.1 us  [swap(): return lax.all_to_all(value, axes, 0, 0, tiled=True)]
    ppermute x10, starting transfers between devices: 27.1 us -> 29.1 us  [shift(): return lax.ppermute(value, axis, [(i, (i + k) % n) for i in range(n)])]
    ppermute x3, starting transfers between devices: 17.4 us -> 19.2 us  [z_move(): return lax.ppermute(value, ('zl', 'zh'), pairs)]
  transfers between devices with their start and end apart: 14 -> 14, of which waited for: 11 -> 10; matrix products, arithmetic and copies ran while one was open for 1% -> 1% of each run, Pallas kernels for 2% -> 3%
where the time goes in v4:
time: 143 us; the launch traced here: 140 us
  starting transfers between devices  56.4 us (39%)
  waiting for transfers between devices  38 us (27%)
  blocking collectives  29.2 us (20%)
  Pallas kernels  11.7 us (8%)
  local copies, waits for them, and re-layouts  3.64 us (3%)
    ppermute x10, starting transfers between devices, shift(): return lax.ppermute(value, axis, [(i, (i + k) % n) for i in range(n)])  29.1 us
    ppermute x10, waiting for transfers between devices, shift(): return lax.ppermute(value, axis, [(i, (i + k) % n) for i in range(n)])  25.4 us
    ppermute x3, starting transfers between devices, z_move(): return lax.ppermute(value, ('zl', 'zh'), pairs)  19.2 us
    all_to_all x1, blocking collectives, swap(): return lax.all_to_all(value, axes, 0, 0, tiled=True)  15.1 us
    all_gather x1, blocking collectives, on_device(): grads = lax.all_gather(grads, 'x', axis=0, tiled=False)  14.1 us
    all_to_all x1, waiting for transfers between devices, swap(): return lax.all_to_all(value, axes, 0, 0, tiled=True)  8.68 us
    all_to_all x1, starting transfers between devices, swap(): return lax.all_to_all(value, axes, 0, 0, tiled=True)  8.14 us
    ppermute x3, waiting for transfers between devices, z_move(): return lax.ppermute(value, ('zl', 'zh'), pairs)  3.96 us
  transfers between devices with their start and end apart: 14, of which 10 were waited for; matrix products, arithmetic and copies ran while one was open for 1% of the time, Pallas kernels for 3%

profile of v4, /device:TPU:6, one launch (start us, length us, event | category | flops | bytes accessed | tf_op | source)
XLA Modules:
  0.0 139.8 jit_solution(17075035138590067348)
XLA Ops:
  0.6 1.0 constant_dynamic-slice_fusion.1
  1.7 10.9 %collective-permute-start.3 = (bf16[256,768]{1,0:T(8,128)(2,1)S(1)}, bf16[256,768]{1,0:T(8,128)(2,1)S(1)}, u32[]{:S(2)}, u32[]{:S(2)}) collective-permute-start(bf16[256,768]{1,0:T(8,128)(2,1)S(1)} %constant_dynamic-slice_fusion.1), channel_id=1, source_target_pairs={{0,259},{1,256},{2,257},{3,258},{256,1},{257,2},{258,3},{259,0},{4... | collective-permute-start | bytes 1179656 | tf_op jit(solution)/shard_map/ppermute | solution.py:176
  12.6 0.0 copy-start
  12.7 1.8 %constant_dynamic-slice_fusion = (bf16[128,2048]{1,0:T(8,128)(2,1)S(1)}, bf16[128,2048]{1,0:T(8,128)(2,1)S(1)}, bf16[128,2048]{1,0:T(8,128)(2,1)S(1)}, bf16[128,2048]{1,0:T(8,128)(2,1)S(1)}) fusion(bf16[128,8192]{1,0:T(8,128)(2,1)} %param.4, s32[]{:T(128)S(6)} %select_n.19, s32[]{:T(128)S(6)} %select_n.16, s32[]{:T(128)S(6)} %select_n.15, s32[]{:T(128)S(6)} %select_n.17), kind=kLoop, calls=%fused_computation | loop fusion | bytes 4194320 | tf_op jit(solution)/shard_map/dynamic_slice | solution.py:201
  14.5 2.7 %collective-permute-start.1 = (bf16[128,2048]{1,0:T(8,128)(2,1)S(1)}, bf16[128,2048]{1,0:T(8,128)(2,1)S(1)}, u32[]{:S(2)}, u32[]{:S(2)}) collective-permute-start(bf16[128,2048]{1,0:T(8,128)(2,1)S(1)} %get-tuple-element.31), channel_id=1, source_target_pairs={{0,12},{4,0},{8,4},{12,8},{1,13},{5,1},{9,5},{13,9},{2,14},{6,2},{... | collective-permute-start | bytes 1572872 | tf_op jit(solution)/shard_map/ppermute | solution.py:163
  17.2 4.3 %collective-permute-start = (bf16[128,2048]{1,0:T(8,128)(2,1)S(1)}, bf16[128,2048]{1,0:T(8,128)(2,1)S(1)}, u32[]{:S(2)}, u32[]{:S(2)}) collective-permute-start(bf16[128,2048]{1,0:T(8,128)(2,1)S(1)} %get-tuple-element.32), channel_id=1, source_target_pairs={{0,4},{4,8},{8,12},{12,0},{1,5},{5,9},{9,13},{13,1},{2,6},{6,10},{... | collective-permute-start | bytes 1572872 | tf_op jit(solution)/shard_map/ppermute | solution.py:163
  21.5 0.2 collective-permute-done.3.a
  21.7 1.9 %collective-permute-start.7 = (bf16[256,768]{1,0:T(8,128)(2,1)S(1)}, bf16[256,768]{1,0:T(8,128)(2,1)S(1)}, u32[]{:S(2)}, u32[]{:S(2)}) collective-permute-start(bf16[256,768]{1,0:T(8,128)(2,1)S(1)} %collective-permute-done.3.a), channel_id=1, source_target_pairs={{0,1},{1,2},{2,3},{3,0},{256,259},{257,256},{258,257},{259,258},{4... | collective-permute-start | bytes 1179656 | tf_op jit(solution)/shard_map/ppermute | solution.py:176
  23.6 6.3 %collective-permute-start.5 = (bf16[256,768]{1,0:T(8,128)(2,1)S(1)}, bf16[256,768]{1,0:T(8,128)(2,1)S(1)}, u32[]{:S(2)}, u32[]{:S(2)}) collective-permute-start(bf16[256,768]{1,0:T(8,128)(2,1)S(1)} %collective-permute-done.3.a), channel_id=1, source_target_pairs={{0,256},{1,257},{2,258},{3,259},{256,0},{257,1},{258,2},{259,3},{4... | collective-permute-start | bytes 1179656 | tf_op jit(solution)/shard_map/ppermute | solution.py:176
  29.9 1.0 collective-permute-done.1.x3
  31.0 1.3 collective-permute-done.x1
  32.2 4.0 %collective-permute-start.2 = (bf16[128,2048]{1,0:T(8,128)(2,1)S(1)}, bf16[128,2048]{1,0:T(8,128)(2,1)S(1)}, u32[]{:S(2)}, u32[]{:S(2)}) collective-permute-start(bf16[128,2048]{1,0:T(8,128)(2,1)S(1)} %get-tuple-element.16), channel_id=1, source_target_pairs={{0,8},{4,12},{8,0},{12,4},{1,9},{5,13},{9,1},{13,5},{2,10},{6,14},... | collective-permute-start | bytes 1572872 | tf_op jit(solution)/shard_map/ppermute | solution.py:163
  36.3 1.9 %collective-permute-start.4 = (bf16[256,768]{1,0:T(8,128)(2,1)S(1)}, bf16[256,768]{1,0:T(8,128)(2,1)S(1)}, u32[]{:S(2)}, u32[]{:S(2)}) collective-permute-start(bf16[256,768]{1,0:T(8,128)(2,1)S(1)} %collective-permute-done.3.a), channel_id=1, source_target_pairs={{0,16},{16,0},{1,17},{17,1},{2,18},{18,2},{3,19},{19,3},{4,20},{20... | collective-permute-start | bytes 1179656 | tf_op jit(solution)/shard_map/ppermute | solution.py:163
  38.2 0.0 collective-permute-done.7.d
  38.2 2.4 %collective-permute-start.8 = (bf16[256,768]{1,0:T(8,128)(2,1)S(1)}, bf16[256,768]{1,0:T(8,128)(2,1)S(1)}, u32[]{:S(2)}, u32[]{:S(2)}) collective-permute-start(bf16[256,768]{1,0:T(8,128)(2,1)S(1)} %collective-permute-done.7.d), channel_id=1, source_target_pairs={{0,16},{16,0},{1,17},{17,1},{2,18},{18,2},{3,19},{19,3},{4,20},{20... | collective-permute-start | bytes 1179656 | tf_op jit(solution)/shard_map/ppermute | solution.py:163
  40.6 3.8 %collective-permute-done.5.b = bf16[256,768]{1,0:T(8,128)(2,1)S(1)} collective-permute-done((bf16[256,768]{1,0:T(8,128)(2,1)S(1)}, bf16[256,768]{1,0:T(8,128)(2,1)S(1)}, u32[]{:S(2)}, u32[]{:S(2)}) %collective-permute-start.5) | collective-permute-done | bytes 393248 | tf_op jit(solution)/shard_map/ppermute | solution.py:176
  44.4 1.9 %collective-permute-start.6 = (bf16[256,768]{1,0:T(8,128)(2,1)S(1)}, bf16[256,768]{1,0:T(8,128)(2,1)S(1)}, u32[]{:S(2)}, u32[]{:S(2)}) collective-permute-start(bf16[256,768]{1,0:T(8,128)(2,1)S(1)} %collective-permute-done.5.b), channel_id=1, source_target_pairs={{0,16},{16,0},{1,17},{17,1},{2,18},{18,2},{3,19},{19,3},{4,20},{20... | collective-permute-start | bytes 1179656 | tf_op jit(solution)/shard_map/ppermute | solution.py:163
  46.3 0.0 collective-permute-done.4.a2
  46.3 0.0 collective-permute-done.8.d2
  46.3 1.7 %collective-permute-done.6.b2 = bf16[256,768]{1,0:T(8,128)(2,1)S(1)} collective-permute-done((bf16[256,768]{1,0:T(8,128)(2,1)S(1)}, bf16[256,768]{1,0:T(8,128)(2,1)S(1)}, u32[]{:S(2)}, u32[]{:S(2)}) %collective-permute-start.6) | collective-permute-done | bytes 393248 | tf_op jit(solution)/shard_map/ppermute | solution.py:163
  48.0 0.0 copy-done
  48.0 1.5 %forward.1 = (bf16[4,128,768]{2,1,0:T(8,128)(2,1)S(1)}, bf16[2048,768]{1,0:T(8,128)(2,1)S(1)}) custom-call(bf16[128,2048]{1,0:T(8,128)(2,1)S(1)} %get-tuple-element.30.x0, bf16[128,2048]{1,0:T(8,128)(2,1)S(1)} %collective-permute-done.x1, bf16[128,2048]{1,0:T(8,128)(2,1)S(1)} %collective-permute-done.1.x3, bf16[512,768]{1,0:T(8,128)(2,1)S(1)} %copy-done, ...), custom_call_target="tpu_custom_call" | custom-call | flops 1207959552 | bytes 6291456 | tf_op jit(solution)/shard_map/forward/pallas_call | solution.py:217
  49.5 0.0 collective-permute-done.2.x2
  49.5 0.0 copy-start.1
  49.5 0.0 copy-start.2
  49.5 0.6 last_forward.1
  50.1 15.1 %all_to_all.10.parts = bf16[4,128,768]{2,1,0:T(8,128)(2,1)S(1)} all-to-all(bf16[4,128,768]{2,1,0:T(8,128)(2,1)S(1)} %last_forward.1), channel_id=1, replica_groups=mesh['zl'=2,'y'=8,'c'=2,'x'=4,'zh'=4] {'x'}, dimensions={0} | all-to-all | bytes 1572864 | tf_op jit(solution)/shard_map/all_to_all | solution.py:167
  65.2 0.0 copy-done.1
  65.2 0.0 copy-done.2
  65.2 1.5 %attention.1 = bf16[128,768]{1,0:T(8,128)(2,1)S(1)} custom-call(bf16[4,128,768]{2,1,0:T(8,128)(2,1)S(1)} %all_to_all.10.parts, s32[1,128]{1,0:T(1,128)S(1)} %copy-done.2, bf16[128,512]{1,0:T(8,128)(2,1)S(1)} %copy-done.1), custom_call_target="tpu_custom_call" | custom-call | flops 268435456 | bytes 1048576 | tf_op jit(solution)/shard_map/attention/pallas_call | solution.py:234
  66.7 14.1 %all-gather = bf16[512,768]{1,0:T(8,128)(2,1)S(1)} all-gather(bf16[128,768]{1,0:T(8,128)(2,1)S(1)} %attention.1), channel_id=2, replica_groups=mesh['zl'=2,'y'=8,'c'=2,'x'=4,'zh'=4] {'x'}, dimensions={0}, use_global_device_ids=true | all-gather | bytes 983040 | tf_op jit(solution)/shard_map/all_gather | solution.py:241
  80.8 1.4 weight_grad_other_core.1
  82.2 1.9 %collective-permute-start.9 = (bf16[64,24,512]{2,1,0:T(8,128)(2,1)S(1)}, bf16[64,24,512]{2,1,0:T(8,128)(2,1)S(1)}, u32[]{:S(2)}, u32[]{:S(2)}) collective-permute-start(bf16[64,24,512]{2,1,0:T(8,128)(2,1)S(1)} %weight_grad_other_core.1), channel_id=1, source_target_pairs={{0,16},{16,0},{1,17},{17,1},{2,18},{18,2},{3,19},{19,3},{4,20},{20... | collective-permute-start | bytes 4718600 | tf_op jit(solution)/shard_map/ppermute | solution.py:163
  84.1 1.8 %input_grad.1 = (bf16[128,2048]{1,0:T(8,128)(2,1)S(1)}, bf16[128,2048]{1,0:T(8,128)(2,1)S(1)}, bf16[128,2048]{1,0:T(8,128)(2,1)S(1)}, bf16[128,2048]{1,0:T(8,128)(2,1)S(1)}) custom-call(bf16[4,128,768]{2,1,0:T(8,128)(2,1)S(1)} %bitcast.3, bf16[2048,768]{1,0:T(8,128)(2,1)S(1)} %get-tuple-element.20.whole), custom_call_target="tpu_custom_call" | custom-call | flops 1610612736 | bytes 6291456 | tf_op jit(solution)/shard_map/input_grad/pallas_call | solution.py:253
  86.0 0.0 copy-start.3
  86.0 0.8 copy-done.3
  86.8 0.7 collective-permute-done.9.got
  87.5 2.5 %weight_grad_this_core.1 = bf16[64,24,512]{2,1,0:T(8,128)(2,1)} custom-call(bf16[4,128,768]{2,1,0:T(8,128)(2,1)S(1)} %bitcast.4, bf16[128,2048]{1,0:T(8,128)(2,1)S(1)} %get-tuple-element.30.x0, bf16[128,2048]{1,0:T(8,128)(2,1)S(1)} %collective-permute-done.x1, bf16[128,2048]{1,0:T(8,128)(2,1)S(1)} %collective-permute-done.2.x2, ...), custom_call_target="tpu_custom_call" | custom-call | flops 805306368 | bytes 6291456 | tf_op jit(solution)/shard_map/weight_grad_this_core/pallas_call | solution.py:263
  90.1 8.1 %all-to-all-start.1 = ((bf16[64,24,512]{2,1,0:T(8,128)(2,1)}), bf16[64,24,512]{2,1,0:T(8,128)(2,1)S(1)}, u32[]{:S(2)}, u32[]{:S(2)}) async-start(bf16[64,24,512]{2,1,0:T(8,128)(2,1)} %weight_grad_this_core.1), calls=%async_computation.1 | async-start | bytes 3145728 | tf_op jit(solution)/shard_map/all_to_all | solution.py:167
  98.2 2.9 %collective-permute-start.10 = (bf16[128,2048]{1,0:T(8,128)(2,1)}, bf16[128,2048]{1,0:T(8,128)(2,1)S(1)}, u32[]{:S(2)}, u32[]{:S(2)}) collective-permute-start(bf16[128,2048]{1,0:T(8,128)(2,1)} %copy-done.3), channel_id=1, source_target_pairs={{0,12},{4,0},{8,4},{12,8},{1,13},{5,1},{9,5},{13,9},{2,14},{6,2},{... | collective-permute-start | bytes 1572872 | tf_op jit(solution)/shard_map/ppermute | solution.py:163
  101.1 4.6 %collective-permute-start.11 = (bf16[128,2048]{1,0:T(8,128)(2,1)S(1)}, bf16[128,2048]{1,0:T(8,128)(2,1)S(1)}, u32[]{:S(2)}, u32[]{:S(2)}) collective-permute-start(bf16[128,2048]{1,0:T(8,128)(2,1)S(1)} %get-tuple-element.27), channel_id=1, source_target_pairs={{0,8},{4,12},{8,0},{12,4},{1,9},{5,13},{9,1},{13,5},{2,10},{6,14},... | collective-permute-start | bytes 1572872 | tf_op jit(solution)/shard_map/ppermute | solution.py:163
  105.7 2.4 %collective-permute-start.12 = (bf16[128,2048]{1,0:T(8,128)(2,1)S(1)}, bf16[128,2048]{1,0:T(8,128)(2,1)S(1)}, u32[]{:S(2)}, u32[]{:S(2)}) collective-permute-start(bf16[128,2048]{1,0:T(8,128)(2,1)S(1)} %get-tuple-element.28), channel_id=1, source_target_pairs={{0,4},{4,8},{8,12},{12,0},{1,5},{5,9},{9,13},{13,1},{2,6},{6,10},{... | collective-permute-start | bytes 1572872 | tf_op jit(solution)/shard_map/ppermute | solution.py:163
  108.1 7.9 %collective-permute-done.10.refs_1_ = bf16[128,2048]{1,0:T(8,128)(2,1)S(1)} collective-permute-done((bf16[128,2048]{1,0:T(8,128)(2,1)}, bf16[128,2048]{1,0:T(8,128)(2,1)S(1)}, u32[]{:S(2)}, u32[]{:S(2)}) %collective-permute-start.10) | collective-permute-done | bytes 524320 | tf_op jit(solution)/shard_map/ppermute | solution.py:163
  115.9 10.9 %collective-permute-done.11.refs_2_ = bf16[128,2048]{1,0:T(8,128)(2,1)S(1)} collective-permute-done((bf16[128,2048]{1,0:T(8,128)(2,1)S(1)}, bf16[128,2048]{1,0:T(8,128)(2,1)S(1)}, u32[]{:S(2)}, u32[]{:S(2)}) %collective-permute-start.11) | collective-permute-done | bytes 524320 | tf_op jit(solution)/shard_map/ppermute | solution.py:163
  126.8 1.9 %collective-permute-done.12.refs_3_ = bf16[128,2048]{1,0:T(8,128)(2,1)S(1)} collective-permute-done((bf16[128,2048]{1,0:T(8,128)(2,1)S(1)}, bf16[128,2048]{1,0:T(8,128)(2,1)S(1)}, u32[]{:S(2)}, u32[]{:S(2)}) %collective-permute-start.12) | collective-permute-done | bytes 524320 | tf_op jit(solution)/shard_map/ppermute | solution.py:163
  128.8 1.5 %join_features.1 = bf16[128,8192]{1,0:T(8,128)(2,1)} custom-call(bf16[128,2048]{1,0:T(8,128)(2,1)S(1)} %get-tuple-element.25.refs_0_, bf16[128,2048]{1,0:T(8,128)(2,1)S(1)} %collective-permute-done.10.refs_1_, bf16[128,2048]{1,0:T(8,128)(2,1)S(1)} %collective-permute-done.11.refs_2_, bf16[128,2048]{1,0:T(8,128)(2,1)S(1)} %collective-permute-done.12.refs_3_), custom_call_target="tpu_custom_call" | custom-call | flops 1048576 | bytes 4194304 | tf_op jit(solution)/shard_map/join_features/pallas_call | solution.py:279
  130.2 8.7 %all-to-all-done.1.ref = bf16[64,24,512]{2,1,0:T(8,128)(2,1)S(1)} async-done(((bf16[64,24,512]{2,1,0:T(8,128)(2,1)}), bf16[64,24,512]{2,1,0:T(8,128)(2,1)S(1)}, u32[]{:S(2)}, u32[]{:S(2)}) %all-to-all-start.1) | async-done | bytes 1572896 | tf_op jit(solution)/shard_map/all_to_all | solution.py:167
  138.9 0.9 add_replicas.1
Async XLA Ops:
  1.7 20.1 %collective-permute-start.3 = (bf16[256,768]{1,0:T(8,128)(2,1)S(1)}, bf16[256,768]{1,0:T(8,128)(2,1)S(1)}, u32[]{:S(2)}, u32[]{:S(2)}) collective-permute-start(bf16[256,768]{1,0:T(8,128)(2,1)S(1)} %constant_dynamic-slice_fusion.1), channel_id=1, source_target_pairs={{0,259},{1,256},{2,257},{3,258},{256,1},{257,2},{258,3},{259,0},{4... | collective-permute-start | bytes 1179656 | tf_op jit(solution)/shard_map/ppermute | solution.py:176
  12.6 35.4 %copy-start = (bf16[512,768]{1,0:T(8,128)(2,1)S(1)}, bf16[512,768]{1,0:T(8,128)(2,1)}, u32[]{:S(2)}) copy-start(bf16[512,768]{1,0:T(8,128)(2,1)} %w0.3) | copy-start | bytes 2359300
  14.5 16.5 %collective-permute-start.1 = (bf16[128,2048]{1,0:T(8,128)(2,1)S(1)}, bf16[128,2048]{1,0:T(8,128)(2,1)S(1)}, u32[]{:S(2)}, u32[]{:S(2)}) collective-permute-start(bf16[128,2048]{1,0:T(8,128)(2,1)S(1)} %get-tuple-element.31), channel_id=1, source_target_pairs={{0,12},{4,0},{8,4},{12,8},{1,13},{5,1},{9,5},{13,9},{2,14},{6,2},{... | collective-permute-start | bytes 1572872 | tf_op jit(solution)/shard_map/ppermute | solution.py:163
  17.2 15.0 %collective-permute-start = (bf16[128,2048]{1,0:T(8,128)(2,1)S(1)}, bf16[128,2048]{1,0:T(8,128)(2,1)S(1)}, u32[]{:S(2)}, u32[]{:S(2)}) collective-permute-start(bf16[128,2048]{1,0:T(8,128)(2,1)S(1)} %get-tuple-element.32), channel_id=1, source_target_pairs={{0,4},{4,8},{8,12},{12,0},{1,5},{5,9},{9,13},{13,1},{2,6},{6,10},{... | collective-permute-start | bytes 1572872 | tf_op jit(solution)/shard_map/ppermute | solution.py:163
  21.7 16.5 %collective-permute-start.7 = (bf16[256,768]{1,0:T(8,128)(2,1)S(1)}, bf16[256,768]{1,0:T(8,128)(2,1)S(1)}, u32[]{:S(2)}, u32[]{:S(2)}) collective-permute-start(bf16[256,768]{1,0:T(8,128)(2,1)S(1)} %collective-permute-done.3.a), channel_id=1, source_target_pairs={{0,1},{1,2},{2,3},{3,0},{256,259},{257,256},{258,257},{259,258},{4... | collective-permute-start | bytes 1179656 | tf_op jit(solution)/shard_map/ppermute | solution.py:176
  23.6 20.8 %collective-permute-start.5 = (bf16[256,768]{1,0:T(8,128)(2,1)S(1)}, bf16[256,768]{1,0:T(8,128)(2,1)S(1)}, u32[]{:S(2)}, u32[]{:S(2)}) collective-permute-start(bf16[256,768]{1,0:T(8,128)(2,1)S(1)} %collective-permute-done.3.a), channel_id=1, source_target_pairs={{0,256},{1,257},{2,258},{3,259},{256,0},{257,1},{258,2},{259,3},{4... | collective-permute-start | bytes 1179656 | tf_op jit(solution)/shard_map/ppermute | solution.py:176
  32.2 17.3 %collective-permute-start.2 = (bf16[128,2048]{1,0:T(8,128)(2,1)S(1)}, bf16[128,2048]{1,0:T(8,128)(2,1)S(1)}, u32[]{:S(2)}, u32[]{:S(2)}) collective-permute-start(bf16[128,2048]{1,0:T(8,128)(2,1)S(1)} %get-tuple-element.16), channel_id=1, source_target_pairs={{0,8},{4,12},{8,0},{12,4},{1,9},{5,13},{9,1},{13,5},{2,10},{6,14},... | collective-permute-start | bytes 1572872 | tf_op jit(solution)/shard_map/ppermute | solution.py:163
  36.3 10.1 %collective-permute-start.4 = (bf16[256,768]{1,0:T(8,128)(2,1)S(1)}, bf16[256,768]{1,0:T(8,128)(2,1)S(1)}, u32[]{:S(2)}, u32[]{:S(2)}) collective-permute-start(bf16[256,768]{1,0:T(8,128)(2,1)S(1)} %collective-permute-done.3.a), channel_id=1, source_target_pairs={{0,16},{16,0},{1,17},{17,1},{2,18},{18,2},{3,19},{19,3},{4,20},{20... | collective-permute-start | bytes 1179656 | tf_op jit(solution)/shard_map/ppermute | solution.py:163
  38.2 8.1 %collective-permute-start.8 = (bf16[256,768]{1,0:T(8,128)(2,1)S(1)}, bf16[256,768]{1,0:T(8,128)(2,1)S(1)}, u32[]{:S(2)}, u32[]{:S(2)}) collective-permute-start(bf16[256,768]{1,0:T(8,128)(2,1)S(1)} %collective-permute-done.7.d), channel_id=1, source_target_pairs={{0,16},{16,0},{1,17},{17,1},{2,18},{18,2},{3,19},{19,3},{4,20},{20... | collective-permute-start | bytes 1179656 | tf_op jit(solution)/shard_map/ppermute | solution.py:163
  44.4 3.6 %collective-permute-start.6 = (bf16[256,768]{1,0:T(8,128)(2,1)S(1)}, bf16[256,768]{1,0:T(8,128)(2,1)S(1)}, u32[]{:S(2)}, u32[]{:S(2)}) collective-permute-start(bf16[256,768]{1,0:T(8,128)(2,1)S(1)} %collective-permute-done.5.b), channel_id=1, source_target_pairs={{0,16},{16,0},{1,17},{17,1},{2,18},{18,2},{3,19},{19,3},{4,20},{20... | collective-permute-start | bytes 1179656 | tf_op jit(solution)/shard_map/ppermute | solution.py:163
  49.5 15.7 %copy-start.1 = (bf16[128,512]{1,0:T(8,128)(2,1)S(1)}, bf16[128,512]{1,0:T(8,128)(2,1)}, u32[]{:S(2)}) copy-start(bf16[128,512]{1,0:T(8,128)(2,1)} %cot_ref.1) | copy-start | bytes 393220
  49.5 15.7 %copy-start.2 = (s32[1,128]{1,0:T(1,128)S(1)}, s32[1,128]{1,0:T(1,128)}, u32[]{:S(2)}) copy-start(s32[1,128]{1,0:T(1,128)} %seg_ref.1) | copy-start | bytes 1540
  82.2 5.3 %collective-permute-start.9 = (bf16[64,24,512]{2,1,0:T(8,128)(2,1)S(1)}, bf16[64,24,512]{2,1,0:T(8,128)(2,1)S(1)}, u32[]{:S(2)}, u32[]{:S(2)}) collective-permute-start(bf16[64,24,512]{2,1,0:T(8,128)(2,1)S(1)} %weight_grad_other_core.1), channel_id=1, source_target_pairs={{0,16},{16,0},{1,17},{17,1},{2,18},{18,2},{3,19},{19,3},{4,20},{20... | collective-permute-start | bytes 4718600 | tf_op jit(solution)/shard_map/ppermute | solution.py:163
  86.0 0.8 copy-start.3
  90.1 48.9 %all-to-all-start.1 = ((bf16[64,24,512]{2,1,0:T(8,128)(2,1)}), bf16[64,24,512]{2,1,0:T(8,128)(2,1)S(1)}, u32[]{:S(2)}, u32[]{:S(2)}) async-start(bf16[64,24,512]{2,1,0:T(8,128)(2,1)} %weight_grad_this_core.1), calls=%async_computation.1 | async-start | bytes 3145728 | tf_op jit(solution)/shard_map/all_to_all | solution.py:167
  98.2 17.7 %collective-permute-start.10 = (bf16[128,2048]{1,0:T(8,128)(2,1)}, bf16[128,2048]{1,0:T(8,128)(2,1)S(1)}, u32[]{:S(2)}, u32[]{:S(2)}) collective-permute-start(bf16[128,2048]{1,0:T(8,128)(2,1)} %copy-done.3), channel_id=1, source_target_pairs={{0,12},{4,0},{8,4},{12,8},{1,13},{5,1},{9,5},{13,9},{2,14},{6,2},{... | collective-permute-start | bytes 1572872 | tf_op jit(solution)/shard_map/ppermute | solution.py:163
  101.1 25.8 %collective-permute-start.11 = (bf16[128,2048]{1,0:T(8,128)(2,1)S(1)}, bf16[128,2048]{1,0:T(8,128)(2,1)S(1)}, u32[]{:S(2)}, u32[]{:S(2)}) collective-permute-start(bf16[128,2048]{1,0:T(8,128)(2,1)S(1)} %get-tuple-element.27), channel_id=1, source_target_pairs={{0,8},{4,12},{8,0},{12,4},{1,9},{5,13},{9,1},{13,5},{2,10},{6,14},... | collective-permute-start | bytes 1572872 | tf_op jit(solution)/shard_map/ppermute | solution.py:163
  105.7 23.1 %collective-permute-start.12 = (bf16[128,2048]{1,0:T(8,128)(2,1)S(1)}, bf16[128,2048]{1,0:T(8,128)(2,1)S(1)}, u32[]{:S(2)}, u32[]{:S(2)}) collective-permute-start(bf16[128,2048]{1,0:T(8,128)(2,1)S(1)} %get-tuple-element.28), channel_id=1, source_target_pairs={{0,4},{4,8},{8,12},{12,0},{1,5},{5,9},{9,13},{13,1},{2,6},{6,10},{... | collective-permute-start | bytes 1572872 | tf_op jit(solution)/shard_map/ppermute | solution.py:163

commit v5 on v3

--- a/solution.py
+++ b/solution.py
@@ -51,21 +51,27 @@
     return [pl.multiple_of(p, rows) for p in places]
 
 
-def forward_kernel(x0, x1, x2, x3, w0, a, a2, b, b2, d, d2, parts, whole, acc):
-    rows = a.shape[0]
-    tokens = x0.shape[0]
-    me = lax.axis_index("x")
-    for i, (place, w) in enumerate(zip(piece_places(rows), (w0, a, a2, b, b2, d, d2))):
-        depth = w.shape[0]
-        x = jnp.concatenate([r[:, pl.ds(place, depth)] for r in (x0, x1, x2, x3)], axis=0)
-        whole[pl.ds(place, depth), :] = w[...]
-        term = dot(x, w[...])
-        if i == 0:
+def weight_product(xs, place, w):
+    return dot(jnp.concatenate([x[:, pl.ds(place, w.shape[0])] for x in xs], axis=0), w[...])
+
+
+def forward_kernel(x0, x1, x2, x3, w0, a, a2, b, d, d2, whole, acc):
+    places = piece_places(a.shape[0])
+    for i, w in ((0, w0), (1, a), (2, a2), (3, b), (5, d), (6, d2)):
+        whole[pl.ds(places[i], w.shape[0]), :] = w[...]
+        term = weight_product((x0, x1, x2, x3), places[i], w)
+        if w is w0:
             acc[...] = term
         else:
             acc[...] += term
+
+
+def last_forward_kernel(x0, x1, x2, x3, b2, acc, parts):
+    tokens = x0.shape[0]
+    me = lax.axis_index("x")
+    total = acc[...] + weight_product((x0, x1, x2, x3), piece_places(b2.shape[0])[4], b2)
     for k in range(4):
-        parts[lax.rem(me + 4 - k, 4)] = acc[k * tokens : (k + 1) * tokens, :].astype(BF16)
+        parts[lax.rem(me + 4 - k, 4)] = total[k * tokens : (k + 1) * tokens, :].astype(BF16)
 
 
 def attention_kernel(parts, seg_ref, cot_ref, out):
@@ -128,19 +134,25 @@
         out[at] = piece.astype(BF16)
 
 
-def mine_kernel(g, x0, x1, x2, x3, got, out):
+def mine_kernel(g, x0, x1, x2, x3, out):
     for at, piece in weight_terms(g, (x0, x1, x2, x3), lax.axis_index("c"), out.shape):
-        out[at] = (piece + got[at].astype(F32)).astype(BF16)
-
-
-def input_kernel(g, whole, *outs):
-    n, tokens, _ = g.shape
+        out[at] = piece
+
+
+def add_kernel(mine, got, out):
+    out[...] = (mine[...] + got[...].astype(F32)).astype(BF16)
+
+
+def input_kernel(g, whole, b2, *outs):
+    tokens = g.shape[1]
+    tile = b2.shape[0]
     grads = relative(g)
-    tile = 256
-    for at in range(0, whole.shape[0], tile):
-        term = dot(grads, whole[at : at + tile, :], NT).astype(BF16)
+    pieces = [(at, whole[at : at + tile, :]) for at in range(0, whole.shape[0], tile)]
+    pieces.append((piece_places(tile)[4], b2[...]))
+    for at, w in pieces:
+        term = dot(grads, w, NT).astype(BF16)
         for k, out in enumerate(outs):
-            out[:, at : at + tile] = term[k * tokens : (k + 1) * tokens]
+            out[:, pl.ds(at, tile)] = term[k * tokens : (k + 1) * tokens]
 
 
 def total_kernel(ref, out):
@@ -167,6 +179,10 @@
 
 def across(value):
     return z_move(value, lambda zl, zh: (0, zh + 1) if zl else (1, zh - 1))
+
+
+def over(value):
+    return z_move(value, lambda zl, zh: (zl, zh - 1 if zl else zh + 1))
 
 
 def beside(value):
@@ -186,27 +202,32 @@
     sent = [lax.dynamic_slice_in_dim(inputs, lax.rem(me + k, n) * width, width, 1) for k in range(n)]
     own = lax.dynamic_slice_in_dim(qkv_weight, c * half, half, 0)
     a = across(own)
-    x1 = shift(sent[1], "x", 1)
-    x3 = shift(sent[3], "x", 3)
     x2 = shift(sent[2], "x", 2)
+    x2, ahead, behind = lax.optimization_barrier((x2, sent[1], sent[3]))
+    x1 = shift(ahead, "x", 1)
+    x3 = shift(behind, "x", 3)
     a2 = shift(a, "c", 1)
     b = beside(a)
-    b, x1, x3 = lax.optimization_barrier((b, x1, x3))
     b2 = shift(b, "c", 1)
-    d = across(b)
+    d = over(a)
     d2 = shift(d, "c", 1)
     xs = (sent[0], x1, x2, x3)
-    weights = (qkv_weight, a, a2, b, b2, d, d2)
 
     flops = 2 * n * tokens * width * cols
-    parts, whole = pl.pallas_call(
+    whole, begun = pl.pallas_call(
         forward_kernel,
-        out_shape=[arr((n, tokens, cols)), arr((width, cols))],
-        scratch_shapes=[pltpu.VMEM((n * tokens, cols), F32)],
-        compiler_params=PARAMS,
-        cost_estimate=cost(flops, 6 << 20),
+        out_shape=[arr((width, cols)), arr((n * tokens, cols), F32)],
+        compiler_params=PARAMS,
+        cost_estimate=cost(flops, 8 << 20),
         name="forward",
-    )(*xs, *weights)
+    )(*xs, qkv_weight, a, a2, b, d, d2)
+    parts = pl.pallas_call(
+        last_forward_kernel,
+        out_shape=arr((n, tokens, cols)),
+        compiler_params=PARAMS,
+        cost_estimate=cost(flops // 8, 3 << 20),
+        name="last_forward",
+    )(*xs, b2, begun)
     parts = swap(parts, "x")
 
     grads = pl.pallas_call(
@@ -234,17 +255,24 @@
         compiler_params=PARAMS,
         cost_estimate=cost(flops, 6 << 20),
         name="input_grad",
-    )(grads, whole)
+    )(grads, whole, b2)
     got, back = lax.optimization_barrier((got, back))
     home = [back[0]] + [shift(back[k], "x", n - k) for k in range(1, n)]
 
-    summed = pl.pallas_call(
+    mine = pl.pallas_call(
         mine_kernel,
-        out_shape=share,
+        out_shape=arr(share.shape, F32),
         compiler_params=PARAMS,
         cost_estimate=cost(flops // 2, 6 << 20),
         name="weight_grad_this_core",
-    )(grads, *xs, got)
+    )(grads, *xs)
+    summed = pl.pallas_call(
+        add_kernel,
+        out_shape=share,
+        compiler_params=PARAMS,
+        cost_estimate=cost(1 << 20, 6 << 20),
+        name="add_cores",
+    )(mine, got)
     pieces = swap(summed, ("zl", "y", "zh"))
     weight_grad = pl.pallas_call(
         total_kernel,

time: 146 us -> 141 us (0.966)
  waiting for transfers between devices: 47.2 us -> 40.7 us
  starting transfers between devices: 53.8 us -> 55.4 us
    ppermute x10, waiting for transfers between devices: 36 us -> 25 us  [shift(): return lax.ppermute(value, axis, [(i, (i + k) % n) for i in range(n)])]
    ppermute x3, waiting for transfers between devices: 2.53 us -> 6.9 us  [z_move(): return lax.ppermute(value, ('zl', 'zh'), pairs)]
    ppermute x3, starting transfers between devices: 17.4 us -> 19.2 us  [z_move(): return lax.ppermute(value, ('zl', 'zh'), pairs)]
    pallas_call x2 -> x4, Pallas kernels: 4.49 us -> 4.87 us  [the longest x1 1.69 us: on_device(): pl.pallas_call(forward_kernel, out_shape=[arr((width, cols)), arr((n * to...]
  transfers between devices with their start and end apart: 14 -> 14, of which waited for: 11 -> 8; matrix products, arithmetic and copies ran while one was open for 1% -> 1% of each run, Pallas kernels for 2% -> 5%
where the time goes in v5:
time: 141 us; the launch traced here: 139 us
  starting transfers between devices  55.4 us (39%)
  waiting for transfers between devices  40.7 us (29%)
  blocking collectives  26.3 us (19%)
  Pallas kernels  12.1 us (9%)
  local copies, waits for them, and re-layouts  3.62 us (3%)
    ppermute x10, starting transfers between devices, shift(): return lax.ppermute(value, axis, [(i, (i + k) % n) for i in range(n)])  27.1 us
    ppermute x10, waiting for transfers between devices, shift(): return lax.ppermute(value, axis, [(i, (i + k) % n) for i in range(n)])  25 us
    ppermute x3, starting transfers between devices, z_move(): return lax.ppermute(value, ('zl', 'zh'), pairs)  19.2 us
    all_gather x1, blocking collectives, on_device(): grads = lax.all_gather(grads, 'x', axis=0, tiled=False)  13.4 us
    all_to_all x1, blocking collectives, swap(): return lax.all_to_all(value, axes, 0, 0, tiled=True)  12.9 us
    all_to_all x1, starting transfers between devices, swap(): return lax.all_to_all(value, axes, 0, 0, tiled=True)  9.12 us
    all_to_all x1, waiting for transfers between devices, swap(): return lax.all_to_all(value, axes, 0, 0, tiled=True)  8.8 us
    ppermute x3, waiting for transfers between devices, z_move(): return lax.ppermute(value, ('zl', 'zh'), pairs)  6.9 us
  transfers between devices with their start and end apart: 14, of which 8 were waited for; matrix products, arithmetic and copies ran while one was open for 1% of the time, Pallas kernels for 5%

profile of v5, /device:TPU:6, one launch (start us, length us, event | category | flops | bytes accessed | tf_op | source)
XLA Modules:
  0.0 139.0 jit_solution(7227341597048964683)
XLA Ops:
  0.6 1.0 constant_dynamic-slice_fusion
  1.7 10.9 %collective-permute-start.3 = (bf16[256,768]{1,0:T(8,128)(2,1)S(1)}, bf16[256,768]{1,0:T(8,128)(2,1)S(1)}, u32[]{:S(2)}, u32[]{:S(2)}) collective-permute-start(bf16[256,768]{1,0:T(8,128)(2,1)S(1)} %constant_dynamic-slice_fusion), channel_id=1, source_target_pairs={{0,259},{1,256},{2,257},{3,258},{256,1},{257,2},{258,3},{259,0},{4... | collective-permute-start | bytes 1179656 | tf_op jit(solution)/shard_map/ppermute | solution.py:177
  12.6 0.0 copy-start
  12.7 1.8 %constant_dynamic-slice_fusion.1 = (bf16[128,2048]{1,0:T(8,128)(2,1)S(1)}, bf16[128,2048]{1,0:T(8,128)(2,1)S(1)}, bf16[128,2048]{1,0:T(8,128)(2,1)S(1)}, bf16[128,2048]{1,0:T(8,128)(2,1)S(1)}) fusion(bf16[128,8192]{1,0:T(8,128)(2,1)} %param.4, s32[]{:T(128)S(6)} %select_n.18, s32[]{:T(128)S(6)} %select_n.16, s32[]{:T(128)S(6)} %select_n.15, s32[]{:T(128)S(6)} %select_n.17), kind=kLoop, calls=%fused_computation.1 | loop fusion | bytes 4194320 | tf_op jit(solution)/shard_map/dynamic_slice | solution.py:202
  14.5 3.3 %collective-permute-start = (bf16[128,2048]{1,0:T(8,128)(2,1)S(1)}, bf16[128,2048]{1,0:T(8,128)(2,1)S(1)}, u32[]{:S(2)}, u32[]{:S(2)}) collective-permute-start(bf16[128,2048]{1,0:T(8,128)(2,1)S(1)} %get-tuple-element.31), channel_id=1, source_target_pairs={{0,8},{4,12},{8,0},{12,4},{1,9},{5,13},{9,1},{13,5},{2,10},{6,14},... | collective-permute-start | bytes 1572872 | tf_op jit(solution)/shard_map/ppermute | solution.py:164
  17.8 3.9 %collective-permute-done.3.a = bf16[256,768]{1,0:T(8,128)(2,1)S(1)} collective-permute-done((bf16[256,768]{1,0:T(8,128)(2,1)S(1)}, bf16[256,768]{1,0:T(8,128)(2,1)S(1)}, u32[]{:S(2)}, u32[]{:S(2)}) %collective-permute-start.3) | collective-permute-done | bytes 393248 | tf_op jit(solution)/shard_map/ppermute | solution.py:177
  21.7 1.9 %collective-permute-start.7 = (bf16[256,768]{1,0:T(8,128)(2,1)S(1)}, bf16[256,768]{1,0:T(8,128)(2,1)S(1)}, u32[]{:S(2)}, u32[]{:S(2)}) collective-permute-start(bf16[256,768]{1,0:T(8,128)(2,1)S(1)} %collective-permute-done.3.a), channel_id=1, source_target_pairs={{0,1},{1,2},{2,3},{3,0},{256,259},{257,256},{258,257},{259,258},{4... | collective-permute-start | bytes 1179656 | tf_op jit(solution)/shard_map/ppermute | solution.py:177
  23.6 6.3 %collective-permute-start.4 = (bf16[256,768]{1,0:T(8,128)(2,1)S(1)}, bf16[256,768]{1,0:T(8,128)(2,1)S(1)}, u32[]{:S(2)}, u32[]{:S(2)}) collective-permute-start(bf16[256,768]{1,0:T(8,128)(2,1)S(1)} %collective-permute-done.3.a), channel_id=1, source_target_pairs={{0,256},{1,257},{2,258},{3,259},{256,0},{257,1},{258,2},{259,3},{4... | collective-permute-start | bytes 1179656 | tf_op jit(solution)/shard_map/ppermute | solution.py:177
  29.9 1.3 collective-permute-done.x2
  31.2 2.4 %collective-permute-start.1 = (bf16[128,2048]{1,0:T(8,128)(2,1)S(1)}, bf16[128,2048]{1,0:T(8,128)(2,1)S(1)}, u32[]{:S(2)}, u32[]{:S(2)}) collective-permute-start(bf16[128,2048]{1,0:T(8,128)(2,1)S(1)} %get-tuple-element.16), channel_id=1, source_target_pairs={{0,4},{4,8},{8,12},{12,0},{1,5},{5,9},{9,13},{13,1},{2,6},{6,10},{... | collective-permute-start | bytes 1572872 | tf_op jit(solution)/shard_map/ppermute | solution.py:164
  33.6 3.5 %collective-permute-start.2 = (bf16[128,2048]{1,0:T(8,128)(2,1)S(1)}, bf16[128,2048]{1,0:T(8,128)(2,1)S(1)}, u32[]{:S(2)}, u32[]{:S(2)}) collective-permute-start(bf16[128,2048]{1,0:T(8,128)(2,1)S(1)} %get-tuple-element.18), channel_id=1, source_target_pairs={{0,12},{4,0},{8,4},{12,8},{1,13},{5,1},{9,5},{13,9},{2,14},{6,2},{... | collective-permute-start | bytes 1572872 | tf_op jit(solution)/shard_map/ppermute | solution.py:164
  37.1 1.9 %collective-permute-start.6 = (bf16[256,768]{1,0:T(8,128)(2,1)S(1)}, bf16[256,768]{1,0:T(8,128)(2,1)S(1)}, u32[]{:S(2)}, u32[]{:S(2)}) collective-permute-start(bf16[256,768]{1,0:T(8,128)(2,1)S(1)} %collective-permute-done.3.a), channel_id=1, source_target_pairs={{0,16},{16,0},{1,17},{17,1},{2,18},{18,2},{3,19},{19,3},{4,20},{20... | collective-permute-start | bytes 1179656 | tf_op jit(solution)/shard_map/ppermute | solution.py:164
  39.0 0.0 collective-permute-done.7.d
  39.0 2.4 %collective-permute-start.8 = (bf16[256,768]{1,0:T(8,128)(2,1)S(1)}, bf16[256,768]{1,0:T(8,128)(2,1)S(1)}, u32[]{:S(2)}, u32[]{:S(2)}) collective-permute-start(bf16[256,768]{1,0:T(8,128)(2,1)S(1)} %collective-permute-done.7.d), channel_id=1, source_target_pairs={{0,16},{16,0},{1,17},{17,1},{2,18},{18,2},{3,19},{19,3},{4,20},{20... | collective-permute-start | bytes 1179656 | tf_op jit(solution)/shard_map/ppermute | solution.py:164
  41.4 3.0 %collective-permute-done.4.b = bf16[256,768]{1,0:T(8,128)(2,1)S(1)} collective-permute-done((bf16[256,768]{1,0:T(8,128)(2,1)S(1)}, bf16[256,768]{1,0:T(8,128)(2,1)S(1)}, u32[]{:S(2)}, u32[]{:S(2)}) %collective-permute-start.4) | collective-permute-done | bytes 393248 | tf_op jit(solution)/shard_map/ppermute | solution.py:177
  44.4 1.9 %collective-permute-start.5 = (bf16[256,768]{1,0:T(8,128)(2,1)S(1)}, bf16[256,768]{1,0:T(8,128)(2,1)S(1)}, u32[]{:S(2)}, u32[]{:S(2)}) collective-permute-start(bf16[256,768]{1,0:T(8,128)(2,1)S(1)} %collective-permute-done.4.b), channel_id=1, source_target_pairs={{0,16},{16,0},{1,17},{17,1},{2,18},{18,2},{3,19},{19,3},{4,20},{20... | collective-permute-start | bytes 1179656 | tf_op jit(solution)/shard_map/ppermute | solution.py:164
  46.3 0.0 collective-permute-done.6.a2
  46.3 0.0 collective-permute-done.1.x1
  46.3 2.6 %collective-permute-done.2.x3 = bf16[128,2048]{1,0:T(8,128)(2,1)S(1)} collective-permute-done((bf16[128,2048]{1,0:T(8,128)(2,1)S(1)}, bf16[128,2048]{1,0:T(8,128)(2,1)S(1)}, u32[]{:S(2)}, u32[]{:S(2)}) %collective-permute-start.2) | collective-permute-done | bytes 524320 | tf_op jit(solution)/shard_map/ppermute | solution.py:164
  48.9 0.0 collective-permute-done.8.d2
  48.9 0.0 copy-done
  48.9 1.7 %forward.1 = (bf16[2048,768]{1,0:T(8,128)(2,1)S(1)}, f32[512,768]{1,0:T(8,128)S(1)}) custom-call(bf16[128,2048]{1,0:T(8,128)(2,1)S(1)} %get-tuple-element.32.x0, bf16[128,2048]{1,0:T(8,128)(2,1)S(1)} %collective-permute-done.1.x1, bf16[128,2048]{1,0:T(8,128)(2,1)S(1)} %collective-permute-done.x2, bf16[128,2048]{1,0:T(8,128)(2,1)S(1)} %collective-permute-done.2.x3, ...), custom_call_target="tpu_custom_call" | custom-call | flops 1610612736 | bytes 8388608 | tf_op jit(solution)/shard_map/forward/pallas_call | solution.py:217
  50.6 0.0 collective-permute-done.5.b2
  50.6 0.0 copy-start.1
  50.6 0.0 copy-start.2
  50.7 0.4 last_forward.1
  51.0 12.9 %all_to_all.10.parts = bf16[4,128,768]{2,1,0:T(8,128)(2,1)S(1)} all-to-all(bf16[4,128,768]{2,1,0:T(8,128)(2,1)S(1)} %last_forward.1), channel_id=1, replica_groups=mesh['zl'=2,'y'=8,'c'=2,'x'=4,'zh'=4] {'x'}, dimensions={0} | all-to-all | bytes 1572864 | tf_op jit(solution)/shard_map/all_to_all | solution.py:168
  63.9 0.0 copy-done.1
  63.9 0.0 copy-done.2
  63.9 1.5 %attention.1 = bf16[128,768]{1,0:T(8,128)(2,1)S(1)} custom-call(bf16[4,128,768]{2,1,0:T(8,128)(2,1)S(1)} %all_to_all.10.parts, s32[1,128]{1,0:T(1,128)S(1)} %copy-done.2, bf16[128,512]{1,0:T(8,128)(2,1)S(1)} %copy-done.1), custom_call_target="tpu_custom_call" | custom-call | flops 268435456 | bytes 1048576 | tf_op jit(solution)/shard_map/attention/pallas_call | solution.py:233
  65.4 13.4 %all-gather = bf16[512,768]{1,0:T(8,128)(2,1)S(1)} all-gather(bf16[128,768]{1,0:T(8,128)(2,1)S(1)} %attention.1), channel_id=2, replica_groups=mesh['zl'=2,'y'=8,'c'=2,'x'=4,'zh'=4] {'x'}, dimensions={0}, use_global_device_ids=true | all-gather | bytes 983040 | tf_op jit(solution)/shard_map/all_gather | solution.py:240
  78.8 1.4 weight_grad_other_core.1
  80.2 1.9 %collective-permute-start.9 = (bf16[64,24,512]{2,1,0:T(8,128)(2,1)S(1)}, bf16[64,24,512]{2,1,0:T(8,128)(2,1)S(1)}, u32[]{:S(2)}, u32[]{:S(2)}) collective-permute-start(bf16[64,24,512]{2,1,0:T(8,128)(2,1)S(1)} %weight_grad_other_core.1), channel_id=1, source_target_pairs={{0,16},{16,0},{1,17},{17,1},{2,18},{18,2},{3,19},{19,3},{4,20},{20... | collective-permute-start | bytes 4718600 | tf_op jit(solution)/shard_map/ppermute | solution.py:164
  82.2 1.4 weight_grad_this_core.1.mine
  83.5 2.0 %input_grad.1 = (bf16[128,2048]{1,0:T(8,128)(2,1)S(1)}, bf16[128,2048]{1,0:T(8,128)(2,1)S(1)}, bf16[128,2048]{1,0:T(8,128)(2,1)S(1)}, bf16[128,2048]{1,0:T(8,128)(2,1)S(1)}) custom-call(bf16[4,128,768]{2,1,0:T(8,128)(2,1)S(1)} %bitcast.4, bf16[2048,768]{1,0:T(8,128)(2,1)S(1)} %get-tuple-element.20.whole, bf16[256,768]{1,0:T(8,128)(2,1)S(1)} %collective-permute-done.5.b2), custom_call_target="tpu_custom_call" | custom-call | flops 1610612736 | bytes 6291456 | tf_op jit(solution)/shard_map/input_grad/pallas_call | solution.py:252
  85.6 0.0 copy-start.3
  85.6 0.8 copy-done.3
  86.4 0.0 collective-permute-done.9.got
  86.4 1.4 %add_cores.1 = bf16[64,24,512]{2,1,0:T(8,128)(2,1)} custom-call(f32[64,24,512]{2,1,0:T(8,128)S(1)} %weight_grad_this_core.1.mine, bf16[64,24,512]{2,1,0:T(8,128)(2,1)S(1)} %collective-permute-done.9.got), custom_call_target="tpu_custom_call" | custom-call | flops 1048576 | bytes 6291456 | tf_op jit(solution)/shard_map/add_cores/pallas_call | solution.py:269
  87.8 9.1 %all-to-all-start.1 = ((bf16[64,24,512]{2,1,0:T(8,128)(2,1)}), bf16[64,24,512]{2,1,0:T(8,128)(2,1)S(1)}, u32[]{:S(2)}, u32[]{:S(2)}) async-start(bf16[64,24,512]{2,1,0:T(8,128)(2,1)} %add_cores.1), calls=%async_computation.1 | async-start | bytes 3145728 | tf_op jit(solution)/shard_map/all_to_all | solution.py:168
  96.9 2.8 %collective-permute-start.10 = (bf16[128,2048]{1,0:T(8,128)(2,1)}, bf16[128,2048]{1,0:T(8,128)(2,1)S(1)}, u32[]{:S(2)}, u32[]{:S(2)}) collective-permute-start(bf16[128,2048]{1,0:T(8,128)(2,1)} %copy-done.3), channel_id=1, source_target_pairs={{0,12},{4,0},{8,4},{12,8},{1,13},{5,1},{9,5},{13,9},{2,14},{6,2},{... | collective-permute-start | bytes 1572872 | tf_op jit(solution)/shard_map/ppermute | solution.py:164
  99.7 4.6 %collective-permute-start.11 = (bf16[128,2048]{1,0:T(8,128)(2,1)S(1)}, bf16[128,2048]{1,0:T(8,128)(2,1)S(1)}, u32[]{:S(2)}, u32[]{:S(2)}) collective-permute-start(bf16[128,2048]{1,0:T(8,128)(2,1)S(1)} %get-tuple-element.27), channel_id=1, source_target_pairs={{0,8},{4,12},{8,0},{12,4},{1,9},{5,13},{9,1},{13,5},{2,10},{6,14},... | collective-permute-start | bytes 1572872 | tf_op jit(solution)/shard_map/ppermute | solution.py:164
  104.3 2.5 %collective-permute-start.12 = (bf16[128,2048]{1,0:T(8,128)(2,1)S(1)}, bf16[128,2048]{1,0:T(8,128)(2,1)S(1)}, u32[]{:S(2)}, u32[]{:S(2)}) collective-permute-start(bf16[128,2048]{1,0:T(8,128)(2,1)S(1)} %get-tuple-element.28), channel_id=1, source_target_pairs={{0,4},{4,8},{8,12},{12,0},{1,5},{5,9},{9,13},{13,1},{2,6},{6,10},{... | collective-permute-start | bytes 1572872 | tf_op jit(solution)/shard_map/ppermute | solution.py:164
  106.8 7.9 %collective-permute-done.10.refs_1_ = bf16[128,2048]{1,0:T(8,128)(2,1)S(1)} collective-permute-done((bf16[128,2048]{1,0:T(8,128)(2,1)}, bf16[128,2048]{1,0:T(8,128)(2,1)S(1)}, u32[]{:S(2)}, u32[]{:S(2)}) %collective-permute-start.10) | collective-permute-done | bytes 524320 | tf_op jit(solution)/shard_map/ppermute | solution.py:164
  114.7 11.1 %collective-permute-done.11.refs_2_ = bf16[128,2048]{1,0:T(8,128)(2,1)S(1)} collective-permute-done((bf16[128,2048]{1,0:T(8,128)(2,1)S(1)}, bf16[128,2048]{1,0:T(8,128)(2,1)S(1)}, u32[]{:S(2)}, u32[]{:S(2)}) %collective-permute-start.11) | collective-permute-done | bytes 524320 | tf_op jit(solution)/shard_map/ppermute | solution.py:164
  125.8 2.0 %collective-permute-done.12.refs_3_ = bf16[128,2048]{1,0:T(8,128)(2,1)S(1)} collective-permute-done((bf16[128,2048]{1,0:T(8,128)(2,1)S(1)}, bf16[128,2048]{1,0:T(8,128)(2,1)S(1)}, u32[]{:S(2)}, u32[]{:S(2)}) %collective-permute-start.12) | collective-permute-done | bytes 524320 | tf_op jit(solution)/shard_map/ppermute | solution.py:164
  127.9 1.5 %join_features.1 = bf16[128,8192]{1,0:T(8,128)(2,1)} custom-call(bf16[128,2048]{1,0:T(8,128)(2,1)S(1)} %get-tuple-element.25.refs_0_, bf16[128,2048]{1,0:T(8,128)(2,1)S(1)} %collective-permute-done.10.refs_1_, bf16[128,2048]{1,0:T(8,128)(2,1)S(1)} %collective-permute-done.11.refs_2_, bf16[128,2048]{1,0:T(8,128)(2,1)S(1)} %collective-permute-done.12.refs_3_), custom_call_target="tpu_custom_call" | custom-call | flops 1048576 | bytes 4194304 | tf_op jit(solution)/shard_map/join_features/pallas_call | solution.py:285
  129.3 8.8 %all-to-all-done.1.ref = bf16[64,24,512]{2,1,0:T(8,128)(2,1)S(1)} async-done(((bf16[64,24,512]{2,1,0:T(8,128)(2,1)}), bf16[64,24,512]{2,1,0:T(8,128)(2,1)S(1)}, u32[]{:S(2)}, u32[]{:S(2)}) %all-to-all-start.1) | async-done | bytes 1572896 | tf_op jit(solution)/shard_map/all_to_all | solution.py:168
  138.1 0.9 add_replicas.1
Async XLA Ops:
  1.7 20.1 %collective-permute-start.3 = (bf16[256,768]{1,0:T(8,128)(2,1)S(1)}, bf16[256,768]{1,0:T(8,128)(2,1)S(1)}, u32[]{:S(2)}, u32[]{:S(2)}) collective-permute-start(bf16[256,768]{1,0:T(8,128)(2,1)S(1)} %constant_dynamic-slice_fusion), channel_id=1, source_target_pairs={{0,259},{1,256},{2,257},{3,258},{256,1},{257,2},{258,3},{259,0},{4... | collective-permute-start | bytes 1179656 | tf_op jit(solution)/shard_map/ppermute | solution.py:177
  12.6 36.3 %copy-start = (bf16[512,768]{1,0:T(8,128)(2,1)S(1)}, bf16[512,768]{1,0:T(8,128)(2,1)}, u32[]{:S(2)}) copy-start(bf16[512,768]{1,0:T(8,128)(2,1)} %w0.1) | copy-start | bytes 2359300
  14.5 16.8 %collective-permute-start = (bf16[128,2048]{1,0:T(8,128)(2,1)S(1)}, bf16[128,2048]{1,0:T(8,128)(2,1)S(1)}, u32[]{:S(2)}, u32[]{:S(2)}) collective-permute-start(bf16[128,2048]{1,0:T(8,128)(2,1)S(1)} %get-tuple-element.31), channel_id=1, source_target_pairs={{0,8},{4,12},{8,0},{12,4},{1,9},{5,13},{9,1},{13,5},{2,10},{6,14},... | collective-permute-start | bytes 1572872 | tf_op jit(solution)/shard_map/ppermute | solution.py:164
  21.7 17.3 %collective-permute-start.7 = (bf16[256,768]{1,0:T(8,128)(2,1)S(1)}, bf16[256,768]{1,0:T(8,128)(2,1)S(1)}, u32[]{:S(2)}, u32[]{:S(2)}) collective-permute-start(bf16[256,768]{1,0:T(8,128)(2,1)S(1)} %collective-permute-done.3.a), channel_id=1, source_target_pairs={{0,1},{1,2},{2,3},{3,0},{256,259},{257,256},{258,257},{259,258},{4... | collective-permute-start | bytes 1179656 | tf_op jit(solution)/shard_map/ppermute | solution.py:177
  23.6 20.8 %collective-permute-start.4 = (bf16[256,768]{1,0:T(8,128)(2,1)S(1)}, bf16[256,768]{1,0:T(8,128)(2,1)S(1)}, u32[]{:S(2)}, u32[]{:S(2)}) collective-permute-start(bf16[256,768]{1,0:T(8,128)(2,1)S(1)} %collective-permute-done.3.a), channel_id=1, source_target_pairs={{0,256},{1,257},{2,258},{3,259},{256,0},{257,1},{258,2},{259,3},{4... | collective-permute-start | bytes 1179656 | tf_op jit(solution)/shard_map/ppermute | solution.py:177
  31.2 15.1 %collective-permute-start.1 = (bf16[128,2048]{1,0:T(8,128)(2,1)S(1)}, bf16[128,2048]{1,0:T(8,128)(2,1)S(1)}, u32[]{:S(2)}, u32[]{:S(2)}) collective-permute-start(bf16[128,2048]{1,0:T(8,128)(2,1)S(1)} %get-tuple-element.16), channel_id=1, source_target_pairs={{0,4},{4,8},{8,12},{12,0},{1,5},{5,9},{9,13},{13,1},{2,6},{6,10},{... | collective-permute-start | bytes 1572872 | tf_op jit(solution)/shard_map/ppermute | solution.py:164
  33.6 15.3 %collective-permute-start.2 = (bf16[128,2048]{1,0:T(8,128)(2,1)S(1)}, bf16[128,2048]{1,0:T(8,128)(2,1)S(1)}, u32[]{:S(2)}, u32[]{:S(2)}) collective-permute-start(bf16[128,2048]{1,0:T(8,128)(2,1)S(1)} %get-tuple-element.18), channel_id=1, source_target_pairs={{0,12},{4,0},{8,4},{12,8},{1,13},{5,1},{9,5},{13,9},{2,14},{6,2},{... | collective-permute-start | bytes 1572872 | tf_op jit(solution)/shard_map/ppermute | solution.py:164
  37.1 9.2 %collective-permute-start.6 = (bf16[256,768]{1,0:T(8,128)(2,1)S(1)}, bf16[256,768]{1,0:T(8,128)(2,1)S(1)}, u32[]{:S(2)}, u32[]{:S(2)}) collective-permute-start(bf16[256,768]{1,0:T(8,128)(2,1)S(1)} %collective-permute-done.3.a), channel_id=1, source_target_pairs={{0,16},{16,0},{1,17},{17,1},{2,18},{18,2},{3,19},{19,3},{4,20},{20... | collective-permute-start | bytes 1179656 | tf_op jit(solution)/shard_map/ppermute | solution.py:164
  39.0 9.9 %collective-permute-start.8 = (bf16[256,768]{1,0:T(8,128)(2,1)S(1)}, bf16[256,768]{1,0:T(8,128)(2,1)S(1)}, u32[]{:S(2)}, u32[]{:S(2)}) collective-permute-start(bf16[256,768]{1,0:T(8,128)(2,1)S(1)} %collective-permute-done.7.d), channel_id=1, source_target_pairs={{0,16},{16,0},{1,17},{17,1},{2,18},{18,2},{3,19},{19,3},{4,20},{20... | collective-permute-start | bytes 1179656 | tf_op jit(solution)/shard_map/ppermute | solution.py:164
  44.4 6.2 %collective-permute-start.5 = (bf16[256,768]{1,0:T(8,128)(2,1)S(1)}, bf16[256,768]{1,0:T(8,128)(2,1)S(1)}, u32[]{:S(2)}, u32[]{:S(2)}) collective-permute-start(bf16[256,768]{1,0:T(8,128)(2,1)S(1)} %collective-permute-done.4.b), channel_id=1, source_target_pairs={{0,16},{16,0},{1,17},{17,1},{2,18},{18,2},{3,19},{19,3},{4,20},{20... | collective-permute-start | bytes 1179656 | tf_op jit(solution)/shard_map/ppermute | solution.py:164
  50.6 13.3 %copy-start.1 = (bf16[128,512]{1,0:T(8,128)(2,1)S(1)}, bf16[128,512]{1,0:T(8,128)(2,1)}, u32[]{:S(2)}) copy-start(bf16[128,512]{1,0:T(8,128)(2,1)} %cot_ref.1) | copy-start | bytes 393220
  50.6 13.3 %copy-start.2 = (s32[1,128]{1,0:T(1,128)S(1)}, s32[1,128]{1,0:T(1,128)}, u32[]{:S(2)}) copy-start(s32[1,128]{1,0:T(1,128)} %seg_ref.1) | copy-start | bytes 1540
  80.2 6.2 %collective-permute-start.9 = (bf16[64,24,512]{2,1,0:T(8,128)(2,1)S(1)}, bf16[64,24,512]{2,1,0:T(8,128)(2,1)S(1)}, u32[]{:S(2)}, u32[]{:S(2)}) collective-permute-start(bf16[64,24,512]{2,1,0:T(8,128)(2,1)S(1)} %weight_grad_other_core.1), channel_id=1, source_target_pairs={{0,16},{16,0},{1,17},{17,1},{2,18},{18,2},{3,19},{19,3},{4,20},{20... | collective-permute-start | bytes 4718600 | tf_op jit(solution)/shard_map/ppermute | solution.py:164
  85.6 0.8 copy-start.3
  87.8 50.3 %all-to-all-start.1 = ((bf16[64,24,512]{2,1,0:T(8,128)(2,1)}), bf16[64,24,512]{2,1,0:T(8,128)(2,1)S(1)}, u32[]{:S(2)}, u32[]{:S(2)}) async-start(bf16[64,24,512]{2,1,0:T(8,128)(2,1)} %add_cores.1), calls=%async_computation.1 | async-start | bytes 3145728 | tf_op jit(solution)/shard_map/all_to_all | solution.py:168
  96.9 17.8 %collective-permute-start.10 = (bf16[128,2048]{1,0:T(8,128)(2,1)}, bf16[128,2048]{1,0:T(8,128)(2,1)S(1)}, u32[]{:S(2)}, u32[]{:S(2)}) collective-permute-start(bf16[128,2048]{1,0:T(8,128)(2,1)} %copy-done.3), channel_id=1, source_target_pairs={{0,12},{4,0},{8,4},{12,8},{1,13},{5,1},{9,5},{13,9},{2,14},{6,2},{... | collective-permute-start | bytes 1572872 | tf_op jit(solution)/shard_map/ppermute | solution.py:164
  99.7 26.1 %collective-permute-start.11 = (bf16[128,2048]{1,0:T(8,128)(2,1)S(1)}, bf16[128,2048]{1,0:T(8,128)(2,1)S(1)}, u32[]{:S(2)}, u32[]{:S(2)}) collective-permute-start(bf16[128,2048]{1,0:T(8,128)(2,1)S(1)} %get-tuple-element.27), channel_id=1, source_target_pairs={{0,8},{4,12},{8,0},{12,4},{1,9},{5,13},{9,1},{13,5},{2,10},{6,14},... | collective-permute-start | bytes 1572872 | tf_op jit(solution)/shard_map/ppermute | solution.py:164
  104.3 23.6 %collective-permute-start.12 = (bf16[128,2048]{1,0:T(8,128)(2,1)S(1)}, bf16[128,2048]{1,0:T(8,128)(2,1)S(1)}, u32[]{:S(2)}, u32[]{:S(2)}) collective-permute-start(bf16[128,2048]{1,0:T(8,128)(2,1)S(1)} %get-tuple-element.28), channel_id=1, source_target_pairs={{0,4},{4,8},{8,12},{12,0},{1,5},{5,9},{9,13},{13,1},{2,6},{6,10},{... | collective-permute-start | bytes 1572872 | tf_op jit(solution)/shard_map/ppermute | solution.py:164

commit v6 on v5

--- a/solution.py
+++ b/solution.py
@@ -55,23 +55,26 @@
     return dot(jnp.concatenate([x[:, pl.ds(place, w.shape[0])] for x in xs], axis=0), w[...])
 
 
-def forward_kernel(x0, x1, x2, x3, w0, a, a2, b, d, d2, whole, acc):
+def forward_kernel(x0, x1, x2, w0, a, a2, b, d, d2, whole, acc):
     places = piece_places(a.shape[0])
     for i, w in ((0, w0), (1, a), (2, a2), (3, b), (5, d), (6, d2)):
         whole[pl.ds(places[i], w.shape[0]), :] = w[...]
-        term = weight_product((x0, x1, x2, x3), places[i], w)
+        term = weight_product((x0, x1, x2), places[i], w)
         if w is w0:
             acc[...] = term
         else:
             acc[...] += term
 
 
-def last_forward_kernel(x0, x1, x2, x3, b2, acc, parts):
+def last_forward_kernel(x0, x1, x2, x3, w0, a, a2, b, b2, d, d2, acc, parts):
     tokens = x0.shape[0]
     me = lax.axis_index("x")
-    total = acc[...] + weight_product((x0, x1, x2, x3), piece_places(b2.shape[0])[4], b2)
-    for k in range(4):
+    places = piece_places(a.shape[0])
+    total = acc[...] + weight_product((x0, x1, x2), places[4], b2)
+    for k in range(3):
         parts[lax.rem(me + 4 - k, 4)] = total[k * tokens : (k + 1) * tokens, :].astype(BF16)
+    total = sum(weight_product((x3,), place, w) for place, w in zip(places, (w0, a, a2, b, b2, d, d2)))
+    parts[lax.rem(me + 1, 4)] = total.astype(BF16)
 
 
 def attention_kernel(parts, seg_ref, cot_ref, out):
@@ -216,18 +219,18 @@
     flops = 2 * n * tokens * width * cols
     whole, begun = pl.pallas_call(
         forward_kernel,
-        out_shape=[arr((width, cols)), arr((n * tokens, cols), F32)],
-        compiler_params=PARAMS,
-        cost_estimate=cost(flops, 8 << 20),
+        out_shape=[arr((width, cols)), arr(((n - 1) * tokens, cols), F32)],
+        compiler_params=PARAMS,
+        cost_estimate=cost(flops * 3 // 4, 8 << 20),
         name="forward",
-    )(*xs, qkv_weight, a, a2, b, d, d2)
+    )(*xs[:3], qkv_weight, a, a2, b, d, d2)
     parts = pl.pallas_call(
         last_forward_kernel,
         out_shape=arr((n, tokens, cols)),
         compiler_params=PARAMS,
-        cost_estimate=cost(flops // 8, 3 << 20),
+        cost_estimate=cost(flops // 4, 5 << 20),
         name="last_forward",
-    )(*xs, b2, begun)
+    )(*xs, qkv_weight, a, a2, b, b2, d, d2, begun)
     parts = swap(parts, "x")
 
     grads = pl.pallas_call(

time: 141 us -> 140 us (level)
  blocking collectives: 26.3 us -> 28.5 us
  transfers between devices with their start and end apart: 14 -> 14, of which waited for: 8 -> 7; matrix products, arithmetic and copies ran while one was open for 1% -> 1% of each run, Pallas kernels for 5% -> 4%
where the time goes in v6:
time: 140 us; the launch traced here: 139 us
  starting transfers between devices  54.4 us (39%)
  waiting for transfers between devices  39.3 us (28%)
  blocking collectives  28.5 us (20%)
  Pallas kernels  12.1 us (9%)
  local copies, waits for them, and re-layouts  3.67 us (3%)
    ppermute x10, starting transfers between devices, shift(): return lax.ppermute(value, axis, [(i, (i + k) % n) for i in range(n)])  27.1 us
    ppermute x10, waiting for transfers between devices, shift(): return lax.ppermute(value, axis, [(i, (i + k) % n) for i in range(n)])  23.7 us
    ppermute x3, starting transfers between devices, z_move(): return lax.ppermute(value, ('zl', 'zh'), pairs)  19.2 us
    all_gather x1, blocking collectives, on_device(): grads = lax.all_gather(grads, 'x', axis=0, tiled=False)  14.3 us
    all_to_all x1, blocking collectives, swap(): return lax.all_to_all(value, axes, 0, 0, tiled=True)  14.2 us
    all_to_all x1, waiting for transfers between devices, swap(): return lax.all_to_all(value, axes, 0, 0, tiled=True)  8.81 us
    all_to_all x1, starting transfers between devices, swap(): return lax.all_to_all(value, axes, 0, 0, tiled=True)  8.16 us
    ppermute x3, waiting for transfers between devices, z_move(): return lax.ppermute(value, ('zl', 'zh'), pairs)  6.8 us
  transfers between devices with their start and end apart: 14, of which 7 were waited for; matrix products, arithmetic and copies ran while one was open for 1% of the time, Pallas kernels for 4%

profile of v6, /device:TPU:6, one launch (start us, length us, event | category | flops | bytes accessed | tf_op | source)
XLA Modules:
  0.0 138.9 jit_solution(6702913690423116569)
XLA Ops:
  0.6 1.0 constant_dynamic-slice_fusion
  1.7 10.9 %collective-permute-start.3 = (bf16[256,768]{1,0:T(8,128)(2,1)S(1)}, bf16[256,768]{1,0:T(8,128)(2,1)S(1)}, u32[]{:S(2)}, u32[]{:S(2)}) collective-permute-start(bf16[256,768]{1,0:T(8,128)(2,1)S(1)} %constant_dynamic-slice_fusion), channel_id=1, source_target_pairs={{0,259},{1,256},{2,257},{3,258},{256,1},{257,2},{258,3},{259,0},{4... | collective-permute-start | bytes 1179656 | tf_op jit(solution)/shard_map/ppermute | solution.py:180
  12.6 0.0 copy-start
  12.7 1.8 %constant_dynamic-slice_fusion.1 = (bf16[128,2048]{1,0:T(8,128)(2,1)S(1)}, bf16[128,2048]{1,0:T(8,128)(2,1)S(1)}, bf16[128,2048]{1,0:T(8,128)(2,1)S(1)}, bf16[128,2048]{1,0:T(8,128)(2,1)S(1)}) fusion(bf16[128,8192]{1,0:T(8,128)(2,1)} %param.4, s32[]{:T(128)S(6)} %select_n.18, s32[]{:T(128)S(6)} %select_n.16, s32[]{:T(128)S(6)} %select_n.15, s32[]{:T(128)S(6)} %select_n.17), kind=kLoop, calls=%fused_computation.1 | loop fusion | bytes 4194320 | tf_op jit(solution)/shard_map/dynamic_slice | solution.py:205
  14.5 3.3 %collective-permute-start = (bf16[128,2048]{1,0:T(8,128)(2,1)S(1)}, bf16[128,2048]{1,0:T(8,128)(2,1)S(1)}, u32[]{:S(2)}, u32[]{:S(2)}) collective-permute-start(bf16[128,2048]{1,0:T(8,128)(2,1)S(1)} %get-tuple-element.31), channel_id=1, source_target_pairs={{0,8},{4,12},{8,0},{12,4},{1,9},{5,13},{9,1},{13,5},{2,10},{6,14},... | collective-permute-start | bytes 1572872 | tf_op jit(solution)/shard_map/ppermute | solution.py:167
  17.8 3.9 %collective-permute-done.3.a = bf16[256,768]{1,0:T(8,128)(2,1)S(1)} collective-permute-done((bf16[256,768]{1,0:T(8,128)(2,1)S(1)}, bf16[256,768]{1,0:T(8,128)(2,1)S(1)}, u32[]{:S(2)}, u32[]{:S(2)}) %collective-permute-start.3) | collective-permute-done | bytes 393248 | tf_op jit(solution)/shard_map/ppermute | solution.py:180
  21.7 1.9 %collective-permute-start.7 = (bf16[256,768]{1,0:T(8,128)(2,1)S(1)}, bf16[256,768]{1,0:T(8,128)(2,1)S(1)}, u32[]{:S(2)}, u32[]{:S(2)}) collective-permute-start(bf16[256,768]{1,0:T(8,128)(2,1)S(1)} %collective-permute-done.3.a), channel_id=1, source_target_pairs={{0,1},{1,2},{2,3},{3,0},{256,259},{257,256},{258,257},{259,258},{4... | collective-permute-start | bytes 1179656 | tf_op jit(solution)/shard_map/ppermute | solution.py:180
  23.6 6.3 %collective-permute-start.5 = (bf16[256,768]{1,0:T(8,128)(2,1)S(1)}, bf16[256,768]{1,0:T(8,128)(2,1)S(1)}, u32[]{:S(2)}, u32[]{:S(2)}) collective-permute-start(bf16[256,768]{1,0:T(8,128)(2,1)S(1)} %collective-permute-done.3.a), channel_id=1, source_target_pairs={{0,256},{1,257},{2,258},{3,259},{256,0},{257,1},{258,2},{259,3},{4... | collective-permute-start | bytes 1179656 | tf_op jit(solution)/shard_map/ppermute | solution.py:180
  29.9 1.3 collective-permute-done.x2
  31.3 2.4 %collective-permute-start.1 = (bf16[128,2048]{1,0:T(8,128)(2,1)S(1)}, bf16[128,2048]{1,0:T(8,128)(2,1)S(1)}, u32[]{:S(2)}, u32[]{:S(2)}) collective-permute-start(bf16[128,2048]{1,0:T(8,128)(2,1)S(1)} %get-tuple-element.16), channel_id=1, source_target_pairs={{0,4},{4,8},{8,12},{12,0},{1,5},{5,9},{9,13},{13,1},{2,6},{6,10},{... | collective-permute-start | bytes 1572872 | tf_op jit(solution)/shard_map/ppermute | solution.py:167
  33.7 3.5 %collective-permute-start.2 = (bf16[128,2048]{1,0:T(8,128)(2,1)S(1)}, bf16[128,2048]{1,0:T(8,128)(2,1)S(1)}, u32[]{:S(2)}, u32[]{:S(2)}) collective-permute-start(bf16[128,2048]{1,0:T(8,128)(2,1)S(1)} %get-tuple-element.18), channel_id=1, source_target_pairs={{0,12},{4,0},{8,4},{12,8},{1,13},{5,1},{9,5},{13,9},{2,14},{6,2},{... | collective-permute-start | bytes 1572872 | tf_op jit(solution)/shard_map/ppermute | solution.py:167
  37.1 1.9 %collective-permute-start.4 = (bf16[256,768]{1,0:T(8,128)(2,1)S(1)}, bf16[256,768]{1,0:T(8,128)(2,1)S(1)}, u32[]{:S(2)}, u32[]{:S(2)}) collective-permute-start(bf16[256,768]{1,0:T(8,128)(2,1)S(1)} %collective-permute-done.3.a), channel_id=1, source_target_pairs={{0,16},{16,0},{1,17},{17,1},{2,18},{18,2},{3,19},{19,3},{4,20},{20... | collective-permute-start | bytes 1179656 | tf_op jit(solution)/shard_map/ppermute | solution.py:167
  39.1 0.0 collective-permute-done.7.d
  39.1 2.4 %collective-permute-start.8 = (bf16[256,768]{1,0:T(8,128)(2,1)S(1)}, bf16[256,768]{1,0:T(8,128)(2,1)S(1)}, u32[]{:S(2)}, u32[]{:S(2)}) collective-permute-start(bf16[256,768]{1,0:T(8,128)(2,1)S(1)} %collective-permute-done.7.d), channel_id=1, source_target_pairs={{0,16},{16,0},{1,17},{17,1},{2,18},{18,2},{3,19},{19,3},{4,20},{20... | collective-permute-start | bytes 1179656 | tf_op jit(solution)/shard_map/ppermute | solution.py:167
  41.5 2.9 %collective-permute-done.5.b = bf16[256,768]{1,0:T(8,128)(2,1)S(1)} collective-permute-done((bf16[256,768]{1,0:T(8,128)(2,1)S(1)}, bf16[256,768]{1,0:T(8,128)(2,1)S(1)}, u32[]{:S(2)}, u32[]{:S(2)}) %collective-permute-start.5) | collective-permute-done | bytes 393248 | tf_op jit(solution)/shard_map/ppermute | solution.py:180
  44.4 1.9 %collective-permute-start.6 = (bf16[256,768]{1,0:T(8,128)(2,1)S(1)}, bf16[256,768]{1,0:T(8,128)(2,1)S(1)}, u32[]{:S(2)}, u32[]{:S(2)}) collective-permute-start(bf16[256,768]{1,0:T(8,128)(2,1)S(1)} %collective-permute-done.5.b), channel_id=1, source_target_pairs={{0,16},{16,0},{1,17},{17,1},{2,18},{18,2},{3,19},{19,3},{4,20},{20... | collective-permute-start | bytes 1179656 | tf_op jit(solution)/shard_map/ppermute | solution.py:167
  46.3 0.0 collective-permute-done.4.a2
  46.3 0.0 collective-permute-done.1.x1
  46.3 0.0 collective-permute-done.8.d2
  46.3 0.0 copy-done
  46.4 1.3 forward.1
  47.7 1.3 collective-permute-done.2.x3
  49.0 0.0 collective-permute-done.6.b2
  49.0 0.0 copy-start.1
  49.0 0.0 copy-start.2
  49.0 0.7 last_forward.1
  49.7 14.2 %all_to_all.10.parts = bf16[4,128,768]{2,1,0:T(8,128)(2,1)S(1)} all-to-all(bf16[4,128,768]{2,1,0:T(8,128)(2,1)S(1)} %last_forward.1), channel_id=1, replica_groups=mesh['zl'=2,'y'=8,'c'=2,'x'=4,'zh'=4] {'x'}, dimensions={0} | all-to-all | bytes 1572864 | tf_op jit(solution)/shard_map/all_to_all | solution.py:171
  64.0 0.0 copy-done.1
  64.0 0.0 copy-done.2
  64.0 1.5 %attention.1 = bf16[128,768]{1,0:T(8,128)(2,1)S(1)} custom-call(bf16[4,128,768]{2,1,0:T(8,128)(2,1)S(1)} %all_to_all.10.parts, s32[1,128]{1,0:T(1,128)S(1)} %copy-done.2, bf16[128,512]{1,0:T(8,128)(2,1)S(1)} %copy-done.1), custom_call_target="tpu_custom_call" | custom-call | flops 268435456 | bytes 1048576 | tf_op jit(solution)/shard_map/attention/pallas_call | solution.py:236
  65.5 14.3 %all-gather = bf16[512,768]{1,0:T(8,128)(2,1)S(1)} all-gather(bf16[128,768]{1,0:T(8,128)(2,1)S(1)} %attention.1), channel_id=2, replica_groups=mesh['zl'=2,'y'=8,'c'=2,'x'=4,'zh'=4] {'x'}, dimensions={0}, use_global_device_ids=true | all-gather | bytes 983040 | tf_op jit(solution)/shard_map/all_gather | solution.py:243
  79.7 1.4 weight_grad_other_core.1
  81.1 1.9 %collective-permute-start.9 = (bf16[64,24,512]{2,1,0:T(8,128)(2,1)S(1)}, bf16[64,24,512]{2,1,0:T(8,128)(2,1)S(1)}, u32[]{:S(2)}, u32[]{:S(2)}) collective-permute-start(bf16[64,24,512]{2,1,0:T(8,128)(2,1)S(1)} %weight_grad_other_core.1), channel_id=1, source_target_pairs={{0,16},{16,0},{1,17},{17,1},{2,18},{18,2},{3,19},{19,3},{4,20},{20... | collective-permute-start | bytes 4718600 | tf_op jit(solution)/shard_map/ppermute | solution.py:167
  83.1 1.4 weight_grad_this_core.1.mine
  84.4 2.0 %input_grad.1 = (bf16[128,2048]{1,0:T(8,128)(2,1)S(1)}, bf16[128,2048]{1,0:T(8,128)(2,1)S(1)}, bf16[128,2048]{1,0:T(8,128)(2,1)S(1)}, bf16[128,2048]{1,0:T(8,128)(2,1)S(1)}) custom-call(bf16[4,128,768]{2,1,0:T(8,128)(2,1)S(1)} %bitcast.4, bf16[2048,768]{1,0:T(8,128)(2,1)S(1)} %get-tuple-element.20.whole, bf16[256,768]{1,0:T(8,128)(2,1)S(1)} %collective-permute-done.6.b2), custom_call_target="tpu_custom_call" | custom-call | flops 1610612736 | bytes 6291456 | tf_op jit(solution)/shard_map/input_grad/pallas_call | solution.py:255
  86.5 0.0 copy-start.3
  86.5 0.8 copy-done.3
  87.3 0.0 collective-permute-done.9.got
  87.3 1.4 %add_cores.1 = bf16[64,24,512]{2,1,0:T(8,128)(2,1)} custom-call(f32[64,24,512]{2,1,0:T(8,128)S(1)} %weight_grad_this_core.1.mine, bf16[64,24,512]{2,1,0:T(8,128)(2,1)S(1)} %collective-permute-done.9.got), custom_call_target="tpu_custom_call" | custom-call | flops 1048576 | bytes 6291456 | tf_op jit(solution)/shard_map/add_cores/pallas_call | solution.py:272
  88.7 8.2 %all-to-all-start.1 = ((bf16[64,24,512]{2,1,0:T(8,128)(2,1)}), bf16[64,24,512]{2,1,0:T(8,128)(2,1)S(1)}, u32[]{:S(2)}, u32[]{:S(2)}) async-start(bf16[64,24,512]{2,1,0:T(8,128)(2,1)} %add_cores.1), calls=%async_computation.1 | async-start | bytes 3145728 | tf_op jit(solution)/shard_map/all_to_all | solution.py:171
  96.9 2.0 %collective-permute-start.10 = (bf16[128,2048]{1,0:T(8,128)(2,1)}, bf16[128,2048]{1,0:T(8,128)(2,1)S(1)}, u32[]{:S(2)}, u32[]{:S(2)}) collective-permute-start(bf16[128,2048]{1,0:T(8,128)(2,1)} %copy-done.3), channel_id=1, source_target_pairs={{0,12},{4,0},{8,4},{12,8},{1,13},{5,1},{9,5},{13,9},{2,14},{6,2},{... | collective-permute-start | bytes 1572872 | tf_op jit(solution)/shard_map/ppermute | solution.py:167
  98.9 4.6 %collective-permute-start.11 = (bf16[128,2048]{1,0:T(8,128)(2,1)S(1)}, bf16[128,2048]{1,0:T(8,128)(2,1)S(1)}, u32[]{:S(2)}, u32[]{:S(2)}) collective-permute-start(bf16[128,2048]{1,0:T(8,128)(2,1)S(1)} %get-tuple-element.27), channel_id=1, source_target_pairs={{0,8},{4,12},{8,0},{12,4},{1,9},{5,13},{9,1},{13,5},{2,10},{6,14},... | collective-permute-start | bytes 1572872 | tf_op jit(solution)/shard_map/ppermute | solution.py:167
  103.5 3.3 %collective-permute-start.12 = (bf16[128,2048]{1,0:T(8,128)(2,1)S(1)}, bf16[128,2048]{1,0:T(8,128)(2,1)S(1)}, u32[]{:S(2)}, u32[]{:S(2)}) collective-permute-start(bf16[128,2048]{1,0:T(8,128)(2,1)S(1)} %get-tuple-element.28), channel_id=1, source_target_pairs={{0,4},{4,8},{8,12},{12,0},{1,5},{5,9},{9,13},{13,1},{2,6},{6,10},{... | collective-permute-start | bytes 1572872 | tf_op jit(solution)/shard_map/ppermute | solution.py:167
  106.7 18.7 %collective-permute-done.10.refs_1_ = bf16[128,2048]{1,0:T(8,128)(2,1)S(1)} collective-permute-done((bf16[128,2048]{1,0:T(8,128)(2,1)}, bf16[128,2048]{1,0:T(8,128)(2,1)S(1)}, u32[]{:S(2)}, u32[]{:S(2)}) %collective-permute-start.10) | collective-permute-done | bytes 524320 | tf_op jit(solution)/shard_map/ppermute | solution.py:167
  125.5 0.0 collective-permute-done.11.refs_2_
  125.5 2.3 %collective-permute-done.12.refs_3_ = bf16[128,2048]{1,0:T(8,128)(2,1)S(1)} collective-permute-done((bf16[128,2048]{1,0:T(8,128)(2,1)S(1)}, bf16[128,2048]{1,0:T(8,128)(2,1)S(1)}, u32[]{:S(2)}, u32[]{:S(2)}) %collective-permute-start.12) | collective-permute-done | bytes 524320 | tf_op jit(solution)/shard_map/ppermute | solution.py:167
  127.8 1.5 %join_features.1 = bf16[128,8192]{1,0:T(8,128)(2,1)} custom-call(bf16[128,2048]{1,0:T(8,128)(2,1)S(1)} %get-tuple-element.25.refs_0_, bf16[128,2048]{1,0:T(8,128)(2,1)S(1)} %collective-permute-done.10.refs_1_, bf16[128,2048]{1,0:T(8,128)(2,1)S(1)} %collective-permute-done.11.refs_2_, bf16[128,2048]{1,0:T(8,128)(2,1)S(1)} %collective-permute-done.12.refs_3_), custom_call_target="tpu_custom_call" | custom-call | flops 1048576 | bytes 4194304 | tf_op jit(solution)/shard_map/join_features/pallas_call | solution.py:288
  129.3 8.8 %all-to-all-done.1.ref = bf16[64,24,512]{2,1,0:T(8,128)(2,1)S(1)} async-done(((bf16[64,24,512]{2,1,0:T(8,128)(2,1)}), bf16[64,24,512]{2,1,0:T(8,128)(2,1)S(1)}, u32[]{:S(2)}, u32[]{:S(2)}) %all-to-all-start.1) | async-done | bytes 1572896 | tf_op jit(solution)/shard_map/all_to_all | solution.py:171
  138.1 0.9 add_replicas.1
Async XLA Ops:
  1.7 20.1 %collective-permute-start.3 = (bf16[256,768]{1,0:T(8,128)(2,1)S(1)}, bf16[256,768]{1,0:T(8,128)(2,1)S(1)}, u32[]{:S(2)}, u32[]{:S(2)}) collective-permute-start(bf16[256,768]{1,0:T(8,128)(2,1)S(1)} %constant_dynamic-slice_fusion), channel_id=1, source_target_pairs={{0,259},{1,256},{2,257},{3,258},{256,1},{257,2},{258,3},{259,0},{4... | collective-permute-start | bytes 1179656 | tf_op jit(solution)/shard_map/ppermute | solution.py:180
  12.6 33.7 %copy-start = (bf16[512,768]{1,0:T(8,128)(2,1)S(1)}, bf16[512,768]{1,0:T(8,128)(2,1)}, u32[]{:S(2)}) copy-start(bf16[512,768]{1,0:T(8,128)(2,1)} %w0.3) | copy-start | bytes 2359300
  14.5 16.8 %collective-permute-start = (bf16[128,2048]{1,0:T(8,128)(2,1)S(1)}, bf16[128,2048]{1,0:T(8,128)(2,1)S(1)}, u32[]{:S(2)}, u32[]{:S(2)}) collective-permute-start(bf16[128,2048]{1,0:T(8,128)(2,1)S(1)} %get-tuple-element.31), channel_id=1, source_target_pairs={{0,8},{4,12},{8,0},{12,4},{1,9},{5,13},{9,1},{13,5},{2,10},{6,14},... | collective-permute-start | bytes 1572872 | tf_op jit(solution)/shard_map/ppermute | solution.py:167
  21.7 17.3 %collective-permute-start.7 = (bf16[256,768]{1,0:T(8,128)(2,1)S(1)}, bf16[256,768]{1,0:T(8,128)(2,1)S(1)}, u32[]{:S(2)}, u32[]{:S(2)}) collective-permute-start(bf16[256,768]{1,0:T(8,128)(2,1)S(1)} %collective-permute-done.3.a), channel_id=1, source_target_pairs={{0,1},{1,2},{2,3},{3,0},{256,259},{257,256},{258,257},{259,258},{4... | collective-permute-start | bytes 1179656 | tf_op jit(solution)/shard_map/ppermute | solution.py:180
  23.6 20.8 %collective-permute-start.5 = (bf16[256,768]{1,0:T(8,128)(2,1)S(1)}, bf16[256,768]{1,0:T(8,128)(2,1)S(1)}, u32[]{:S(2)}, u32[]{:S(2)}) collective-permute-start(bf16[256,768]{1,0:T(8,128)(2,1)S(1)} %collective-permute-done.3.a), channel_id=1, source_target_pairs={{0,256},{1,257},{2,258},{3,259},{256,0},{257,1},{258,2},{259,3},{4... | collective-permute-start | bytes 1179656 | tf_op jit(solution)/shard_map/ppermute | solution.py:180
  31.3 15.0 %collective-permute-start.1 = (bf16[128,2048]{1,0:T(8,128)(2,1)S(1)}, bf16[128,2048]{1,0:T(8,128)(2,1)S(1)}, u32[]{:S(2)}, u32[]{:S(2)}) collective-permute-start(bf16[128,2048]{1,0:T(8,128)(2,1)S(1)} %get-tuple-element.16), channel_id=1, source_target_pairs={{0,4},{4,8},{8,12},{12,0},{1,5},{5,9},{9,13},{13,1},{2,6},{6,10},{... | collective-permute-start | bytes 1572872 | tf_op jit(solution)/shard_map/ppermute | solution.py:167
  33.7 15.3 %collective-permute-start.2 = (bf16[128,2048]{1,0:T(8,128)(2,1)S(1)}, bf16[128,2048]{1,0:T(8,128)(2,1)S(1)}, u32[]{:S(2)}, u32[]{:S(2)}) collective-permute-start(bf16[128,2048]{1,0:T(8,128)(2,1)S(1)} %get-tuple-element.18), channel_id=1, source_target_pairs={{0,12},{4,0},{8,4},{12,8},{1,13},{5,1},{9,5},{13,9},{2,14},{6,2},{... | collective-permute-start | bytes 1572872 | tf_op jit(solution)/shard_map/ppermute | solution.py:167
  37.1 9.2 %collective-permute-start.4 = (bf16[256,768]{1,0:T(8,128)(2,1)S(1)}, bf16[256,768]{1,0:T(8,128)(2,1)S(1)}, u32[]{:S(2)}, u32[]{:S(2)}) collective-permute-start(bf16[256,768]{1,0:T(8,128)(2,1)S(1)} %collective-permute-done.3.a), channel_id=1, source_target_pairs={{0,16},{16,0},{1,17},{17,1},{2,18},{18,2},{3,19},{19,3},{4,20},{20... | collective-permute-start | bytes 1179656 | tf_op jit(solution)/shard_map/ppermute | solution.py:167
  39.1 7.3 %collective-permute-start.8 = (bf16[256,768]{1,0:T(8,128)(2,1)S(1)}, bf16[256,768]{1,0:T(8,128)(2,1)S(1)}, u32[]{:S(2)}, u32[]{:S(2)}) collective-permute-start(bf16[256,768]{1,0:T(8,128)(2,1)S(1)} %collective-permute-done.7.d), channel_id=1, source_target_pairs={{0,16},{16,0},{1,17},{17,1},{2,18},{18,2},{3,19},{19,3},{4,20},{20... | collective-permute-start | bytes 1179656 | tf_op jit(solution)/shard_map/ppermute | solution.py:167
  44.4 4.6 %collective-permute-start.6 = (bf16[256,768]{1,0:T(8,128)(2,1)S(1)}, bf16[256,768]{1,0:T(8,128)(2,1)S(1)}, u32[]{:S(2)}, u32[]{:S(2)}) collective-permute-start(bf16[256,768]{1,0:T(8,128)(2,1)S(1)} %collective-permute-done.5.b), channel_id=1, source_target_pairs={{0,16},{16,0},{1,17},{17,1},{2,18},{18,2},{3,19},{19,3},{4,20},{20... | collective-permute-start | bytes 1179656 | tf_op jit(solution)/shard_map/ppermute | solution.py:167
  49.0 15.0 %copy-start.1 = (bf16[128,512]{1,0:T(8,128)(2,1)S(1)}, bf16[128,512]{1,0:T(8,128)(2,1)}, u32[]{:S(2)}) copy-start(bf16[128,512]{1,0:T(8,128)(2,1)} %cot_ref.1) | copy-start | bytes 393220
  49.0 15.0 %copy-start.2 = (s32[1,128]{1,0:T(1,128)S(1)}, s32[1,128]{1,0:T(1,128)}, u32[]{:S(2)}) copy-start(s32[1,128]{1,0:T(1,128)} %seg_ref.1) | copy-start | bytes 1540
  81.1 6.2 %collective-permute-start.9 = (bf16[64,24,512]{2,1,0:T(8,128)(2,1)S(1)}, bf16[64,24,512]{2,1,0:T(8,128)(2,1)S(1)}, u32[]{:S(2)}, u32[]{:S(2)}) collective-permute-start(bf16[64,24,512]{2,1,0:T(8,128)(2,1)S(1)} %weight_grad_other_core.1), channel_id=1, source_target_pairs={{0,16},{16,0},{1,17},{17,1},{2,18},{18,2},{3,19},{19,3},{4,20},{20... | collective-permute-start | bytes 4718600 | tf_op jit(solution)/shard_map/ppermute | solution.py:167
  86.5 0.8 copy-start.3
  88.7 49.4 %all-to-all-start.1 = ((bf16[64,24,512]{2,1,0:T(8,128)(2,1)}), bf16[64,24,512]{2,1,0:T(8,128)(2,1)S(1)}, u32[]{:S(2)}, u32[]{:S(2)}) async-start(bf16[64,24,512]{2,1,0:T(8,128)(2,1)} %add_cores.1), calls=%async_computation.1 | async-start | bytes 3145728 | tf_op jit(solution)/shard_map/all_to_all | solution.py:171
  96.9 28.6 %collective-permute-start.10 = (bf16[128,2048]{1,0:T(8,128)(2,1)}, bf16[128,2048]{1,0:T(8,128)(2,1)S(1)}, u32[]{:S(2)}, u32[]{:S(2)}) collective-permute-start(bf16[128,2048]{1,0:T(8,128)(2,1)} %copy-done.3), channel_id=1, source_target_pairs={{0,12},{4,0},{8,4},{12,8},{1,13},{5,1},{9,5},{13,9},{2,14},{6,2},{... | collective-permute-start | bytes 1572872 | tf_op jit(solution)/shard_map/ppermute | solution.py:167
  98.9 26.6 %collective-permute-start.11 = (bf16[128,2048]{1,0:T(8,128)(2,1)S(1)}, bf16[128,2048]{1,0:T(8,128)(2,1)S(1)}, u32[]{:S(2)}, u32[]{:S(2)}) collective-permute-start(bf16[128,2048]{1,0:T(8,128)(2,1)S(1)} %get-tuple-element.27), channel_id=1, source_target_pairs={{0,8},{4,12},{8,0},{12,4},{1,9},{5,13},{9,1},{13,5},{2,10},{6,14},... | collective-permute-start | bytes 1572872 | tf_op jit(solution)/shard_map/ppermute | solution.py:167
  103.5 24.3 %collective-permute-start.12 = (bf16[128,2048]{1,0:T(8,128)(2,1)S(1)}, bf16[128,2048]{1,0:T(8,128)(2,1)S(1)}, u32[]{:S(2)}, u32[]{:S(2)}) collective-permute-start(bf16[128,2048]{1,0:T(8,128)(2,1)S(1)} %get-tuple-element.28), channel_id=1, source_target_pairs={{0,4},{4,8},{8,12},{12,0},{1,5},{5,9},{9,13},{13,1},{2,6},{6,10},{... | collective-permute-start | bytes 1572872 | tf_op jit(solution)/shard_map/ppermute | solution.py:167

commit v7 on v6

--- a/solution.py
+++ b/solution.py
@@ -202,7 +202,11 @@
     c = lax.axis_index("c")
 
     me = lax.axis_index("x")
-    sent = [lax.dynamic_slice_in_dim(inputs, lax.rem(me + k, n) * width, width, 1) for k in range(n)]
+    def cut(value, k):
+        return lax.dynamic_slice_in_dim(value, lax.rem(me + k, n) * width, width, 1)
+
+    opposite, rest = lax.optimization_barrier((cut(inputs, 2), inputs))
+    sent = [cut(rest, 0), cut(rest, 1), opposite, cut(rest, 3)]
     own = lax.dynamic_slice_in_dim(qkv_weight, c * half, half, 0)
     a = across(own)
     x2 = shift(sent[2], "x", 2)

time: 140 us -> 141 us (level)
  transfers between devices with their start and end apart: 14 -> 14, of which waited for: 7 -> 6; matrix products, arithmetic and copies ran while one was open for 1% -> 2% of each run, Pallas kernels for 4% -> 4%
where the time goes in v7:
time: 141 us; the launch traced here: 139 us
  starting transfers between devices  54.4 us (39%)
  waiting for transfers between devices  38.4 us (27%)
  blocking collectives  28.6 us (20%)
  Pallas kernels  12.1 us (9%)
  local copies, waits for them, and re-layouts  4.52 us (3%)
    ppermute x10, starting transfers between devices, shift(): return lax.ppermute(value, axis, [(i, (i + k) % n) for i in range(n)])  27.1 us
    ppermute x10, waiting for transfers between devices, shift(): return lax.ppermute(value, axis, [(i, (i + k) % n) for i in range(n)])  22.4 us
    ppermute x3, starting transfers between devices, z_move(): return lax.ppermute(value, ('zl', 'zh'), pairs)  19.2 us
    all_gather x1, blocking collectives, on_device(): grads = lax.all_gather(grads, 'x', axis=0, tiled=False)  14.4 us
    all_to_all x1, blocking collectives, swap(): return lax.all_to_all(value, axes, 0, 0, tiled=True)  14.3 us
    all_to_all x1, waiting for transfers between devices, swap(): return lax.all_to_all(value, axes, 0, 0, tiled=True)  8.8 us
    all_to_all x1, starting transfers between devices, swap(): return lax.all_to_all(value, axes, 0, 0, tiled=True)  8.11 us
    ppermute x3, waiting for transfers between devices, z_move(): return lax.ppermute(value, ('zl', 'zh'), pairs)  7.26 us
  transfers between devices with their start and end apart: 14, of which 6 were waited for; matrix products, arithmetic and copies ran while one was open for 2% of the time, Pallas kernels for 4%

profile of v7, /device:TPU:6, one launch (start us, length us, event | category | flops | bytes accessed | tf_op | source)
XLA Modules:
  0.0 139.0 jit_solution(1648286609792394629)
XLA Ops:
  0.6 1.0 constant_dynamic-slice_fusion
  1.7 10.9 %collective-permute-start.3 = (bf16[256,768]{1,0:T(8,128)(2,1)S(1)}, bf16[256,768]{1,0:T(8,128)(2,1)S(1)}, u32[]{:S(2)}, u32[]{:S(2)}) collective-permute-start(bf16[256,768]{1,0:T(8,128)(2,1)S(1)} %constant_dynamic-slice_fusion), channel_id=1, source_target_pairs={{0,259},{1,256},{2,257},{3,258},{256,1},{257,2},{258,3},{259,0},{4... | collective-permute-start | bytes 1179656 | tf_op jit(solution)/shard_map/ppermute | solution.py:180
  12.6 0.0 copy-start
  12.6 1.2 constant_dynamic-slice_fusion.4
  13.8 3.3 %collective-permute-start = (bf16[128,2048]{1,0:T(8,128)(2,1)S(1)}, bf16[128,2048]{1,0:T(8,128)(2,1)S(1)}, u32[]{:S(2)}, u32[]{:S(2)}) collective-permute-start(bf16[128,2048]{1,0:T(8,128)(2,1)S(1)} %constant_dynamic-slice_fusion.4), channel_id=1, source_target_pairs={{0,8},{4,12},{8,0},{12,4},{1,9},{5,13},{9,1},{13,5},{2,10},{6,14},... | collective-permute-start | bytes 1572872 | tf_op jit(solution)/shard_map/ppermute | solution.py:167
  17.1 4.6 %collective-permute-done.3.a = bf16[256,768]{1,0:T(8,128)(2,1)S(1)} collective-permute-done((bf16[256,768]{1,0:T(8,128)(2,1)S(1)}, bf16[256,768]{1,0:T(8,128)(2,1)S(1)}, u32[]{:S(2)}, u32[]{:S(2)}) %collective-permute-start.3) | collective-permute-done | bytes 393248 | tf_op jit(solution)/shard_map/ppermute | solution.py:180
  21.7 1.9 %collective-permute-start.7 = (bf16[256,768]{1,0:T(8,128)(2,1)S(1)}, bf16[256,768]{1,0:T(8,128)(2,1)S(1)}, u32[]{:S(2)}, u32[]{:S(2)}) collective-permute-start(bf16[256,768]{1,0:T(8,128)(2,1)S(1)} %collective-permute-done.3.a), channel_id=1, source_target_pairs={{0,1},{1,2},{2,3},{3,0},{256,259},{257,256},{258,257},{259,258},{4... | collective-permute-start | bytes 1179656 | tf_op jit(solution)/shard_map/ppermute | solution.py:180
  23.6 6.3 %collective-permute-start.5 = (bf16[256,768]{1,0:T(8,128)(2,1)S(1)}, bf16[256,768]{1,0:T(8,128)(2,1)S(1)}, u32[]{:S(2)}, u32[]{:S(2)}) collective-permute-start(bf16[256,768]{1,0:T(8,128)(2,1)S(1)} %collective-permute-done.3.a), channel_id=1, source_target_pairs={{0,256},{1,257},{2,258},{3,259},{256,0},{257,1},{258,2},{259,3},{4... | collective-permute-start | bytes 1179656 | tf_op jit(solution)/shard_map/ppermute | solution.py:180
  29.9 1.5 %constant_dynamic-slice_fusion.1 = (bf16[128,2048]{1,0:T(8,128)(2,1)S(1)}, bf16[128,2048]{1,0:T(8,128)(2,1)S(1)}, bf16[128,2048]{1,0:T(8,128)(2,1)S(1)}) fusion(bf16[128,8192]{1,0:T(8,128)(2,1)} %param.4, s32[]{:T(128)S(6)} %select_n.18, s32[]{:T(128)S(6)} %select_n.17, s32[]{:T(128)S(6)} %select_n.16), kind=kLoop, calls=%fused_computation.1 | loop fusion | bytes 3145740 | tf_op jit(solution)/shard_map/dynamic_slice | solution.py:206
  31.5 0.0 collective-permute-done.x2
  31.5 2.4 %collective-permute-start.1 = (bf16[128,2048]{1,0:T(8,128)(2,1)S(1)}, bf16[128,2048]{1,0:T(8,128)(2,1)S(1)}, u32[]{:S(2)}, u32[]{:S(2)}) collective-permute-start(bf16[128,2048]{1,0:T(8,128)(2,1)S(1)} %get-tuple-element.20), channel_id=1, source_target_pairs={{0,4},{4,8},{8,12},{12,0},{1,5},{5,9},{9,13},{13,1},{2,6},{6,10},{... | collective-permute-start | bytes 1572872 | tf_op jit(solution)/shard_map/ppermute | solution.py:167
  33.9 3.5 %collective-permute-start.2 = (bf16[128,2048]{1,0:T(8,128)(2,1)S(1)}, bf16[128,2048]{1,0:T(8,128)(2,1)S(1)}, u32[]{:S(2)}, u32[]{:S(2)}) collective-permute-start(bf16[128,2048]{1,0:T(8,128)(2,1)S(1)} %get-tuple-element.22), channel_id=1, source_target_pairs={{0,12},{4,0},{8,4},{12,8},{1,13},{5,1},{9,5},{13,9},{2,14},{6,2},{... | collective-permute-start | bytes 1572872 | tf_op jit(solution)/shard_map/ppermute | solution.py:167
  37.4 1.9 %collective-permute-start.4 = (bf16[256,768]{1,0:T(8,128)(2,1)S(1)}, bf16[256,768]{1,0:T(8,128)(2,1)S(1)}, u32[]{:S(2)}, u32[]{:S(2)}) collective-permute-start(bf16[256,768]{1,0:T(8,128)(2,1)S(1)} %collective-permute-done.3.a), channel_id=1, source_target_pairs={{0,16},{16,0},{1,17},{17,1},{2,18},{18,2},{3,19},{19,3},{4,20},{20... | collective-permute-start | bytes 1179656 | tf_op jit(solution)/shard_map/ppermute | solution.py:167
  39.3 0.0 collective-permute-done.7.d
  39.3 2.4 %collective-permute-start.8 = (bf16[256,768]{1,0:T(8,128)(2,1)S(1)}, bf16[256,768]{1,0:T(8,128)(2,1)S(1)}, u32[]{:S(2)}, u32[]{:S(2)}) collective-permute-start(bf16[256,768]{1,0:T(8,128)(2,1)S(1)} %collective-permute-done.7.d), channel_id=1, source_target_pairs={{0,16},{16,0},{1,17},{17,1},{2,18},{18,2},{3,19},{19,3},{4,20},{20... | collective-permute-start | bytes 1179656 | tf_op jit(solution)/shard_map/ppermute | solution.py:167
  41.7 2.7 %collective-permute-done.5.b = bf16[256,768]{1,0:T(8,128)(2,1)S(1)} collective-permute-done((bf16[256,768]{1,0:T(8,128)(2,1)S(1)}, bf16[256,768]{1,0:T(8,128)(2,1)S(1)}, u32[]{:S(2)}, u32[]{:S(2)}) %collective-permute-start.5) | collective-permute-done | bytes 393248 | tf_op jit(solution)/shard_map/ppermute | solution.py:180
  44.4 1.9 %collective-permute-start.6 = (bf16[256,768]{1,0:T(8,128)(2,1)S(1)}, bf16[256,768]{1,0:T(8,128)(2,1)S(1)}, u32[]{:S(2)}, u32[]{:S(2)}) collective-permute-start(bf16[256,768]{1,0:T(8,128)(2,1)S(1)} %collective-permute-done.5.b), channel_id=1, source_target_pairs={{0,16},{16,0},{1,17},{17,1},{2,18},{18,2},{3,19},{19,3},{4,20},{20... | collective-permute-start | bytes 1179656 | tf_op jit(solution)/shard_map/ppermute | solution.py:167
  46.3 0.0 collective-permute-done.4.a2
  46.3 0.0 collective-permute-done.1.x1
  46.3 0.0 collective-permute-done.8.d2
  46.3 0.0 copy-done
  46.4 1.3 forward.1
  47.7 1.3 collective-permute-done.2.x3
  49.0 0.0 collective-permute-done.6.b2
  49.0 0.0 copy-start.1
  49.0 0.0 copy-start.2
  49.0 0.7 last_forward.1
  49.7 14.3 %all_to_all.10.parts = bf16[4,128,768]{2,1,0:T(8,128)(2,1)S(1)} all-to-all(bf16[4,128,768]{2,1,0:T(8,128)(2,1)S(1)} %last_forward.1), channel_id=1, replica_groups=mesh['zl'=2,'y'=8,'c'=2,'x'=4,'zh'=4] {'x'}, dimensions={0} | all-to-all | bytes 1572864 | tf_op jit(solution)/shard_map/all_to_all | solution.py:171
  64.0 0.0 copy-done.1
  64.0 0.0 copy-done.2
  64.0 1.5 %attention.1 = bf16[128,768]{1,0:T(8,128)(2,1)S(1)} custom-call(bf16[4,128,768]{2,1,0:T(8,128)(2,1)S(1)} %all_to_all.10.parts, s32[1,128]{1,0:T(1,128)S(1)} %copy-done.2, bf16[128,512]{1,0:T(8,128)(2,1)S(1)} %copy-done.1), custom_call_target="tpu_custom_call" | custom-call | flops 268435456 | bytes 1048576 | tf_op jit(solution)/shard_map/attention/pallas_call | solution.py:240
  65.5 14.4 %all-gather = bf16[512,768]{1,0:T(8,128)(2,1)S(1)} all-gather(bf16[128,768]{1,0:T(8,128)(2,1)S(1)} %attention.1), channel_id=2, replica_groups=mesh['zl'=2,'y'=8,'c'=2,'x'=4,'zh'=4] {'x'}, dimensions={0}, use_global_device_ids=true | all-gather | bytes 983040 | tf_op jit(solution)/shard_map/all_gather | solution.py:247
  79.8 1.4 weight_grad_other_core.1
  81.2 1.9 %collective-permute-start.9 = (bf16[64,24,512]{2,1,0:T(8,128)(2,1)S(1)}, bf16[64,24,512]{2,1,0:T(8,128)(2,1)S(1)}, u32[]{:S(2)}, u32[]{:S(2)}) collective-permute-start(bf16[64,24,512]{2,1,0:T(8,128)(2,1)S(1)} %weight_grad_other_core.1), channel_id=1, source_target_pairs={{0,16},{16,0},{1,17},{17,1},{2,18},{18,2},{3,19},{19,3},{4,20},{20... | collective-permute-start | bytes 4718600 | tf_op jit(solution)/shard_map/ppermute | solution.py:167
  83.1 1.4 weight_grad_this_core.1.mine
  84.5 2.0 %input_grad.1 = (bf16[128,2048]{1,0:T(8,128)(2,1)S(1)}, bf16[128,2048]{1,0:T(8,128)(2,1)S(1)}, bf16[128,2048]{1,0:T(8,128)(2,1)S(1)}, bf16[128,2048]{1,0:T(8,128)(2,1)S(1)}) custom-call(bf16[4,128,768]{2,1,0:T(8,128)(2,1)S(1)} %bitcast.4, bf16[2048,768]{1,0:T(8,128)(2,1)S(1)} %get-tuple-element.24.whole, bf16[256,768]{1,0:T(8,128)(2,1)S(1)} %collective-permute-done.6.b2), custom_call_target="tpu_custom_call" | custom-call | flops 1610612736 | bytes 6291456 | tf_op jit(solution)/shard_map/input_grad/pallas_call | solution.py:259
  86.6 0.0 copy-start.3
  86.6 0.8 copy-done.3
  87.4 0.0 collective-permute-done.9.got
  87.4 1.4 %add_cores.1 = bf16[64,24,512]{2,1,0:T(8,128)(2,1)} custom-call(f32[64,24,512]{2,1,0:T(8,128)S(1)} %weight_grad_this_core.1.mine, bf16[64,24,512]{2,1,0:T(8,128)(2,1)S(1)} %collective-permute-done.9.got), custom_call_target="tpu_custom_call" | custom-call | flops 1048576 | bytes 6291456 | tf_op jit(solution)/shard_map/add_cores/pallas_call | solution.py:276
  88.8 8.1 %all-to-all-start.1 = ((bf16[64,24,512]{2,1,0:T(8,128)(2,1)}), bf16[64,24,512]{2,1,0:T(8,128)(2,1)S(1)}, u32[]{:S(2)}, u32[]{:S(2)}) async-start(bf16[64,24,512]{2,1,0:T(8,128)(2,1)} %add_cores.1), calls=%async_computation.1 | async-start | bytes 3145728 | tf_op jit(solution)/shard_map/all_to_all | solution.py:171
  96.9 2.3 %collective-permute-start.10 = (bf16[128,2048]{1,0:T(8,128)(2,1)}, bf16[128,2048]{1,0:T(8,128)(2,1)S(1)}, u32[]{:S(2)}, u32[]{:S(2)}) collective-permute-start(bf16[128,2048]{1,0:T(8,128)(2,1)} %copy-done.3), channel_id=1, source_target_pairs={{0,12},{4,0},{8,4},{12,8},{1,13},{5,1},{9,5},{13,9},{2,14},{6,2},{... | collective-permute-start | bytes 1572872 | tf_op jit(solution)/shard_map/ppermute | solution.py:167
  99.2 4.6 %collective-permute-start.11 = (bf16[128,2048]{1,0:T(8,128)(2,1)S(1)}, bf16[128,2048]{1,0:T(8,128)(2,1)S(1)}, u32[]{:S(2)}, u32[]{:S(2)}) collective-permute-start(bf16[128,2048]{1,0:T(8,128)(2,1)S(1)} %get-tuple-element.31), channel_id=1, source_target_pairs={{0,8},{4,12},{8,0},{12,4},{1,9},{5,13},{9,1},{13,5},{2,10},{6,14},... | collective-permute-start | bytes 1572872 | tf_op jit(solution)/shard_map/ppermute | solution.py:167
  103.8 3.0 %collective-permute-start.12 = (bf16[128,2048]{1,0:T(8,128)(2,1)S(1)}, bf16[128,2048]{1,0:T(8,128)(2,1)S(1)}, u32[]{:S(2)}, u32[]{:S(2)}) collective-permute-start(bf16[128,2048]{1,0:T(8,128)(2,1)S(1)} %get-tuple-element.32), channel_id=1, source_target_pairs={{0,4},{4,8},{8,12},{12,0},{1,5},{5,9},{9,13},{13,1},{2,6},{6,10},{... | collective-permute-start | bytes 1572872 | tf_op jit(solution)/shard_map/ppermute | solution.py:167
  106.8 18.8 %collective-permute-done.10.refs_1_ = bf16[128,2048]{1,0:T(8,128)(2,1)S(1)} collective-permute-done((bf16[128,2048]{1,0:T(8,128)(2,1)}, bf16[128,2048]{1,0:T(8,128)(2,1)S(1)}, u32[]{:S(2)}, u32[]{:S(2)}) %collective-permute-start.10) | collective-permute-done | bytes 524320 | tf_op jit(solution)/shard_map/ppermute | solution.py:167
  125.5 0.0 collective-permute-done.11.refs_2_
  125.5 2.3 %collective-permute-done.12.refs_3_ = bf16[128,2048]{1,0:T(8,128)(2,1)S(1)} collective-permute-done((bf16[128,2048]{1,0:T(8,128)(2,1)S(1)}, bf16[128,2048]{1,0:T(8,128)(2,1)S(1)}, u32[]{:S(2)}, u32[]{:S(2)}) %collective-permute-start.12) | collective-permute-done | bytes 524320 | tf_op jit(solution)/shard_map/ppermute | solution.py:167
  127.8 1.5 %join_features.1 = bf16[128,8192]{1,0:T(8,128)(2,1)} custom-call(bf16[128,2048]{1,0:T(8,128)(2,1)S(1)} %get-tuple-element.29.refs_0_, bf16[128,2048]{1,0:T(8,128)(2,1)S(1)} %collective-permute-done.10.refs_1_, bf16[128,2048]{1,0:T(8,128)(2,1)S(1)} %collective-permute-done.11.refs_2_, bf16[128,2048]{1,0:T(8,128)(2,1)S(1)} %collective-permute-done.12.refs_3_), custom_call_target="tpu_custom_call" | custom-call | flops 1048576 | bytes 4194304 | tf_op jit(solution)/shard_map/join_features/pallas_call | solution.py:292
  129.3 8.8 %all-to-all-done.1.ref = bf16[64,24,512]{2,1,0:T(8,128)(2,1)S(1)} async-done(((bf16[64,24,512]{2,1,0:T(8,128)(2,1)}), bf16[64,24,512]{2,1,0:T(8,128)(2,1)S(1)}, u32[]{:S(2)}, u32[]{:S(2)}) %all-to-all-start.1) | async-done | bytes 1572896 | tf_op jit(solution)/shard_map/all_to_all | solution.py:171
  138.1 0.9 add_replicas.1
Async XLA Ops:
  1.7 20.1 %collective-permute-start.3 = (bf16[256,768]{1,0:T(8,128)(2,1)S(1)}, bf16[256,768]{1,0:T(8,128)(2,1)S(1)}, u32[]{:S(2)}, u32[]{:S(2)}) collective-permute-start(bf16[256,768]{1,0:T(8,128)(2,1)S(1)} %constant_dynamic-slice_fusion), channel_id=1, source_target_pairs={{0,259},{1,256},{2,257},{3,258},{256,1},{257,2},{258,3},{259,0},{4... | collective-permute-start | bytes 1179656 | tf_op jit(solution)/shard_map/ppermute | solution.py:180
  12.6 33.7 %copy-start = (bf16[512,768]{1,0:T(8,128)(2,1)S(1)}, bf16[512,768]{1,0:T(8,128)(2,1)}, u32[]{:S(2)}) copy-start(bf16[512,768]{1,0:T(8,128)(2,1)} %w0.3) | copy-start | bytes 2359300
  13.8 17.7 %collective-permute-start = (bf16[128,2048]{1,0:T(8,128)(2,1)S(1)}, bf16[128,2048]{1,0:T(8,128)(2,1)S(1)}, u32[]{:S(2)}, u32[]{:S(2)}) collective-permute-start(bf16[128,2048]{1,0:T(8,128)(2,1)S(1)} %constant_dynamic-slice_fusion.4), channel_id=1, source_target_pairs={{0,8},{4,12},{8,0},{12,4},{1,9},{5,13},{9,1},{13,5},{2,10},{6,14},... | collective-permute-start | bytes 1572872 | tf_op jit(solution)/shard_map/ppermute | solution.py:167
  21.7 17.6 %collective-permute-start.7 = (bf16[256,768]{1,0:T(8,128)(2,1)S(1)}, bf16[256,768]{1,0:T(8,128)(2,1)S(1)}, u32[]{:S(2)}, u32[]{:S(2)}) collective-permute-start(bf16[256,768]{1,0:T(8,128)(2,1)S(1)} %collective-permute-done.3.a), channel_id=1, source_target_pairs={{0,1},{1,2},{2,3},{3,0},{256,259},{257,256},{258,257},{259,258},{4... | collective-permute-start | bytes 1179656 | tf_op jit(solution)/shard_map/ppermute | solution.py:180
  23.6 20.8 %collective-permute-start.5 = (bf16[256,768]{1,0:T(8,128)(2,1)S(1)}, bf16[256,768]{1,0:T(8,128)(2,1)S(1)}, u32[]{:S(2)}, u32[]{:S(2)}) collective-permute-start(bf16[256,768]{1,0:T(8,128)(2,1)S(1)} %collective-permute-done.3.a), channel_id=1, source_target_pairs={{0,256},{1,257},{2,258},{3,259},{256,0},{257,1},{258,2},{259,3},{4... | collective-permute-start | bytes 1179656 | tf_op jit(solution)/shard_map/ppermute | solution.py:180
  31.5 14.8 %collective-permute-start.1 = (bf16[128,2048]{1,0:T(8,128)(2,1)S(1)}, bf16[128,2048]{1,0:T(8,128)(2,1)S(1)}, u32[]{:S(2)}, u32[]{:S(2)}) collective-permute-start(bf16[128,2048]{1,0:T(8,128)(2,1)S(1)} %get-tuple-element.20), channel_id=1, source_target_pairs={{0,4},{4,8},{8,12},{12,0},{1,5},{5,9},{9,13},{13,1},{2,6},{6,10},{... | collective-permute-start | bytes 1572872 | tf_op jit(solution)/shard_map/ppermute | solution.py:167
  33.9 15.1 %collective-permute-start.2 = (bf16[128,2048]{1,0:T(8,128)(2,1)S(1)}, bf16[128,2048]{1,0:T(8,128)(2,1)S(1)}, u32[]{:S(2)}, u32[]{:S(2)}) collective-permute-start(bf16[128,2048]{1,0:T(8,128)(2,1)S(1)} %get-tuple-element.22), channel_id=1, source_target_pairs={{0,12},{4,0},{8,4},{12,8},{1,13},{5,1},{9,5},{13,9},{2,14},{6,2},{... | collective-permute-start | bytes 1572872 | tf_op jit(solution)/shard_map/ppermute | solution.py:167
  37.4 9.0 %collective-permute-start.4 = (bf16[256,768]{1,0:T(8,128)(2,1)S(1)}, bf16[256,768]{1,0:T(8,128)(2,1)S(1)}, u32[]{:S(2)}, u32[]{:S(2)}) collective-permute-start(bf16[256,768]{1,0:T(8,128)(2,1)S(1)} %collective-permute-done.3.a), channel_id=1, source_target_pairs={{0,16},{16,0},{1,17},{17,1},{2,18},{18,2},{3,19},{19,3},{4,20},{20... | collective-permute-start | bytes 1179656 | tf_op jit(solution)/shard_map/ppermute | solution.py:167
  39.3 7.0 %collective-permute-start.8 = (bf16[256,768]{1,0:T(8,128)(2,1)S(1)}, bf16[256,768]{1,0:T(8,128)(2,1)S(1)}, u32[]{:S(2)}, u32[]{:S(2)}) collective-permute-start(bf16[256,768]{1,0:T(8,128)(2,1)S(1)} %collective-permute-done.7.d), channel_id=1, source_target_pairs={{0,16},{16,0},{1,17},{17,1},{2,18},{18,2},{3,19},{19,3},{4,20},{20... | collective-permute-start | bytes 1179656 | tf_op jit(solution)/shard_map/ppermute | solution.py:167
  44.4 4.6 %collective-permute-start.6 = (bf16[256,768]{1,0:T(8,128)(2,1)S(1)}, bf16[256,768]{1,0:T(8,128)(2,1)S(1)}, u32[]{:S(2)}, u32[]{:S(2)}) collective-permute-start(bf16[256,768]{1,0:T(8,128)(2,1)S(1)} %collective-permute-done.5.b), channel_id=1, source_target_pairs={{0,16},{16,0},{1,17},{17,1},{2,18},{18,2},{3,19},{19,3},{4,20},{20... | collective-permute-start | bytes 1179656 | tf_op jit(solution)/shard_map/ppermute | solution.py:167
  49.0 15.0 %copy-start.1 = (bf16[128,512]{1,0:T(8,128)(2,1)S(1)}, bf16[128,512]{1,0:T(8,128)(2,1)}, u32[]{:S(2)}) copy-start(bf16[128,512]{1,0:T(8,128)(2,1)} %cot_ref.1) | copy-start | bytes 393220
  49.0 15.0 %copy-start.2 = (s32[1,128]{1,0:T(1,128)S(1)}, s32[1,128]{1,0:T(1,128)}, u32[]{:S(2)}) copy-start(s32[1,128]{1,0:T(1,128)} %seg_ref.1) | copy-start | bytes 1540
  81.2 6.2 %collective-permute-start.9 = (bf16[64,24,512]{2,1,0:T(8,128)(2,1)S(1)}, bf16[64,24,512]{2,1,0:T(8,128)(2,1)S(1)}, u32[]{:S(2)}, u32[]{:S(2)}) collective-permute-start(bf16[64,24,512]{2,1,0:T(8,128)(2,1)S(1)} %weight_grad_other_core.1), channel_id=1, source_target_pairs={{0,16},{16,0},{1,17},{17,1},{2,18},{18,2},{3,19},{19,3},{4,20},{20... | collective-permute-start | bytes 4718600 | tf_op jit(solution)/shard_map/ppermute | solution.py:167
  86.6 0.8 copy-start.3
  88.8 49.3 %all-to-all-start.1 = ((bf16[64,24,512]{2,1,0:T(8,128)(2,1)}), bf16[64,24,512]{2,1,0:T(8,128)(2,1)S(1)}, u32[]{:S(2)}, u32[]{:S(2)}) async-start(bf16[64,24,512]{2,1,0:T(8,128)(2,1)} %add_cores.1), calls=%async_computation.1 | async-start | bytes 3145728 | tf_op jit(solution)/shard_map/all_to_all | solution.py:171
  96.9 28.6 %collective-permute-start.10 = (bf16[128,2048]{1,0:T(8,128)(2,1)}, bf16[128,2048]{1,0:T(8,128)(2,1)S(1)}, u32[]{:S(2)}, u32[]{:S(2)}) collective-permute-start(bf16[128,2048]{1,0:T(8,128)(2,1)} %copy-done.3), channel_id=1, source_target_pairs={{0,12},{4,0},{8,4},{12,8},{1,13},{5,1},{9,5},{13,9},{2,14},{6,2},{... | collective-permute-start | bytes 1572872 | tf_op jit(solution)/shard_map/ppermute | solution.py:167
  99.2 26.3 %collective-permute-start.11 = (bf16[128,2048]{1,0:T(8,128)(2,1)S(1)}, bf16[128,2048]{1,0:T(8,128)(2,1)S(1)}, u32[]{:S(2)}, u32[]{:S(2)}) collective-permute-start(bf16[128,2048]{1,0:T(8,128)(2,1)S(1)} %get-tuple-element.31), channel_id=1, source_target_pairs={{0,8},{4,12},{8,0},{12,4},{1,9},{5,13},{9,1},{13,5},{2,10},{6,14},... | collective-permute-start | bytes 1572872 | tf_op jit(solution)/shard_map/ppermute | solution.py:167
  103.8 24.1 %collective-permute-start.12 = (bf16[128,2048]{1,0:T(8,128)(2,1)S(1)}, bf16[128,2048]{1,0:T(8,128)(2,1)S(1)}, u32[]{:S(2)}, u32[]{:S(2)}) collective-permute-start(bf16[128,2048]{1,0:T(8,128)(2,1)S(1)} %get-tuple-element.32), channel_id=1, source_target_pairs={{0,4},{4,8},{8,12},{12,0},{1,5},{5,9},{9,13},{13,1},{2,6},{6,10},{... | collective-permute-start | bytes 1572872 | tf_op jit(solution)/shard_map/ppermute | solution.py:167

commit v8 on v7

--- a/solution.py
+++ b/solution.py
@@ -206,9 +206,9 @@
         return lax.dynamic_slice_in_dim(value, lax.rem(me + k, n) * width, width, 1)
 
     opposite, rest = lax.optimization_barrier((cut(inputs, 2), inputs))
-    sent = [cut(rest, 0), cut(rest, 1), opposite, cut(rest, 3)]
     own = lax.dynamic_slice_in_dim(qkv_weight, c * half, half, 0)
-    a = across(own)
+    a, same, ahead, behind = lax.optimization_barrier((across(own), cut(rest, 0), cut(rest, 1), cut(rest, 3)))
+    sent = [same, ahead, opposite, behind]
     x2 = shift(sent[2], "x", 2)
     x2, ahead, behind = lax.optimization_barrier((x2, sent[1], sent[3]))
     x1 = shift(ahead, "x", 1)

time: 141 us -> 141 us (level)
  transfers between devices with their start and end apart: 14 -> 14, of which waited for: 6 -> 8; matrix products, arithmetic and copies ran while one was open for 2% -> 2% of each run, Pallas kernels for 4% -> 4%
where the time goes in v8:
time: 141 us; the launch traced here: 139 us
  starting transfers between devices  54.5 us (39%)
  waiting for transfers between devices  37.8 us (27%)
  blocking collectives  29 us (21%)
  Pallas kernels  12.1 us (9%)
  local copies, waits for them, and re-layouts  4.52 us (3%)
    ppermute x10, starting transfers between devices, shift(): return lax.ppermute(value, axis, [(i, (i + k) % n) for i in range(n)])  27.1 us
    ppermute x10, waiting for transfers between devices, shift(): return lax.ppermute(value, axis, [(i, (i + k) % n) for i in range(n)])  22.3 us
    ppermute x3, starting transfers between devices, z_move(): return lax.ppermute(value, ('zl', 'zh'), pairs)  19.2 us
    all_to_all x1, blocking collectives, swap(): return lax.all_to_all(value, axes, 0, 0, tiled=True)  15 us
    all_gather x1, blocking collectives, on_device(): grads = lax.all_gather(grads, 'x', axis=0, tiled=False)  14.1 us
    all_to_all x1, waiting for transfers between devices, swap(): return lax.all_to_all(value, axes, 0, 0, tiled=True)  8.8 us
    all_to_all x1, starting transfers between devices, swap(): return lax.all_to_all(value, axes, 0, 0, tiled=True)  8.19 us
    ppermute x3, waiting for transfers between devices, z_move(): return lax.ppermute(value, ('zl', 'zh'), pairs)  6.65 us
  transfers between devices with their start and end apart: 14, of which 8 were waited for; matrix products, arithmetic and copies ran while one was open for 2% of the time, Pallas kernels for 4%

profile of v8, /device:TPU:6, one launch (start us, length us, event | category | flops | bytes accessed | tf_op | source)
XLA Modules:
  0.0 138.8 jit_solution(7046921101007883854)
XLA Ops:
  0.6 1.0 constant_dynamic-slice_fusion.4
  1.7 10.9 %collective-permute-start = (bf16[256,768]{1,0:T(8,128)(2,1)S(1)}, bf16[256,768]{1,0:T(8,128)(2,1)S(1)}, u32[]{:S(2)}, u32[]{:S(2)}) collective-permute-start(bf16[256,768]{1,0:T(8,128)(2,1)S(1)} %constant_dynamic-slice_fusion.4), channel_id=1, source_target_pairs={{0,259},{1,256},{2,257},{3,258},{256,1},{257,2},{258,3},{259,0},{4... | collective-permute-start | bytes 1179656 | tf_op jit(solution)/shard_map/ppermute | solution.py:180
  12.6 0.0 copy-start
  12.6 1.2 constant_dynamic-slice_fusion.3
  13.8 3.3 %collective-permute-start.1 = (bf16[128,2048]{1,0:T(8,128)(2,1)S(1)}, bf16[128,2048]{1,0:T(8,128)(2,1)S(1)}, u32[]{:S(2)}, u32[]{:S(2)}) collective-permute-start(bf16[128,2048]{1,0:T(8,128)(2,1)S(1)} %constant_dynamic-slice_fusion.3), channel_id=1, source_target_pairs={{0,8},{4,12},{8,0},{12,4},{1,9},{5,13},{9,1},{13,5},{2,10},{6,14},... | collective-permute-start | bytes 1572872 | tf_op jit(solution)/shard_map/ppermute | solution.py:167
  17.1 1.5 %constant_dynamic-slice_fusion = (bf16[128,2048]{1,0:T(8,128)(2,1)S(1)}, bf16[128,2048]{1,0:T(8,128)(2,1)S(1)}, bf16[128,2048]{1,0:T(8,128)(2,1)S(1)}) fusion(bf16[128,8192]{1,0:T(8,128)(2,1)} %param.4, s32[]{:T(128)S(6)} %select_n.19, s32[]{:T(128)S(6)} %select_n.18, s32[]{:T(128)S(6)} %select_n.17), kind=kLoop, calls=%fused_computation | loop fusion | bytes 3145740 | tf_op jit(solution)/shard_map/dynamic_slice | solution.py:206
  18.7 3.0 %collective-permute-done.a = bf16[256,768]{1,0:T(8,128)(2,1)S(1)} collective-permute-done((bf16[256,768]{1,0:T(8,128)(2,1)S(1)}, bf16[256,768]{1,0:T(8,128)(2,1)S(1)}, u32[]{:S(2)}, u32[]{:S(2)}) %collective-permute-start) | collective-permute-done | bytes 393248 | tf_op jit(solution)/shard_map/ppermute | solution.py:180
  21.7 1.9 %collective-permute-start.7 = (bf16[256,768]{1,0:T(8,128)(2,1)S(1)}, bf16[256,768]{1,0:T(8,128)(2,1)S(1)}, u32[]{:S(2)}, u32[]{:S(2)}) collective-permute-start(bf16[256,768]{1,0:T(8,128)(2,1)S(1)} %collective-permute-done.a), channel_id=1, source_target_pairs={{0,1},{1,2},{2,3},{3,0},{256,259},{257,256},{258,257},{259,258},{4... | collective-permute-start | bytes 1179656 | tf_op jit(solution)/shard_map/ppermute | solution.py:180
  23.6 6.3 %collective-permute-start.5 = (bf16[256,768]{1,0:T(8,128)(2,1)S(1)}, bf16[256,768]{1,0:T(8,128)(2,1)S(1)}, u32[]{:S(2)}, u32[]{:S(2)}) collective-permute-start(bf16[256,768]{1,0:T(8,128)(2,1)S(1)} %collective-permute-done.a), channel_id=1, source_target_pairs={{0,256},{1,257},{2,258},{3,259},{256,0},{257,1},{258,2},{259,3},{4... | collective-permute-start | bytes 1179656 | tf_op jit(solution)/shard_map/ppermute | solution.py:180
  29.9 0.6 collective-permute-done.1.x2
  30.6 2.4 %collective-permute-start.2 = (bf16[128,2048]{1,0:T(8,128)(2,1)S(1)}, bf16[128,2048]{1,0:T(8,128)(2,1)S(1)}, u32[]{:S(2)}, u32[]{:S(2)}) collective-permute-start(bf16[128,2048]{1,0:T(8,128)(2,1)S(1)} %get-tuple-element.27), channel_id=1, source_target_pairs={{0,4},{4,8},{8,12},{12,0},{1,5},{5,9},{9,13},{13,1},{2,6},{6,10},{... | collective-permute-start | bytes 1572872 | tf_op jit(solution)/shard_map/ppermute | solution.py:167
  33.0 3.5 %collective-permute-start.3 = (bf16[128,2048]{1,0:T(8,128)(2,1)S(1)}, bf16[128,2048]{1,0:T(8,128)(2,1)S(1)}, u32[]{:S(2)}, u32[]{:S(2)}) collective-permute-start(bf16[128,2048]{1,0:T(8,128)(2,1)S(1)} %get-tuple-element.29), channel_id=1, source_target_pairs={{0,12},{4,0},{8,4},{12,8},{1,13},{5,1},{9,5},{13,9},{2,14},{6,2},{... | collective-permute-start | bytes 1572872 | tf_op jit(solution)/shard_map/ppermute | solution.py:167
  36.4 1.9 %collective-permute-start.4 = (bf16[256,768]{1,0:T(8,128)(2,1)S(1)}, bf16[256,768]{1,0:T(8,128)(2,1)S(1)}, u32[]{:S(2)}, u32[]{:S(2)}) collective-permute-start(bf16[256,768]{1,0:T(8,128)(2,1)S(1)} %collective-permute-done.a), channel_id=1, source_target_pairs={{0,16},{16,0},{1,17},{17,1},{2,18},{18,2},{3,19},{19,3},{4,20},{20... | collective-permute-start | bytes 1179656 | tf_op jit(solution)/shard_map/ppermute | solution.py:167
  38.4 0.0 collective-permute-done.7.d
  38.4 2.4 %collective-permute-start.8 = (bf16[256,768]{1,0:T(8,128)(2,1)S(1)}, bf16[256,768]{1,0:T(8,128)(2,1)S(1)}, u32[]{:S(2)}, u32[]{:S(2)}) collective-permute-start(bf16[256,768]{1,0:T(8,128)(2,1)S(1)} %collective-permute-done.7.d), channel_id=1, source_target_pairs={{0,16},{16,0},{1,17},{17,1},{2,18},{18,2},{3,19},{19,3},{4,20},{20... | collective-permute-start | bytes 1179656 | tf_op jit(solution)/shard_map/ppermute | solution.py:167
  40.8 3.6 %collective-permute-done.5.b = bf16[256,768]{1,0:T(8,128)(2,1)S(1)} collective-permute-done((bf16[256,768]{1,0:T(8,128)(2,1)S(1)}, bf16[256,768]{1,0:T(8,128)(2,1)S(1)}, u32[]{:S(2)}, u32[]{:S(2)}) %collective-permute-start.5) | collective-permute-done | bytes 393248 | tf_op jit(solution)/shard_map/ppermute | solution.py:180
  44.4 1.9 %collective-permute-start.6 = (bf16[256,768]{1,0:T(8,128)(2,1)S(1)}, bf16[256,768]{1,0:T(8,128)(2,1)S(1)}, u32[]{:S(2)}, u32[]{:S(2)}) collective-permute-start(bf16[256,768]{1,0:T(8,128)(2,1)S(1)} %collective-permute-done.5.b), channel_id=1, source_target_pairs={{0,16},{16,0},{1,17},{17,1},{2,18},{18,2},{3,19},{19,3},{4,20},{20... | collective-permute-start | bytes 1179656 | tf_op jit(solution)/shard_map/ppermute | solution.py:167
  46.3 0.0 collective-permute-done.4.a2
  46.3 0.0 collective-permute-done.2.x1
  46.3 0.0 collective-permute-done.8.d2
  46.3 0.0 copy-done
  46.4 1.3 forward.1
  47.7 0.6 collective-permute-done.3.x3
  48.3 0.0 collective-permute-done.6.b2
  48.3 0.0 copy-start.1
  48.3 0.0 copy-start.2
  48.3 0.7 last_forward.1
  49.0 15.0 %all_to_all.10.parts = bf16[4,128,768]{2,1,0:T(8,128)(2,1)S(1)} all-to-all(bf16[4,128,768]{2,1,0:T(8,128)(2,1)S(1)} %last_forward.1), channel_id=1, replica_groups=mesh['zl'=2,'y'=8,'c'=2,'x'=4,'zh'=4] {'x'}, dimensions={0} | all-to-all | bytes 1572864 | tf_op jit(solution)/shard_map/all_to_all | solution.py:171
  64.0 0.0 copy-done.1
  64.0 0.0 copy-done.2
  64.0 1.5 %attention.1 = bf16[128,768]{1,0:T(8,128)(2,1)S(1)} custom-call(bf16[4,128,768]{2,1,0:T(8,128)(2,1)S(1)} %all_to_all.10.parts, s32[1,128]{1,0:T(1,128)S(1)} %copy-done.2, bf16[128,512]{1,0:T(8,128)(2,1)S(1)} %copy-done.1), custom_call_target="tpu_custom_call" | custom-call | flops 268435456 | bytes 1048576 | tf_op jit(solution)/shard_map/attention/pallas_call | solution.py:240
  65.5 14.1 %all-gather = bf16[512,768]{1,0:T(8,128)(2,1)S(1)} all-gather(bf16[128,768]{1,0:T(8,128)(2,1)S(1)} %attention.1), channel_id=2, replica_groups=mesh['zl'=2,'y'=8,'c'=2,'x'=4,'zh'=4] {'x'}, dimensions={0}, use_global_device_ids=true | all-gather | bytes 983040 | tf_op jit(solution)/shard_map/all_gather | solution.py:247
  79.5 1.4 weight_grad_other_core.1
  80.9 1.9 %collective-permute-start.9 = (bf16[64,24,512]{2,1,0:T(8,128)(2,1)S(1)}, bf16[64,24,512]{2,1,0:T(8,128)(2,1)S(1)}, u32[]{:S(2)}, u32[]{:S(2)}) collective-permute-start(bf16[64,24,512]{2,1,0:T(8,128)(2,1)S(1)} %weight_grad_other_core.1), channel_id=1, source_target_pairs={{0,16},{16,0},{1,17},{17,1},{2,18},{18,2},{3,19},{19,3},{4,20},{20... | collective-permute-start | bytes 4718600 | tf_op jit(solution)/shard_map/ppermute | solution.py:167
  82.9 1.4 weight_grad_this_core.1.mine
  84.2 2.0 %input_grad.1 = (bf16[128,2048]{1,0:T(8,128)(2,1)S(1)}, bf16[128,2048]{1,0:T(8,128)(2,1)S(1)}, bf16[128,2048]{1,0:T(8,128)(2,1)S(1)}, bf16[128,2048]{1,0:T(8,128)(2,1)S(1)}) custom-call(bf16[4,128,768]{2,1,0:T(8,128)(2,1)S(1)} %bitcast.4, bf16[2048,768]{1,0:T(8,128)(2,1)S(1)} %get-tuple-element.32.whole, bf16[256,768]{1,0:T(8,128)(2,1)S(1)} %collective-permute-done.6.b2), custom_call_target="tpu_custom_call" | custom-call | flops 1610612736 | bytes 6291456 | tf_op jit(solution)/shard_map/input_grad/pallas_call | solution.py:259
  86.3 0.0 copy-start.3
  86.3 0.8 copy-done.3
  87.1 0.0 collective-permute-done.9.got
  87.1 1.4 %add_cores.1 = bf16[64,24,512]{2,1,0:T(8,128)(2,1)} custom-call(f32[64,24,512]{2,1,0:T(8,128)S(1)} %weight_grad_this_core.1.mine, bf16[64,24,512]{2,1,0:T(8,128)(2,1)S(1)} %collective-permute-done.9.got), custom_call_target="tpu_custom_call" | custom-call | flops 1048576 | bytes 6291456 | tf_op jit(solution)/shard_map/add_cores/pallas_call | solution.py:276
  88.5 8.2 %all-to-all-start.1 = ((bf16[64,24,512]{2,1,0:T(8,128)(2,1)}), bf16[64,24,512]{2,1,0:T(8,128)(2,1)S(1)}, u32[]{:S(2)}, u32[]{:S(2)}) async-start(bf16[64,24,512]{2,1,0:T(8,128)(2,1)} %add_cores.1), calls=%async_computation.1 | async-start | bytes 3145728 | tf_op jit(solution)/shard_map/all_to_all | solution.py:171
  96.7 2.9 %collective-permute-start.10 = (bf16[128,2048]{1,0:T(8,128)(2,1)}, bf16[128,2048]{1,0:T(8,128)(2,1)S(1)}, u32[]{:S(2)}, u32[]{:S(2)}) collective-permute-start(bf16[128,2048]{1,0:T(8,128)(2,1)} %copy-done.3), channel_id=1, source_target_pairs={{0,12},{4,0},{8,4},{12,8},{1,13},{5,1},{9,5},{13,9},{2,14},{6,2},{... | collective-permute-start | bytes 1572872 | tf_op jit(solution)/shard_map/ppermute | solution.py:167
  99.6 4.6 %collective-permute-start.11 = (bf16[128,2048]{1,0:T(8,128)(2,1)S(1)}, bf16[128,2048]{1,0:T(8,128)(2,1)S(1)}, u32[]{:S(2)}, u32[]{:S(2)}) collective-permute-start(bf16[128,2048]{1,0:T(8,128)(2,1)S(1)} %get-tuple-element.39), channel_id=1, source_target_pairs={{0,8},{4,12},{8,0},{12,4},{1,9},{5,13},{9,1},{13,5},{2,10},{6,14},... | collective-permute-start | bytes 1572872 | tf_op jit(solution)/shard_map/ppermute | solution.py:167
  104.2 2.3 %collective-permute-start.12 = (bf16[128,2048]{1,0:T(8,128)(2,1)S(1)}, bf16[128,2048]{1,0:T(8,128)(2,1)S(1)}, u32[]{:S(2)}, u32[]{:S(2)}) collective-permute-start(bf16[128,2048]{1,0:T(8,128)(2,1)S(1)} %get-tuple-element.40), channel_id=1, source_target_pairs={{0,4},{4,8},{8,12},{12,0},{1,5},{5,9},{9,13},{13,1},{2,6},{6,10},{... | collective-permute-start | bytes 1572872 | tf_op jit(solution)/shard_map/ppermute | solution.py:167
  106.5 7.8 %collective-permute-done.10.refs_1_ = bf16[128,2048]{1,0:T(8,128)(2,1)S(1)} collective-permute-done((bf16[128,2048]{1,0:T(8,128)(2,1)}, bf16[128,2048]{1,0:T(8,128)(2,1)S(1)}, u32[]{:S(2)}, u32[]{:S(2)}) %collective-permute-start.10) | collective-permute-done | bytes 524320 | tf_op jit(solution)/shard_map/ppermute | solution.py:167
  114.3 11.5 %collective-permute-done.11.refs_2_ = bf16[128,2048]{1,0:T(8,128)(2,1)S(1)} collective-permute-done((bf16[128,2048]{1,0:T(8,128)(2,1)S(1)}, bf16[128,2048]{1,0:T(8,128)(2,1)S(1)}, u32[]{:S(2)}, u32[]{:S(2)}) %collective-permute-start.11) | collective-permute-done | bytes 524320 | tf_op jit(solution)/shard_map/ppermute | solution.py:167
  125.8 1.9 %collective-permute-done.12.refs_3_ = bf16[128,2048]{1,0:T(8,128)(2,1)S(1)} collective-permute-done((bf16[128,2048]{1,0:T(8,128)(2,1)S(1)}, bf16[128,2048]{1,0:T(8,128)(2,1)S(1)}, u32[]{:S(2)}, u32[]{:S(2)}) %collective-permute-start.12) | collective-permute-done | bytes 524320 | tf_op jit(solution)/shard_map/ppermute | solution.py:167
  127.6 1.5 %join_features.1 = bf16[128,8192]{1,0:T(8,128)(2,1)} custom-call(bf16[128,2048]{1,0:T(8,128)(2,1)S(1)} %get-tuple-element.37.refs_0_, bf16[128,2048]{1,0:T(8,128)(2,1)S(1)} %collective-permute-done.10.refs_1_, bf16[128,2048]{1,0:T(8,128)(2,1)S(1)} %collective-permute-done.11.refs_2_, bf16[128,2048]{1,0:T(8,128)(2,1)S(1)} %collective-permute-done.12.refs_3_), custom_call_target="tpu_custom_call" | custom-call | flops 1048576 | bytes 4194304 | tf_op jit(solution)/shard_map/join_features/pallas_call | solution.py:292
  129.1 8.8 %all-to-all-done.1.ref = bf16[64,24,512]{2,1,0:T(8,128)(2,1)S(1)} async-done(((bf16[64,24,512]{2,1,0:T(8,128)(2,1)}), bf16[64,24,512]{2,1,0:T(8,128)(2,1)S(1)}, u32[]{:S(2)}, u32[]{:S(2)}) %all-to-all-start.1) | async-done | bytes 1572896 | tf_op jit(solution)/shard_map/all_to_all | solution.py:171
  137.9 0.9 add_replicas.1
Async XLA Ops:
  1.7 20.1 %collective-permute-start = (bf16[256,768]{1,0:T(8,128)(2,1)S(1)}, bf16[256,768]{1,0:T(8,128)(2,1)S(1)}, u32[]{:S(2)}, u32[]{:S(2)}) collective-permute-start(bf16[256,768]{1,0:T(8,128)(2,1)S(1)} %constant_dynamic-slice_fusion.4), channel_id=1, source_target_pairs={{0,259},{1,256},{2,257},{3,258},{256,1},{257,2},{258,3},{259,0},{4... | collective-permute-start | bytes 1179656 | tf_op jit(solution)/shard_map/ppermute | solution.py:180
  12.6 33.7 %copy-start = (bf16[512,768]{1,0:T(8,128)(2,1)S(1)}, bf16[512,768]{1,0:T(8,128)(2,1)}, u32[]{:S(2)}) copy-start(bf16[512,768]{1,0:T(8,128)(2,1)} %w0.3) | copy-start | bytes 2359300
  13.8 16.8 %collective-permute-start.1 = (bf16[128,2048]{1,0:T(8,128)(2,1)S(1)}, bf16[128,2048]{1,0:T(8,128)(2,1)S(1)}, u32[]{:S(2)}, u32[]{:S(2)}) collective-permute-start(bf16[128,2048]{1,0:T(8,128)(2,1)S(1)} %constant_dynamic-slice_fusion.3), channel_id=1, source_target_pairs={{0,8},{4,12},{8,0},{12,4},{1,9},{5,13},{9,1},{13,5},{2,10},{6,14},... | collective-permute-start | bytes 1572872 | tf_op jit(solution)/shard_map/ppermute | solution.py:167
  21.7 16.6 %collective-permute-start.7 = (bf16[256,768]{1,0:T(8,128)(2,1)S(1)}, bf16[256,768]{1,0:T(8,128)(2,1)S(1)}, u32[]{:S(2)}, u32[]{:S(2)}) collective-permute-start(bf16[256,768]{1,0:T(8,128)(2,1)S(1)} %collective-permute-done.a), channel_id=1, source_target_pairs={{0,1},{1,2},{2,3},{3,0},{256,259},{257,256},{258,257},{259,258},{4... | collective-permute-start | bytes 1179656 | tf_op jit(solution)/shard_map/ppermute | solution.py:180
  23.6 20.8 %collective-permute-start.5 = (bf16[256,768]{1,0:T(8,128)(2,1)S(1)}, bf16[256,768]{1,0:T(8,128)(2,1)S(1)}, u32[]{:S(2)}, u32[]{:S(2)}) collective-permute-start(bf16[256,768]{1,0:T(8,128)(2,1)S(1)} %collective-permute-done.a), channel_id=1, source_target_pairs={{0,256},{1,257},{2,258},{3,259},{256,0},{257,1},{258,2},{259,3},{4... | collective-permute-start | bytes 1179656 | tf_op jit(solution)/shard_map/ppermute | solution.py:180
  30.6 15.7 %collective-permute-start.2 = (bf16[128,2048]{1,0:T(8,128)(2,1)S(1)}, bf16[128,2048]{1,0:T(8,128)(2,1)S(1)}, u32[]{:S(2)}, u32[]{:S(2)}) collective-permute-start(bf16[128,2048]{1,0:T(8,128)(2,1)S(1)} %get-tuple-element.27), channel_id=1, source_target_pairs={{0,4},{4,8},{8,12},{12,0},{1,5},{5,9},{9,13},{13,1},{2,6},{6,10},{... | collective-permute-start | bytes 1572872 | tf_op jit(solution)/shard_map/ppermute | solution.py:167
  33.0 15.3 %collective-permute-start.3 = (bf16[128,2048]{1,0:T(8,128)(2,1)S(1)}, bf16[128,2048]{1,0:T(8,128)(2,1)S(1)}, u32[]{:S(2)}, u32[]{:S(2)}) collective-permute-start(bf16[128,2048]{1,0:T(8,128)(2,1)S(1)} %get-tuple-element.29), channel_id=1, source_target_pairs={{0,12},{4,0},{8,4},{12,8},{1,13},{5,1},{9,5},{13,9},{2,14},{6,2},{... | collective-permute-start | bytes 1572872 | tf_op jit(solution)/shard_map/ppermute | solution.py:167
  36.4 9.9 %collective-permute-start.4 = (bf16[256,768]{1,0:T(8,128)(2,1)S(1)}, bf16[256,768]{1,0:T(8,128)(2,1)S(1)}, u32[]{:S(2)}, u32[]{:S(2)}) collective-permute-start(bf16[256,768]{1,0:T(8,128)(2,1)S(1)} %collective-permute-done.a), channel_id=1, source_target_pairs={{0,16},{16,0},{1,17},{17,1},{2,18},{18,2},{3,19},{19,3},{4,20},{20... | collective-permute-start | bytes 1179656 | tf_op jit(solution)/shard_map/ppermute | solution.py:167
  38.4 8.0 %collective-permute-start.8 = (bf16[256,768]{1,0:T(8,128)(2,1)S(1)}, bf16[256,768]{1,0:T(8,128)(2,1)S(1)}, u32[]{:S(2)}, u32[]{:S(2)}) collective-permute-start(bf16[256,768]{1,0:T(8,128)(2,1)S(1)} %collective-permute-done.7.d), channel_id=1, source_target_pairs={{0,16},{16,0},{1,17},{17,1},{2,18},{18,2},{3,19},{19,3},{4,20},{20... | collective-permute-start | bytes 1179656 | tf_op jit(solution)/shard_map/ppermute | solution.py:167
  44.4 3.9 %collective-permute-start.6 = (bf16[256,768]{1,0:T(8,128)(2,1)S(1)}, bf16[256,768]{1,0:T(8,128)(2,1)S(1)}, u32[]{:S(2)}, u32[]{:S(2)}) collective-permute-start(bf16[256,768]{1,0:T(8,128)(2,1)S(1)} %collective-permute-done.5.b), channel_id=1, source_target_pairs={{0,16},{16,0},{1,17},{17,1},{2,18},{18,2},{3,19},{19,3},{4,20},{20... | collective-permute-start | bytes 1179656 | tf_op jit(solution)/shard_map/ppermute | solution.py:167
  48.3 15.7 %copy-start.1 = (bf16[128,512]{1,0:T(8,128)(2,1)S(1)}, bf16[128,512]{1,0:T(8,128)(2,1)}, u32[]{:S(2)}) copy-start(bf16[128,512]{1,0:T(8,128)(2,1)} %cot_ref.1) | copy-start | bytes 393220
  48.3 15.7 %copy-start.2 = (s32[1,128]{1,0:T(1,128)S(1)}, s32[1,128]{1,0:T(1,128)}, u32[]{:S(2)}) copy-start(s32[1,128]{1,0:T(1,128)} %seg_ref.1) | copy-start | bytes 1540
  80.9 6.2 %collective-permute-start.9 = (bf16[64,24,512]{2,1,0:T(8,128)(2,1)S(1)}, bf16[64,24,512]{2,1,0:T(8,128)(2,1)S(1)}, u32[]{:S(2)}, u32[]{:S(2)}) collective-permute-start(bf16[64,24,512]{2,1,0:T(8,128)(2,1)S(1)} %weight_grad_other_core.1), channel_id=1, source_target_pairs={{0,16},{16,0},{1,17},{17,1},{2,18},{18,2},{3,19},{19,3},{4,20},{20... | collective-permute-start | bytes 4718600 | tf_op jit(solution)/shard_map/ppermute | solution.py:167
  86.3 0.8 copy-start.3
  88.5 49.4 %all-to-all-start.1 = ((bf16[64,24,512]{2,1,0:T(8,128)(2,1)}), bf16[64,24,512]{2,1,0:T(8,128)(2,1)S(1)}, u32[]{:S(2)}, u32[]{:S(2)}) async-start(bf16[64,24,512]{2,1,0:T(8,128)(2,1)} %add_cores.1), calls=%async_computation.1 | async-start | bytes 3145728 | tf_op jit(solution)/shard_map/all_to_all | solution.py:171
  96.7 17.6 %collective-permute-start.10 = (bf16[128,2048]{1,0:T(8,128)(2,1)}, bf16[128,2048]{1,0:T(8,128)(2,1)S(1)}, u32[]{:S(2)}, u32[]{:S(2)}) collective-permute-start(bf16[128,2048]{1,0:T(8,128)(2,1)} %copy-done.3), channel_id=1, source_target_pairs={{0,12},{4,0},{8,4},{12,8},{1,13},{5,1},{9,5},{13,9},{2,14},{6,2},{... | collective-permute-start | bytes 1572872 | tf_op jit(solution)/shard_map/ppermute | solution.py:167
  99.6 26.1 %collective-permute-start.11 = (bf16[128,2048]{1,0:T(8,128)(2,1)S(1)}, bf16[128,2048]{1,0:T(8,128)(2,1)S(1)}, u32[]{:S(2)}, u32[]{:S(2)}) collective-permute-start(bf16[128,2048]{1,0:T(8,128)(2,1)S(1)} %get-tuple-element.39), channel_id=1, source_target_pairs={{0,8},{4,12},{8,0},{12,4},{1,9},{5,13},{9,1},{13,5},{2,10},{6,14},... | collective-permute-start | bytes 1572872 | tf_op jit(solution)/shard_map/ppermute | solution.py:167
  104.2 23.4 %collective-permute-start.12 = (bf16[128,2048]{1,0:T(8,128)(2,1)S(1)}, bf16[128,2048]{1,0:T(8,128)(2,1)S(1)}, u32[]{:S(2)}, u32[]{:S(2)}) collective-permute-start(bf16[128,2048]{1,0:T(8,128)(2,1)S(1)} %get-tuple-element.40), channel_id=1, source_target_pairs={{0,4},{4,8},{8,12},{12,0},{1,5},{5,9},{9,13},{13,1},{2,6},{6,10},{... | collective-permute-start | bytes 1572872 | tf_op jit(solution)/shard_map/ppermute | solution.py:167
